TPU v7x, 32 devices: a whole 2x2x4 slice. The times are simulated.
32 devices in a mesh: dp: 16 (over z, x, core), seq: 2 (over y).
Axes of the slice: x: 2, y: 2, z: 4, core: 2. Of those that a mesh axis runs over, the one named last changes fastest.
Arguments:
- tokens: bfloat16 [32, 1024, 768], P('dp', 'seq'), may hold values from -6 to 6
- lengths: int32 [32], P('dp'), may hold values from 256 to 1024, as said below
- gain_one: float32 [768], replicated, may hold values from 0.5 to 1.5
- w_query: bfloat16 [768, 768], replicated, may hold values from -0.21875 to 0.21875
- w_key: bfloat16 [768, 768], replicated, may hold values from -0.21875 to 0.21875
- w_value: bfloat16 [768, 768], replicated, may hold values from -0.21875 to 0.21875
- w_out: bfloat16 [768, 768], replicated, may hold values from -0.21875 to 0.21875
- gain_two: float32 [768], replicated, may hold values from 0.5 to 1.5
- w_up: bfloat16 [768, 3072], replicated, may hold values from -0.21875 to 0.21875
- w_down: bfloat16 [3072, 768], replicated, may hold values from -0.109375 to 0.109375
- shift_taps: float32 [768, 64], P('seq'), may hold values from -0.75 to 0.75
- diag_coef: float32 [768, 64], P('seq'), may hold values from -0.09375 to 0.09375
- diag_rate: float32 [768, 64], P('seq'), may hold values from 0.001 to 0.3
- cotangent: bfloat16 [32, 1024, 768], P('dp', 'seq'), may hold values from -6 to 6
Outputs:
- out: bfloat16 [32, 1024, 768], P('dp', 'seq')
- d_tokens: bfloat16 [32, 1024, 768], P('dp', 'seq')
- grad_gain_one: float32 [768], P('dp')
- grad_w_query: float32 [768, 768], P('dp')
- grad_w_key: float32 [768, 768], P('dp')
- grad_w_value: float32 [768, 768], P('dp')
- grad_w_out: float32 [768, 768], P('dp')
- grad_gain_two: float32 [768], P('dp')
- grad_w_up: float32 [768, 3072], P('dp')
- grad_w_down: float32 [3072, 768], P('dp')
- grad_shift_taps: float32 [768, 64], P('seq', 'dp')
- grad_diag_coef: float32 [768, 64], P('seq', 'dp')
- grad_diag_rate: float32 [768, 64], P('seq', 'dp')
Inputs may be any that keep to these rules, and one draw needn't show every extreme that they name: `lengths`: in each aligned block of 2 rows at least one row has length 1024.
All inputs are finite; a program needn't handle non-finite values.
Results may differ from a plain program's by a relative error of at most 0.02.
Values may be sent and summed in bfloat16 or wider, within the bound.
A program may use at most 256 MiB of HBM per device.

v0:
```python
import math

import jax
import jax.numpy as jnp
from jax import lax
from jax.sharding import PartitionSpec as P

MICRO = 2


epsilon = 1e-05
highest = lax.Precision.HIGHEST


def layer_norm(rows, gain):
    center = rows - jnp.mean(rows, axis=-1, keepdims=True)
    spread = jnp.mean(center * center, axis=-1, keepdims=True)
    return center * lax.rsqrt(spread + epsilon) * gain


def exact_gelu(values):
    return jax.nn.gelu(values, approximate=False)


def project(rows, weight):
    return jnp.einsum("rtd,de->rte", rows, weight, preferred_element_type=jnp.float32)


def project_back(rows, weight):
    return jnp.einsum("rte,de->rtd", rows, weight, preferred_element_type=jnp.float32)


def weight_grad(left, right):
    return jnp.einsum("rtd,rte->de", left, right, preferred_element_type=jnp.float32)


def depth_conv(signal, kernel_taps):
    channels = signal.shape[2]
    return lax.conv_general_dilated(
        signal,
        kernel_taps,
        (1,),
        "VALID",
        dimension_numbers=("NWC", "WIO", "NWC"),
        feature_group_count=channels,
        precision=highest,
    )


def shift_conv(extended, taps, length):
    flipped = jnp.transpose(taps[:, ::-1])[:, None, :]
    return depth_conv(extended[:, 1:, :], flipped)[:, :length, :]


def shift_back(extended, taps, length):
    forward_taps = jnp.transpose(taps)[:, None, :]
    return depth_conv(extended, forward_taps)[:, :length, :]


def taps_grad(grad_rows, extended, width_taps):
    rows_count, span, channels = extended.shape
    left = jnp.transpose(extended, (2, 0, 1)).reshape(1, channels * rows_count, span)
    right = jnp.transpose(grad_rows, (2, 0, 1))
    result = lax.conv_general_dilated(
        left,
        right,
        (1,),
        "VALID",
        dimension_numbers=("NCW", "OIW", "NCW"),
        feature_group_count=channels,
        precision=highest,
    )
    return result[0][:, ::-1][:, :width_taps]


def diag_kernel(coef, rate, length):
    steps = lax.iota(jnp.float32, length)
    return jnp.sum(coef[:, :, None] * jnp.exp(-rate[:, :, None] * steps), axis=1)


def dft_tables(length):
    period = 2 * length
    time_index = lax.iota(jnp.int32, length)[:, None]
    freq_index = lax.iota(jnp.int32, length + 1)[None, :]
    phase_index = time_index * freq_index % period
    angles = phase_index.astype(jnp.float32) * (2.0 * math.pi / period)
    cos_table = jnp.cos(angles)
    sin_table = jnp.sin(angles)
    edges = (freq_index == 0) | (freq_index == length)
    weights = jnp.where(edges, 1.0, 2.0).astype(jnp.float32) / period
    return (cos_table, sin_table, cos_table * weights, sin_table * weights)


def spectrum(signal, cos_table, sin_table):
    real_part = jnp.einsum("rtc,tf->rfc", signal, cos_table, precision=highest)
    imag_part = -jnp.einsum("rtc,tf->rfc", signal, sin_table, precision=highest)
    return (real_part, imag_part)


def inverse(real_part, imag_part, cos_weighted, sin_weighted):
    first = jnp.einsum("rfc,tf->rtc", real_part, cos_weighted, precision=highest)
    second = jnp.einsum("rfc,tf->rtc", imag_part, sin_weighted, precision=highest)
    return first - second


def per_device(
    tokens,
    lengths,
    gain_one,
    w_query,
    w_key,
    w_value,
    w_out,
    gain_two,
    w_up,
    w_down,
    shift_taps,
    diag_coef,
    diag_rate,
    cotangent,
):
    rows_dev, tok_len, model_width = tokens.shape
    length = tok_len * lax.axis_size("seq")
    width_taps = shift_taps.shape[1]
    first_pos = lax.axis_index("seq") * tok_len
    positions = first_pos + lax.iota(jnp.int32, tok_len)
    mask_all = (positions[None, :] < lengths[:, None]).astype(jnp.float32)[:, :, None]
    cos_table, sin_table, cos_weighted, sin_weighted = dft_tables(length)

    def kernel_of(coef_in, rate_in):
        return diag_kernel(coef_in, rate_in, length)

    kernel, kernel_pull = jax.vjp(kernel_of, diag_coef, diag_rate)
    kernel_real = jnp.einsum("ct,tf->fc", kernel, cos_table, precision=highest)
    kernel_imag = -jnp.einsum("ct,tf->fc", kernel, sin_table, precision=highest)
    taps_acc = jnp.zeros(shift_taps.shape, jnp.float32)
    spec_real_acc = jnp.zeros((length + 1, shift_taps.shape[0]), jnp.float32)
    spec_imag_acc = jnp.zeros((length + 1, shift_taps.shape[0]), jnp.float32)
    grad_gain_one = jnp.zeros(gain_one.shape, jnp.float32)
    grad_gain_two = jnp.zeros(gain_two.shape, jnp.float32)
    grad_query = jnp.zeros(w_query.shape, jnp.float32)
    grad_key = jnp.zeros(w_key.shape, jnp.float32)
    grad_value = jnp.zeros(w_value.shape, jnp.float32)
    grad_out = jnp.zeros(w_out.shape, jnp.float32)
    grad_up = jnp.zeros(w_up.shape, jnp.float32)
    grad_down = jnp.zeros(w_down.shape, jnp.float32)
    rows_mb = rows_dev // MICRO
    out_list = []
    dx_list = []
    for micro_step in range(MICRO):
        low_row = micro_step * rows_mb
        x_rows = tokens[low_row : low_row + rows_mb].astype(jnp.float32)
        live_mask = mask_all[low_row : low_row + rows_mb]
        grad_rows = cotangent[low_row : low_row + rows_mb].astype(jnp.float32)
        norm_one, norm_one_pull = jax.vjp(layer_norm, x_rows, gain_one)
        a_one = norm_one.astype(jnp.bfloat16)
        query_rows = project(a_one, w_query)
        key_rows = (project(a_one, w_key) * live_mask).astype(jnp.bfloat16)
        value_rows = (project(a_one, w_value) * live_mask).astype(jnp.bfloat16)
        keys_ch, values_ch = (
            lax.all_to_all(key_rows, "seq", split_axis=2, concat_axis=1, tiled=True),
            lax.all_to_all(value_rows, "seq", split_axis=2, concat_axis=1, tiled=True),
        )
        key_ext = jnp.pad(keys_ch.astype(jnp.float32), ((0, 0), (width_taps, 0), (0, 0)))
        shifted = shift_conv(key_ext, shift_taps, length)
        values_here = values_ch.astype(jnp.float32)
        mixed_ch = (shifted * values_here).astype(jnp.bfloat16)
        mixed_real, mixed_imag = spectrum(mixed_ch.astype(jnp.float32), cos_table, sin_table)
        state = inverse(
            mixed_real * kernel_real - mixed_imag * kernel_imag,
            mixed_real * kernel_imag + mixed_imag * kernel_real,
            cos_weighted,
            sin_weighted,
        )
        state_tok = lax.all_to_all(
            state.astype(jnp.bfloat16), "seq", split_axis=1, concat_axis=2, tiled=True
        )
        state_rows = state_tok.astype(jnp.float32)
        gated_rows = (query_rows * state_rows).astype(jnp.bfloat16)
        hidden = x_rows + live_mask * project(gated_rows, w_out)
        norm_two, norm_two_pull = jax.vjp(layer_norm, hidden, gain_two)
        a_two = norm_two.astype(jnp.bfloat16)
        pre_act = project(a_two, w_up)
        act_value, gelu_pull = jax.vjp(exact_gelu, pre_act)
        activation = act_value.astype(jnp.bfloat16)
        result = hidden + live_mask * project(activation, w_down)
        out_list.append(result.astype(jnp.bfloat16))
        d_down = (live_mask * grad_rows).astype(jnp.bfloat16)
        grad_down = grad_down + weight_grad(activation, d_down)
        d_act = project_back(d_down, w_down)
        d_pre = gelu_pull(d_act)[0].astype(jnp.bfloat16)
        grad_up = grad_up + weight_grad(a_two, d_pre)
        d_a_two = project_back(d_pre, w_up)
        d_hidden_norm, d_gain_two = norm_two_pull(d_a_two)
        grad_gain_two = grad_gain_two + d_gain_two
        d_hidden = grad_rows + d_hidden_norm
        d_mixer = (live_mask * d_hidden).astype(jnp.bfloat16)
        grad_out = grad_out + weight_grad(gated_rows, d_mixer)
        d_gated = project_back(d_mixer, w_out)
        d_query = (d_gated * state_rows).astype(jnp.bfloat16)
        d_state = (d_gated * query_rows).astype(jnp.bfloat16)
        d_state_ch = lax.all_to_all(d_state, "seq", split_axis=2, concat_axis=1, tiled=True)
        grad_real, grad_imag = spectrum(d_state_ch.astype(jnp.float32), cos_table, sin_table)
        d_mixed = inverse(
            kernel_real * grad_real + kernel_imag * grad_imag,
            kernel_real * grad_imag - kernel_imag * grad_real,
            cos_weighted,
            sin_weighted,
        )
        spec_real_acc = spec_real_acc + jnp.sum(
            mixed_real * grad_real + mixed_imag * grad_imag, axis=0
        )
        spec_imag_acc = spec_imag_acc + jnp.sum(
            mixed_real * grad_imag - mixed_imag * grad_real, axis=0
        )
        d_mixed_low = d_mixed.astype(jnp.bfloat16)
        d_mix_ch = d_mixed_low.astype(jnp.float32)
        d_shifted = d_mix_ch * values_here
        d_values_ch = (d_mix_ch * shifted).astype(jnp.bfloat16)
        grad_ext = jnp.pad(d_shifted, ((0, 0), (0, width_taps), (0, 0)))
        d_keys_ch = shift_back(grad_ext, shift_taps, length).astype(jnp.bfloat16)
        taps_acc = taps_acc + taps_grad(d_shifted, key_ext, width_taps)
        keys_back, values_back = (
            lax.all_to_all(d_keys_ch, "seq", split_axis=1, concat_axis=2, tiled=True),
            lax.all_to_all(d_values_ch, "seq", split_axis=1, concat_axis=2, tiled=True),
        )
        mask_low = live_mask.astype(jnp.bfloat16)
        d_keys = keys_back * mask_low
        d_values = values_back * mask_low
        grad_query = grad_query + weight_grad(a_one, d_query)
        grad_key = grad_key + weight_grad(a_one, d_keys)
        grad_value = grad_value + weight_grad(a_one, d_values)
        d_a_one = (
            project_back(d_query, w_query)
            + project_back(d_keys, w_key)
            + project_back(d_values, w_value)
        )
        d_x_norm, d_gain_one = norm_one_pull(d_a_one)
        grad_gain_one = grad_gain_one + d_gain_one
        dx_list.append((d_hidden + d_x_norm).astype(jnp.bfloat16))
    d_kernel = jnp.einsum("fc,tf->ct", spec_real_acc, cos_weighted, precision=highest) - jnp.einsum(
        "fc,tf->ct", spec_imag_acc, sin_weighted, precision=highest
    )
    d_coef, d_rate = kernel_pull(d_kernel)
    taps_part, coef_part, rate_part = (
        lax.psum_scatter(
            taps_acc.astype(jnp.bfloat16), "dp", scatter_dimension=1, tiled=True
        ).astype(jnp.float32),
        lax.psum_scatter(d_coef.astype(jnp.bfloat16), "dp", scatter_dimension=1, tiled=True).astype(
            jnp.float32
        ),
        lax.psum_scatter(d_rate.astype(jnp.bfloat16), "dp", scatter_dimension=1, tiled=True).astype(
            jnp.float32
        ),
    )
    shares = (
        lax.psum_scatter(
            grad_gain_one.astype(jnp.bfloat16), "dp", scatter_dimension=0, tiled=True
        ).astype(jnp.float32),
        lax.psum_scatter(
            grad_query.astype(jnp.bfloat16), "dp", scatter_dimension=0, tiled=True
        ).astype(jnp.float32),
        lax.psum_scatter(
            grad_key.astype(jnp.bfloat16), "dp", scatter_dimension=0, tiled=True
        ).astype(jnp.float32),
        lax.psum_scatter(
            grad_value.astype(jnp.bfloat16), "dp", scatter_dimension=0, tiled=True
        ).astype(jnp.float32),
        lax.psum_scatter(
            grad_out.astype(jnp.bfloat16), "dp", scatter_dimension=0, tiled=True
        ).astype(jnp.float32),
        lax.psum_scatter(
            grad_gain_two.astype(jnp.bfloat16), "dp", scatter_dimension=0, tiled=True
        ).astype(jnp.float32),
        lax.psum_scatter(
            grad_up.astype(jnp.bfloat16), "dp", scatter_dimension=0, tiled=True
        ).astype(jnp.float32),
        lax.psum_scatter(
            grad_down.astype(jnp.bfloat16), "dp", scatter_dimension=0, tiled=True
        ).astype(jnp.float32),
    )
    totals = (
        lax.psum(shares[0].astype(jnp.bfloat16), "seq").astype(jnp.float32),
        lax.psum(shares[1].astype(jnp.bfloat16), "seq").astype(jnp.float32),
        lax.psum(shares[2].astype(jnp.bfloat16), "seq").astype(jnp.float32),
        lax.psum(shares[3].astype(jnp.bfloat16), "seq").astype(jnp.float32),
        lax.psum(shares[4].astype(jnp.bfloat16), "seq").astype(jnp.float32),
        lax.psum(shares[5].astype(jnp.bfloat16), "seq").astype(jnp.float32),
        lax.psum(shares[6].astype(jnp.bfloat16), "seq").astype(jnp.float32),
        lax.psum(shares[7].astype(jnp.bfloat16), "seq").astype(jnp.float32),
    )
    out_rows = jnp.concatenate(out_list, axis=0)
    dx_rows = jnp.concatenate(dx_list, axis=0)
    return (
        out_rows,
        dx_rows,
        totals[0],
        totals[1],
        totals[2],
        totals[3],
        totals[4],
        totals[5],
        totals[6],
        totals[7],
        taps_part,
        coef_part,
        rate_part,
    )


def solution(mesh):
    in_specs = (
        P("dp", "seq", None),
        P("dp"),
        P(),
        P(),
        P(),
        P(),
        P(),
        P(),
        P(),
        P(),
        P("seq", None),
        P("seq", None),
        P("seq", None),
        P("dp", "seq", None),
    )
    out_specs = (
        P("dp", "seq", None),
        P("dp", "seq", None),
        P("dp"),
        P("dp", None),
        P("dp", None),
        P("dp", None),
        P("dp", None),
        P("dp"),
        P("dp", None),
        P("dp", None),
        P("seq", "dp"),
        P("seq", "dp"),
        P("seq", "dp"),
    )
    return jax.shard_map(
        per_device, mesh=mesh, in_specs=in_specs, out_specs=out_specs, check_vma=False
    )
```

profile of v0, /device:TPU:0, one launch (start us, length us, event | category | flops | bytes accessed | tf_op | source)
XLA Modules:
  0.0 1359.5 jit_solution(15726768175770644608)
XLA Ops:
  16.5 6.4 reduce.20
  24.3 5.0 all-to-all-start.4
  38.5 6.4 reduce.21
  51.3 6.4 reduce.23
  59.1 24.6 %multiply_reduce_fusion.2 = f32[384,1024]{1,0:T(8,128)S(1)} fusion(f32[384,64]{1,0:T(8,128)} %copy.232, f32[384,64]{1,0:T(8,128)} %copy.231), kind=kLoop, calls=%fused_computation.2 | loop fusion | flops 75104256 | bytes 1769472 | tf_op jit(solution)/shard_map/jvp()/reduce_sum | solution.py:78
  84.9 33.1 %fusion.96 = f32[1025,384]{1,0:T(8,128)} fusion(f32[384,1024]{1,0:T(8,128)S(1)} %multiply_reduce_fusion.2), kind=kOutput, calls=%fused_computation.124 | convolution fusion | flops 4851251200 | bytes 3147264 | tf_op jit(solution)/shard_map/ct,tf->fc/dot_general | solution.py:135
  122.2 34.6 %fusion.80 = f32[1025,384]{1,0:T(8,128)} fusion(f32[384,1024]{1,0:T(8,128)} %copy-done.149), kind=kOutput, calls=%fused_computation.119 | convolution fusion | flops 4851251200 | bytes 3147264 | tf_op jit(solution)/shard_map/ct,tf->fc/dot_general | solution.py:134
  164.2 5.1 copy.223
  169.3 6.4 reduce.24
  180.3 4.9 copy.242
  197.8 5.0 copy.230
  203.9 8.0 convolution_select_fusion
  213.8 23.9 %fusion.93 = f32[1025,384]{1,0:T(8,128)} fusion(bf16[1,1024,384]{2,1,0:T(8,128)(2,1)S(1)} %fusion.162), kind=kOutput, calls=%fused_computation.123 | convolution fusion | flops 4851251200 | bytes 2360832 | tf_op jit(solution)/shard_map/rtc,tf->rfc/dot_general | solution.py:96
  237.7 23.3 %fusion.78 = f32[1025,384]{1,0:T(8,128)} fusion(bf16[1,1024,384]{2,1,0:T(8,128)(2,1)S(1)} %fusion.162), kind=kOutput, calls=%fused_computation.118 | convolution fusion | flops 4851251200 | bytes 2360832 | tf_op jit(solution)/shard_map/rtc,tf->rfc/dot_general | solution.py:95
  268.7 8.0 convolution_select_fusion.1
  278.6 23.7 %fusion.98 = f32[1025,384]{1,0:T(8,128)} fusion(bf16[1,1024,384]{2,1,0:T(8,128)(2,1)S(1)} %fusion.163), kind=kOutput, calls=%fused_computation.125 | convolution fusion | flops 4851251200 | bytes 2360832 | tf_op jit(solution)/shard_map/rtc,tf->rfc/dot_general | solution.py:96
  302.3 23.3 %fusion.82 = f32[1025,384]{1,0:T(8,128)} fusion(bf16[1,1024,384]{2,1,0:T(8,128)(2,1)S(1)} %fusion.163), kind=kOutput, calls=%fused_computation.120 | convolution fusion | flops 4851251200 | bytes 2360832 | tf_op jit(solution)/shard_map/rtc,tf->rfc/dot_general | solution.py:95
  325.6 26.8 %fusion.24 = f32[1024,384]{1,0:T(8,128)S(1)} fusion(f32[1025]{0:T(1024)S(1)} %copy-done.111, f32[1025,384]{1,0:T(8,128)S(1)} %copy-done.145, f32[1025,384]{1,0:T(8,128)S(1)} %copy-done.127, f32[1025,384]{1,0:T(8,128)S(1)} %copy-done.125, f32[1025,384]{1,0:T(8,128)S(1)} %copy-done.141), kind=kOutput, calls=%fused_computation.55 | convolution fusion | flops 4854268928 | bytes 7874564 | tf_op jit(solution)/shard_map/rfc,tf->rtc/dot_general | solution.py:102
  352.4 26.1 %fusion.218 = bf16[1,1024,384]{2,1,0:T(8,128)(2,1)S(1)} fusion(f32[1024,384]{1,0:T(8,128)S(1)} %fusion.24, f32[1025,384]{1,0:T(8,128)S(1)} %copy-done.125, f32[1025,384]{1,0:T(8,128)S(1)} %copy-done.141, f32[1025,384]{1,0:T(8,128)S(1)} %copy-done.127, f32[1025,384]{1,0:T(8,128)S(1)} %copy-done.145, f32[1025]{0:T(1024)S(1)} %copy-done.111), kind=kOutput, calls=%fused_computation.264 | convolution fusion | flops 4854267904 | bytes 8660996 | tf_op jit(solution)/shard_map/rfc,tf->rtc/dot_general | solution.py:101
  380.9 6.4 reduce.22
  392.7 29.8 %fusion.26 = f32[1024,384]{1,0:T(8,128)S(1)} fusion(f32[1025]{0:T(1024)} %select_multiply_fusion, f32[1025,384]{1,0:T(8,128)} %fusion.80, f32[1025,384]{1,0:T(8,128)} %fusion.82, f32[1025,384]{1,0:T(8,128)} %fusion.98, f32[1025,384]{1,0:T(8,128)} %fusion.96), kind=kOutput, calls=%fused_computation.57 | convolution fusion | flops 4854268928 | bytes 7874564 | tf_op jit(solution)/shard_map/rfc,tf->rtc/dot_general | solution.py:102
  422.6 26.1 %fusion.211 = bf16[1,1024,384]{2,1,0:T(8,128)(2,1)S(1)} fusion(f32[1024,384]{1,0:T(8,128)S(1)} %fusion.26, f32[1025,384]{1,0:T(8,128)S(1)} %copy-done.129, f32[1025,384]{1,0:T(8,128)S(1)} %copy-done.142, f32[1025,384]{1,0:T(8,128)S(1)} %copy-done.131, f32[1025,384]{1,0:T(8,128)S(1)} %copy-done.146, f32[1025]{0:T(1024)S(1)} %copy-done.112), kind=kOutput, calls=%fused_computation.261 | convolution fusion | flops 4854267904 | bytes 8660996 | tf_op jit(solution)/shard_map/rfc,tf->rtc/dot_general | solution.py:101
  451.1 6.4 reduce.25
  468.6 5.2 all-to-all-done.2
  485.6 19.5 %multiply_convert_fusion = (bf16[512,3072]{1,0:T(8,128)(2,1)}, f32[512,3072]{1,0:T(8,128)}, f32[512,3072]{1,0:T(8,128)}) fusion(bf16[768,3072]{1,0:T(8,128)(2,1)} %param.22, f32[1,512,768]{2,1,0:T(8,128)S(1)} %get-tuple-element.77, f32[512]{0:T(512)S(1)} %fusion.274, f32[512]{0:T(512)S(1)} %broadcast_multiply_fusion.4, f32[768]{0:T(1024)S(1)} %copy-done.65), kind=kOutput, calls=%fused_computation.15 | convolution fusion | flops 2519728128 | bytes 22027264 | tf_op jit(solution)/shard_map/rtd,de->rte/dot_general | solution.py:26
  505.2 8.7 add_convert_fusion.2
  513.9 5.9 fusion.402
  519.8 19.5 %multiply_convert_fusion.1 = (bf16[512,3072]{1,0:T(8,128)(2,1)}, f32[512,3072]{1,0:T(8,128)}, f32[512,3072]{1,0:T(8,128)}) fusion(bf16[768,3072]{1,0:T(8,128)(2,1)} %param.22, f32[1,512,768]{2,1,0:T(8,128)S(1)} %get-tuple-element.82, f32[768]{0:T(1024)S(1)} %copy-done.65, f32[512]{0:T(512)S(1)} %fusion.272, f32[512]{0:T(512)S(1)} %broadcast_multiply_fusion.6), kind=kOutput, calls=%fused_computation.28 | convolution fusion | flops 2519728128 | bytes 22027264 | tf_op jit(solution)/shard_map/rtd,de->rte/dot_general | solution.py:26
  539.3 8.4 add_convert_fusion.3
  547.7 7.2 fusion.165
  569.6 7.3 reduce.26
  579.4 4.5 all-to-all-start.9
  587.3 4.8 copy.245
  592.1 6.5 reduce.29
  612.6 23.2 %fusion.89 = f32[1025,384]{1,0:T(8,128)} fusion(bf16[1024,384]{1,0:T(8,128)(2,1)} %bitcast.417), kind=kOutput, calls=%fused_computation.121 | convolution fusion | flops 4851251200 | bytes 2360832 | tf_op jit(solution)/shard_map/rtc,tf->rfc/dot_general | solution.py:96
  635.9 23.2 %fusion.74 = f32[1025,384]{1,0:T(8,128)} fusion(bf16[1024,384]{1,0:T(8,128)(2,1)S(1)} %bitcast.418), kind=kOutput, calls=%fused_computation.116 | convolution fusion | flops 4851251200 | bytes 2360832 | tf_op jit(solution)/shard_map/rtc,tf->rfc/dot_general | solution.py:95
  662.6 23.8 %fusion.91 = f32[1025,384]{1,0:T(8,128)} fusion(bf16[1024,384]{1,0:T(8,128)(2,1)S(1)} %bitcast.419), kind=kOutput, calls=%fused_computation.122 | convolution fusion | flops 4851251200 | bytes 2360832 | tf_op jit(solution)/shard_map/rtc,tf->rfc/dot_general | solution.py:96
  686.5 23.2 %fusion.76 = f32[1025,384]{1,0:T(8,128)} fusion(bf16[1024,384]{1,0:T(8,128)(2,1)S(1)} %bitcast.420), kind=kOutput, calls=%fused_computation.117 | convolution fusion | flops 4851251200 | bytes 2360832 | tf_op jit(solution)/shard_map/rtc,tf->rfc/dot_general | solution.py:95
  709.7 27.0 %fusion.20 = f32[1024,384]{1,0:T(8,128)S(1)} fusion(f32[1025]{0:T(1024)S(1)} %copy-done.113, f32[1025,384]{1,0:T(8,128)S(1)} %copy-done.135, f32[1025,384]{1,0:T(8,128)S(1)} %copy-done.147, f32[1025,384]{1,0:T(8,128)S(1)} %copy-done.133, f32[1025,384]{1,0:T(8,128)S(1)} %copy-done.143), kind=kOutput, calls=%fused_computation.51 | convolution fusion | flops 4854268928 | bytes 7874564 | tf_op jit(solution)/shard_map/rfc,tf->rtc/dot_general | solution.py:102
  736.7 26.9 %fusion.157 = (bf16[1,1024,384]{2,1,0:T(8,128)(2,1)}, bf16[1024,384]{1,0:T(8,128)(2,1)S(1)}) fusion(f32[1,1088,384]{2,1,0:T(8,128)S(1)} %bitcast.380, f32[1024,384]{1,0:T(8,128)S(1)} %fusion.20, f32[1025,384]{1,0:T(8,128)S(1)} %copy-done.143, f32[1025,384]{1,0:T(8,128)S(1)} %copy-done.133, f32[1025,384]{1,0:T(8,128)S(1)} %copy-done.147, ...), kind=kOutput, calls=%fused_computation.195 | convolution fusion | flops 4855447552 | bytes 11020292 | tf_op jit(solution)/shard_map/rfc,tf->rtc/dot_general | solution.py:101
  765.8 9.4 select_convert_fusion
  777.8 6.4 reduce.28
  788.8 30.0 %fusion.22 = f32[1024,384]{1,0:T(8,128)S(1)} fusion(f32[1025]{0:T(1024)S(1)} %copy-done.113, f32[1025,384]{1,0:T(8,128)} %fusion.76, f32[1025,384]{1,0:T(8,128)} %fusion.80, f32[1025,384]{1,0:T(8,128)} %fusion.91, f32[1025,384]{1,0:T(8,128)} %fusion.96), kind=kOutput, calls=%fused_computation.53 | convolution fusion | flops 4854268928 | bytes 7874564 | tf_op jit(solution)/shard_map/rfc,tf->rtc/dot_general | solution.py:102
  818.9 27.2 %fusion.153 = (bf16[1,1024,384]{2,1,0:T(8,128)(2,1)}, bf16[1024,384]{1,0:T(8,128)(2,1)}) fusion(f32[1,1088,384]{2,1,0:T(8,128)S(1)} %bitcast.378, f32[1024,384]{1,0:T(8,128)S(1)} %fusion.22, f32[1025,384]{1,0:T(8,128)S(1)} %copy-done.144, f32[1025,384]{1,0:T(8,128)S(1)} %copy-done.137, f32[1025,384]{1,0:T(8,128)S(1)} %copy-done.148, ...), kind=kOutput, calls=%fused_computation.191 | convolution fusion | flops 4855447552 | bytes 11020292 | tf_op jit(solution)/shard_map/rfc,tf->rtc/dot_general | solution.py:101
  848.5 6.4 reduce.27
  864.8 9.5 select_convert_fusion.1
  876.8 6.6 reduce.31
  884.5 4.4 all-to-all-start.7
  891.3 6.4 reduce.30
  936.6 5.3 fusion.372
  941.9 4.7 add_convert_fusion.1
  953.3 5.1 fusion.168
  958.4 5.0 fusion.169
  972.3 4.5 add_convert_fusion
  977.5 35.5 %fusion.18 = f32[384,1024]{1,0:T(8,128)S(1)} fusion(f32[1025]{0:T(1024)S(1)} %copy-done.114, f32[1025,384]{1,0:T(8,128)} %fusion.74, f32[1025,384]{1,0:T(8,128)} %fusion.78, f32[1025,384]{1,0:T(8,128)} %fusion.76, f32[1025,384]{1,0:T(8,128)} %fusion.82, f32[1025,384]{1,0:T(8,128)} %fusion.89, f32[1025,384]{1,0:T(8,128)} %fusion.91, ...), kind=kOutput, calls=%fused_computation.49 | convolution fusion | flops 4856630272 | bytes 14172164 | tf_op jit(solution)/shard_map/fc,tf->ct/dot_general | solution.py:241
  1013.1 30.0 %fusion.196 = f32[384,1024]{1,0:T(8,128)S(1)} fusion(f32[384,1024]{1,0:T(8,128)S(1)} %fusion.18, f32[1025]{0:T(1024)S(1)} %copy-done.114, f32[1025,384]{1,0:T(8,128)S(1)} %copy-done.126, f32[1025,384]{1,0:T(8,128)S(1)} %copy-done.134, f32[1025,384]{1,0:T(8,128)S(1)} %copy-done.128, f32[1025,384]{1,0:T(8,128)S(1)} %copy-done.136, ...), kind=kOutput, calls=%fused_computation.252 | convolution fusion | flops 4855449088 | bytes 15745028 | tf_op jit(solution)/shard_map/fc,tf->ct/dot_general | solution.py:241
  1043.1 36.6 %multiply_reduce_fusion = (f32[384,64]{1,0:T(8,128)S(1)}, bf16[384,64]{1,0:T(8,128)(2,1)S(1)}) fusion(f32[384,1024]{1,0:T(8,128)S(1)} %fusion.196, f32[384,64]{1,0:T(8,128)S(1)} %copy-done.67, f32[384,64]{1,0:T(8,128)S(1)} %copy-done.68), kind=kLoop, calls=%fused_computation | loop fusion | flops 176111616 | bytes 1916928 | tf_op jit(solution)/shard_map/transpose(jvp())/reduce_sum | solution.py:78
  1079.8 8.9 fusion.104
  1090.3 10.4 fusion.106
  1118.3 12.1 reduce-scatter.15.cloned.1.call-done
  1130.3 78.8 %reduce-scatter.17.cloned.1.call-done = bf16[192,768]{1,0:T(8,128)(2,1)} async-done(((bf16[3072,768]{1,0:T(8,128)(2,1)}), bf16[192,768]{1,0:T(8,128)(2,1)}) %reduce-scatter.17.cloned.1.call-update) | async-done | bytes 294928 | tf_op jit(solution)/shard_map/reduce_scatter | solution.py:278
  1214.5 87.8 %all-reduce.13.cloned.1.call-done = (bf16[768]{0:T(1024)(128)(2,1)}, bf16[768]{0:T(1024)(128)(2,1)}, bf16[384,64]{0,1:T(8,128)(2,1)}, bf16[384,64]{0,1:T(8,128)(2,1)}, bf16[384,64]{0,1:T(8,128)(2,1)}) async-done(((bf16[768]{0:T(1024)(128)(2,1)}, bf16[768]{0:T(1024)(128)(2,1)}, bf16[384,64]{0,1:T(8,128)(2,1)}, bf16[384,64]{0,1:T(8,128)(2,1)}, bf16[384,64]{0,1:T(8,128)(2,1)}), (bf16[768]{0:T(1024)(128)(2,1)}, ...) | async-done | bytes 150544
  1303.8 4.9 all-reduce.8
  1313.6 29.8 %all-reduce.15.cloned.1.call-done = (bf16[48,768]{1,0:T(8,128)(2,1)}, bf16[48,768]{1,0:T(8,128)(2,1)}, bf16[48,768]{1,0:T(8,128)(2,1)}, bf16[48,768]{1,0:T(8,128...) async-done(((bf16[48,768]{1,0:T(8,128)(2,1)}, bf16[48,768]{1,0:T(8,128)(2,1)}, bf16[48,768]{1,0:T(8,128)(2,1)}, bf16[48,768]{1,0:T(8,128)(2,1)}, ...) | async-done | bytes 884752 | tf_op jit(solution)/shard_map/psum | solution.py:284
  (520 shorter events, 261.4 us)
Async XLA Ops:
  7.2 472.9 %copy-start = (bf16[768,768]{1,0:T(8,128)(2,1)S(1)}, bf16[768,768]{1,0:T(8,128)(2,1)}, u32[]{:S(2)}) copy-start(bf16[768,768]{1,0:T(8,128)(2,1)} %param.20) | copy-start | bytes 3538948
  24.3 93.7 %all-to-all-start.4 = ((bf16[2,2,98304]{2,1,0:T(2,128)(2,1)}), bf16[2,2,98304]{2,1,0:T(2,128)(2,1)}, u32[]{:S(2)}, u32[]{:S(2)}) async-start(bf16[2,2,98304]{2,1,0:T(2,128)(2,1)} %reshape.963), calls=%async_computation.4 | async-start | bytes 1572864 | tf_op jit(solution)/shard_map/all_to_all | solution.py:162
  118.0 38.9 %all-to-all-start.3 = ((bf16[2,2,98304]{2,1,0:T(2,128)(2,1)}), bf16[2,2,98304]{2,1,0:T(2,128)(2,1)S(1)}, u32[]{:S(2)}, u32[]{:S(2)}) async-start(bf16[2,2,98304]{2,1,0:T(2,128)(2,1)} %reshape.965), calls=%async_computation.3 | async-start | bytes 1572864 | tf_op jit(solution)/shard_map/all_to_all | solution.py:161
  156.8 33.9 %all-to-all-start.1 = ((bf16[2,2,98304]{2,1,0:T(2,128)(2,1)}), bf16[2,2,98304]{2,1,0:T(2,128)(2,1)}, u32[]{:S(2)}, u32[]{:S(2)}) async-start(bf16[2,2,98304]{2,1,0:T(2,128)(2,1)} %reshape.969), calls=%async_computation.1 | async-start | bytes 1572864 | tf_op jit(solution)/shard_map/all_to_all | solution.py:162
  190.8 70.2 %all-to-all-start = ((bf16[2,2,98304]{2,1,0:T(2,128)(2,1)}), bf16[2,2,98304]{2,1,0:T(2,128)(2,1)}, u32[]{:S(2)}, u32[]{:S(2)}) async-start(bf16[2,2,98304]{2,1,0:T(2,128)(2,1)} %reshape.971), calls=%async_computation | async-start | bytes 1572864 | tf_op jit(solution)/shard_map/all_to_all | solution.py:161
  302.3 23.3 %copy-start.111 = (f32[1025]{0:T(1024)S(1)}, f32[1025]{0:T(1024)}, u32[]{:S(2)}) copy-start(f32[1025]{0:T(1024)} %select_multiply_fusion) | copy-start | bytes 12304
  302.3 23.3 %copy-start.125 = (f32[1025,384]{1,0:T(8,128)S(1)}, f32[1025,384]{1,0:T(8,128)}, u32[]{:S(2)}) copy-start(f32[1025,384]{1,0:T(8,128)} %fusion.93) | copy-start | bytes 4723204
  302.3 23.3 %copy-start.127 = (f32[1025,384]{1,0:T(8,128)S(1)}, f32[1025,384]{1,0:T(8,128)}, u32[]{:S(2)}) copy-start(f32[1025,384]{1,0:T(8,128)} %fusion.78) | copy-start | bytes 4723204
  302.3 23.4 %copy-start.141 = (f32[1025,384]{1,0:T(8,128)S(1)}, f32[1025,384]{1,0:T(8,128)}, u32[]{:S(2)}) copy-start(f32[1025,384]{1,0:T(8,128)} %fusion.96) | copy-start | bytes 4723204
  302.3 23.4 %copy-start.145 = (f32[1025,384]{1,0:T(8,128)S(1)}, f32[1025,384]{1,0:T(8,128)}, u32[]{:S(2)}) copy-start(f32[1025,384]{1,0:T(8,128)} %fusion.80) | copy-start | bytes 4723204
  388.4 70.1 %all-to-all-start.5 = ((bf16[2,2,98304]{2,1,0:T(2,128)(2,1)}), bf16[2,2,98304]{2,1,0:T(2,128)(2,1)}, u32[]{:S(2)}, u32[]{:S(2)}) async-start(bf16[2,2,98304]{2,1,0:T(2,128)(2,1)} %reshape.967), calls=%async_computation.5 | async-start | bytes 1572864 | tf_op jit(solution)/shard_map/all_to_all | solution.py:175
  392.7 29.8 %copy-start.112 = (f32[1025]{0:T(1024)S(1)}, f32[1025]{0:T(1024)}, u32[]{:S(2)}) copy-start(f32[1025]{0:T(1024)} %select_multiply_fusion) | copy-start | bytes 12304
  392.7 29.8 %copy-start.129 = (f32[1025,384]{1,0:T(8,128)S(1)}, f32[1025,384]{1,0:T(8,128)}, u32[]{:S(2)}) copy-start(f32[1025,384]{1,0:T(8,128)} %fusion.98) | copy-start | bytes 4723204
  392.7 29.8 %copy-start.131 = (f32[1025,384]{1,0:T(8,128)S(1)}, f32[1025,384]{1,0:T(8,128)}, u32[]{:S(2)}) copy-start(f32[1025,384]{1,0:T(8,128)} %fusion.82) | copy-start | bytes 4723204
  392.7 29.8 %copy-start.142 = (f32[1025,384]{1,0:T(8,128)S(1)}, f32[1025,384]{1,0:T(8,128)}, u32[]{:S(2)}) copy-start(f32[1025,384]{1,0:T(8,128)} %fusion.96) | copy-start | bytes 4723204
  392.7 29.8 %copy-start.146 = (f32[1025,384]{1,0:T(8,128)S(1)}, f32[1025,384]{1,0:T(8,128)}, u32[]{:S(2)}) copy-start(f32[1025,384]{1,0:T(8,128)} %fusion.80) | copy-start | bytes 4723204
  458.5 15.2 %all-to-all-start.2 = ((bf16[2,2,98304]{2,1,0:T(2,128)(2,1)}), bf16[2,2,98304]{2,1,0:T(2,128)(2,1)S(1)}, u32[]{:S(2)}, u32[]{:S(2)}) async-start(bf16[2,2,98304]{2,1,0:T(2,128)(2,1)} %reshape.973), calls=%async_computation.2 | async-start | bytes 1572864 | tf_op jit(solution)/shard_map/all_to_all | solution.py:175
  462.1 656.0 %reduce-scatter.7.cloned.1.call-start = ((), (), s32[]{:S(2)}) async-start(), calls=%async_computation.18 | async-start | bytes 1253376 | tf_op jit(solution)/shard_map/reduce_scatter | solution.py:260
  481.0 73.9 %copy-start.11 = (f32[1,512,768]{2,1,0:T(8,128)}, f32[1,512,768]{2,1,0:T(8,128)S(1)}, u32[]{:S(2)}) copy-start(f32[1,512,768]{2,1,0:T(8,128)S(1)} %get-tuple-element.82) | copy-start | bytes 4718596
  481.1 73.9 %copy-start.76 = (f32[512]{0:T(512)}, f32[512]{0:T(512)S(1)}, u32[]{:S(2)}) copy-start(f32[512]{0:T(512)S(1)} %broadcast_multiply_fusion.6) | copy-start | bytes 6148
  481.4 73.6 %copy-start.86 = (f32[512]{0:T(512)}, f32[512]{0:T(512)S(1)}, u32[]{:S(2)}) copy-start(f32[512]{0:T(512)S(1)} %fusion.272) | copy-start | bytes 6148
  484.8 70.1 %copy-start.36 = (f32[1,512,768]{2,1,0:T(8,128)}, f32[1,512,768]{2,1,0:T(8,128)S(1)}, u32[]{:S(2)}) copy-start(f32[1,512,768]{2,1,0:T(8,128)S(1)} %get-tuple-element.77) | copy-start | bytes 4718596
  484.9 70.1 %copy-start.92 = (f32[512]{0:T(512)}, f32[512]{0:T(512)S(1)}, u32[]{:S(2)}) copy-start(f32[512]{0:T(512)S(1)} %broadcast_multiply_fusion.4) | copy-start | bytes 6148
  485.6 69.4 %copy-start.109 = (f32[512]{0:T(512)}, f32[512]{0:T(512)S(1)}, u32[]{:S(2)}) copy-start(f32[512]{0:T(512)S(1)} %fusion.274) | copy-start | bytes 6148
  579.4 24.4 %all-to-all-start.9 = ((bf16[2,2,98304]{2,1,0:T(2,128)(2,1)}), bf16[2,2,98304]{2,1,0:T(2,128)(2,1)}, u32[]{:S(2)}, u32[]{:S(2)}) async-start(bf16[2,2,98304]{2,1,0:T(2,128)(2,1)} %reshape.981), calls=%async_computation.9 | async-start | bytes 1572864 | tf_op jit(solution)/shard_map/all_to_all | solution.py:202
  583.9 534.3 %reduce-scatter.13.cloned.1.call-start = ((), (), s32[]{:S(2)}) async-start(), calls=%async_computation.21 | async-start | bytes 1253376 | tf_op jit(solution)/shard_map/reduce_scatter | solution.py:269
  603.7 55.3 %all-to-all-start.6 = ((bf16[2,2,98304]{2,1,0:T(2,128)(2,1)}), bf16[2,2,98304]{2,1,0:T(2,128)(2,1)S(1)}, u32[]{:S(2)}, u32[]{:S(2)}) async-start(bf16[2,2,98304]{2,1,0:T(2,128)(2,1)} %reshape.975), calls=%async_computation.6 | async-start | bytes 1572864 | tf_op jit(solution)/shard_map/all_to_all | solution.py:202
  612.6 23.3 %copy-start.61 = (bf16[1,2,512,384]{3,2,1,0:T(8,128)(2,1)S(1)}, bf16[1,2,512,384]{3,2,1,0:T(8,128)(2,1)}, u32[]{:S(2)}) copy-start(bf16[1,2,512,384]{3,2,1,0:T(8,128)(2,1)} %copy.256) | copy-start | bytes 2359300
  686.4 23.2 %copy-start.135 = (f32[1025,384]{1,0:T(8,128)S(1)}, f32[1025,384]{1,0:T(8,128)}, u32[]{:S(2)}) copy-start(f32[1025,384]{1,0:T(8,128)} %fusion.74) | copy-start | bytes 4723204
  686.4 23.2 %copy-start.143 = (f32[1025,384]{1,0:T(8,128)S(1)}, f32[1025,384]{1,0:T(8,128)}, u32[]{:S(2)}) copy-start(f32[1025,384]{1,0:T(8,128)} %fusion.96) | copy-start | bytes 4723204
  686.5 23.2 %copy-start.147 = (f32[1025,384]{1,0:T(8,128)S(1)}, f32[1025,384]{1,0:T(8,128)}, u32[]{:S(2)}) copy-start(f32[1025,384]{1,0:T(8,128)} %fusion.80) | copy-start | bytes 4723204
  709.7 27.0 %copy-start.30 = (f32[8,136,384]{2,1,0:T(8,128)S(1)}, f32[8,136,384]{2,1,0:T(8,128)}, u32[]{:S(2)}) copy-start(f32[8,136,384]{2,1,0:T(8,128)} %copy-done.29) | copy-start | bytes 5013508
  736.7 26.9 %copy-start.7 = (f32[1,512,2,384]{3,1,2,0:T(8,128)S(1)}, f32[1,512,2,384]{3,1,2,0:T(8,128)}, u32[]{:S(2)}) copy-start(f32[1,512,2,384]{3,1,2,0:T(8,128)} %copy.242) | copy-start | bytes 4718596
  785.2 75.3 %all-to-all-start.10 = ((bf16[2,2,98304]{2,1,0:T(2,128)(2,1)}), bf16[2,2,98304]{2,1,0:T(2,128)(2,1)S(1)}, u32[]{:S(2)}, u32[]{:S(2)}) async-start(bf16[2,2,98304]{2,1,0:T(2,128)(2,1)} %reshape.983), calls=%async_computation.10 | async-start | bytes 1572864 | tf_op jit(solution)/shard_map/all_to_all | solution.py:224
  788.8 30.1 %copy-start.28 = (f32[8,136,384]{2,1,0:T(8,128)S(1)}, f32[8,136,384]{2,1,0:T(8,128)}, u32[]{:S(2)}) copy-start(f32[8,136,384]{2,1,0:T(8,128)} %copy-done.27) | copy-start | bytes 5013508
  788.8 30.1 %copy-start.137 = (f32[1025,384]{1,0:T(8,128)S(1)}, f32[1025,384]{1,0:T(8,128)}, u32[]{:S(2)}) copy-start(f32[1025,384]{1,0:T(8,128)} %fusion.91) | copy-start | bytes 4723204
  788.8 30.1 %copy-start.139 = (f32[1025,384]{1,0:T(8,128)S(1)}, f32[1025,384]{1,0:T(8,128)}, u32[]{:S(2)}) copy-start(f32[1025,384]{1,0:T(8,128)} %fusion.76) | copy-start | bytes 4723204
  788.8 30.1 %copy-start.144 = (f32[1025,384]{1,0:T(8,128)S(1)}, f32[1025,384]{1,0:T(8,128)}, u32[]{:S(2)}) copy-start(f32[1025,384]{1,0:T(8,128)} %fusion.96) | copy-start | bytes 4723204
  788.8 30.1 %copy-start.148 = (f32[1025,384]{1,0:T(8,128)S(1)}, f32[1025,384]{1,0:T(8,128)}, u32[]{:S(2)}) copy-start(f32[1025,384]{1,0:T(8,128)} %fusion.80) | copy-start | bytes 4723204
  818.9 27.3 %copy-start.63 = (bf16[1,1024,384]{2,1,0:T(8,128)(2,1)S(1)}, bf16[1,1024,384]{2,1,0:T(8,128)(2,1)}, u32[]{:S(2)}) copy-start(bf16[1,1024,384]{2,1,0:T(8,128)(2,1)} %get-tuple-element.87) | copy-start | bytes 2359300
  860.5 24.0 %all-to-all-start.11 = ((bf16[2,2,98304]{2,1,0:T(2,128)(2,1)}), bf16[2,2,98304]{2,1,0:T(2,128)(2,1)}, u32[]{:S(2)}, u32[]{:S(2)}) async-start(bf16[2,2,98304]{2,1,0:T(2,128)(2,1)} %reshape.985), calls=%async_computation.11 | async-start | bytes 1572864 | tf_op jit(solution)/shard_map/all_to_all | solution.py:225
  884.5 15.0 %all-to-all-start.7 = ((bf16[2,2,98304]{2,1,0:T(2,128)(2,1)}), bf16[2,2,98304]{2,1,0:T(2,128)(2,1)}, u32[]{:S(2)}, u32[]{:S(2)}) async-start(bf16[2,2,98304]{2,1,0:T(2,128)(2,1)} %reshape.977), calls=%async_computation.7 | async-start | bytes 1572864 | tf_op jit(solution)/shard_map/all_to_all | solution.py:224
  899.5 19.8 %all-to-all-start.8 = ((bf16[2,2,98304]{2,1,0:T(2,128)(2,1)}), bf16[2,2,98304]{2,1,0:T(2,128)(2,1)}, u32[]{:S(2)}, u32[]{:S(2)}) async-start(bf16[2,2,98304]{2,1,0:T(2,128)(2,1)} %reshape.979), calls=%async_computation.8 | async-start | bytes 1572864 | tf_op jit(solution)/shard_map/all_to_all | solution.py:225
  903.8 214.4 %reduce-scatter.9.cloned.1.call-start = ((), (), s32[]{:S(2)}) async-start(), calls=%async_computation.19 | async-start | bytes 1253376 | tf_op jit(solution)/shard_map/reduce_scatter | solution.py:263
  931.7 186.6 %reduce-scatter.11.cloned.1.call-start = ((), (), s32[]{:S(2)}) async-start(), calls=%async_computation.20 | async-start | bytes 1253376 | tf_op jit(solution)/shard_map/reduce_scatter | solution.py:266
  936.5 193.9 %reduce-scatter.15.cloned.1.call-start = ((), (), s32[]{:S(2)}) async-start(), calls=%async_computation.22 | async-start | bytes 5013504 | tf_op jit(solution)/shard_map/reduce_scatter | solution.py:275
  946.6 262.5 %reduce-scatter.17.cloned.1.call-start = ((), (), s32[]{:S(2)}) async-start(), calls=%async_computation.23 | async-start | bytes 5013504 | tf_op jit(solution)/shard_map/reduce_scatter | solution.py:278
  976.8 325.5 %all-reduce.13.cloned.1.call-start = ((), (), s32[]{:S(2)}) async-start(), calls=%async_computation.24 | async-start | bytes 303104
  977.5 35.5 %copy-start.126 = (f32[1025,384]{1,0:T(8,128)S(1)}, f32[1025,384]{1,0:T(8,128)}, u32[]{:S(2)}) copy-start(f32[1025,384]{1,0:T(8,128)} %fusion.93) | copy-start | bytes 4723204
  977.5 35.5 %copy-start.128 = (f32[1025,384]{1,0:T(8,128)S(1)}, f32[1025,384]{1,0:T(8,128)}, u32[]{:S(2)}) copy-start(f32[1025,384]{1,0:T(8,128)} %fusion.78) | copy-start | bytes 4723204
  977.5 35.5 %copy-start.130 = (f32[1025,384]{1,0:T(8,128)S(1)}, f32[1025,384]{1,0:T(8,128)}, u32[]{:S(2)}) copy-start(f32[1025,384]{1,0:T(8,128)} %fusion.98) | copy-start | bytes 4723204
  977.5 35.6 %copy-start.132 = (f32[1025,384]{1,0:T(8,128)S(1)}, f32[1025,384]{1,0:T(8,128)}, u32[]{:S(2)}) copy-start(f32[1025,384]{1,0:T(8,128)} %fusion.82) | copy-start | bytes 4723204
  977.5 35.6 %copy-start.134 = (f32[1025,384]{1,0:T(8,128)S(1)}, f32[1025,384]{1,0:T(8,128)}, u32[]{:S(2)}) copy-start(f32[1025,384]{1,0:T(8,128)} %fusion.89) | copy-start | bytes 4723204
  977.5 35.6 %copy-start.136 = (f32[1025,384]{1,0:T(8,128)S(1)}, f32[1025,384]{1,0:T(8,128)}, u32[]{:S(2)}) copy-start(f32[1025,384]{1,0:T(8,128)} %fusion.74) | copy-start | bytes 4723204
  977.5 35.6 %copy-start.138 = (f32[1025,384]{1,0:T(8,128)S(1)}, f32[1025,384]{1,0:T(8,128)}, u32[]{:S(2)}) copy-start(f32[1025,384]{1,0:T(8,128)} %fusion.91) | copy-start | bytes 4723204
  977.5 35.6 %copy-start.140 = (f32[1025,384]{1,0:T(8,128)S(1)}, f32[1025,384]{1,0:T(8,128)}, u32[]{:S(2)}) copy-start(f32[1025,384]{1,0:T(8,128)} %fusion.76) | copy-start | bytes 4723204
  1013.1 30.0 %copy-start.67 = (f32[384,64]{1,0:T(8,128)S(1)}, f32[384,64]{1,0:T(8,128)}, u32[]{:S(2)}) copy-start(f32[384,64]{1,0:T(8,128)} %copy.232) | copy-start | bytes 294916
  1013.1 30.0 %copy-start.68 = (f32[384,64]{1,0:T(8,128)S(1)}, f32[384,64]{1,0:T(8,128)}, u32[]{:S(2)}) copy-start(f32[384,64]{1,0:T(8,128)} %copy.231) | copy-start | bytes 294916
  1043.1 36.6 %copy-start.34 = (f32[1,1024,384]{2,1,0:T(8,128)S(1)}, f32[1,1024,384]{2,1,0:T(8,128)}, u32[]{:S(2)}) copy-start(f32[1,1024,384]{2,1,0:T(8,128)} %copy-done.33) | copy-start | bytes 4718596
  1043.1 36.6 %copy-start.52 = (f32[1,384,1088]{1,2,0:T(8,128)S(1)}, f32[1,384,1088]{1,2,0:T(8,128)}, u32[]{:S(2)}) copy-start(f32[1,384,1088]{1,2,0:T(8,128)} %pad_bitcast_fusion) | copy-start | bytes 5013508
  1115.6 93.5 %copy-start.89 = (f32[512]{0:T(512)S(1)}, f32[512]{0:T(512)}, u32[]{:S(2)}) copy-start(f32[512]{0:T(512)} %copy-done.88) | copy-start | bytes 6148
  1115.6 93.5 %copy-start.91 = (f32[512]{0:T(512)S(1)}, f32[512]{0:T(512)}, u32[]{:S(2)}) copy-start(f32[512]{0:T(512)} %copy-done.90) | copy-start | bytes 6148
  1118.1 225.4 %all-reduce.15.cloned.1.call-start = ((), (), s32[]{:S(2)}) async-start(), calls=%async_computation.25 | async-start | bytes 1769472 | tf_op jit(solution)/shard_map/psum | solution.py:284
  1213.2 139.1 %copy-start.1 = (bf16[768,768]{1,0:T(8,128)(2,1)S(1)}, bf16[768,768]{1,0:T(8,128)(2,1)}, u32[]{:S(2)}) copy-start(bf16[768,768]{1,0:T(8,128)(2,1)} %param.20) | copy-start | bytes 3538948
  (108 other events, 479.0 us)
Sparse Core Ops, SparseCore 0:
  565.7 58.4 reduce-scatter.6
  627.8 57.0 reduce-scatter.12
  931.8 59.6 reduce-scatter.8
  994.9 57.0 reduce-scatter.10
  1055.8 74.5 reduce-scatter.14
  1134.5 74.5 reduce-scatter.16
  1214.4 87.8 all-reduce.12
  1305.0 38.4 all-reduce.14
where the time goes:
time: 1370 us; the launch traced here: 1360 us
  matrix products  732 us (53%)
  waiting for transfers between devices  215 us (16%)
  other arithmetic  180 us (13%)
  local copies, waits for them, and re-layouts  159 us (12%)
  starting transfers between devices  51.4 us (4%)
  between operations  17.9 us (1%)
    dot_general x4, matrix products, inverse(): jnp.einsum('rfc,tf->rtc', imag_part, sin_weighted, precision=highest)  114 us
    dot_general x4, matrix products, inverse(): jnp.einsum('rfc,tf->rtc', real_part, cos_weighted, precision=highest)  106 us
    dot_general x4, matrix products, spectrum(): imag_part = -jnp.einsum('rtc,tf->rfc', signal, sin_table, precision=highest)  94.6 us
    dot_general x4, matrix products, spectrum(): real_part = jnp.einsum('rtc,tf->rfc', signal, cos_table, precision=highest)  93 us
    unnamed x9, waiting for transfers between devices  87.9 us
    unnamed x345, local copies, waits for them, and re-layouts  83.3 us
    reduce_scatter x1, waiting for transfers between devices, per_device(): lax.psum_scatter(grad_down.astype(jnp.bfloat16), 'dp', scatter_dimension=...  78.8 us
    unnamed x13, other arithmetic  77.9 us
  transfers between devices with their start and end apart: 20, of which 6 were waited for; matrix products, arithmetic and copies ran while one was open for 60% of the time, Pallas kernels for 0%

commit v1 on v0

--- a/solution.py
+++ b/solution.py
@@ -1,9 +1,731 @@
+import functools
 import math
 
 import jax
 import jax.numpy as jnp
+import numpy as np
 from jax import lax
+from jax.experimental import pallas as pl
+from jax.experimental.pallas import tpu as pltpu
 from jax.sharding import PartitionSpec as P
+
+BLOCK = 256
+CHUNK = 16
+LANES = 128
+EPS = 1e-05
+F32 = jnp.float32
+BF16 = jnp.bfloat16
+VMEM_BYTES = 60 * 1024 * 1024
+
+
+def dot(a, b):
+    return lax.dot_general(a, b, (((1,), (0,)), ((), ())), preferred_element_type=F32)
+
+
+def dot_nt(a, b):
+    return lax.dot_general(a, b, (((1,), (1,)), ((), ())), preferred_element_type=F32)
+
+
+def dot_tn(a, b):
+    return lax.dot_general(a, b, (((0,), (0,)), ((), ())), preferred_element_type=F32)
+
+
+def params():
+    return pltpu.CompilerParams(vmem_limit_bytes=VMEM_BYTES)
+
+
+def cost(flops, byte_count):
+    return pl.CostEstimate(flops=int(flops), bytes_accessed=int(byte_count), transcendentals=0)
+
+
+def transform_tables():
+    freq = np.concatenate([np.arange(0, BLOCK, 2), np.arange(1, BLOCK, 2)]).astype(np.float64)
+    time = np.arange(BLOCK, dtype=np.float64)
+    angle = (2.0 * math.pi / (2 * BLOCK)) * (freq[:, None] + 0.5) * time[None, :]
+    table = np.concatenate([np.cos(angle), -np.sin(angle)], axis=0)
+    return jnp.asarray(table, dtype=BF16), jnp.asarray(table.T.copy(), dtype=BF16)
+
+
+def norm_stats(rows):
+    center = rows - jnp.mean(rows, axis=-1, keepdims=True)
+    spread = jnp.mean(center * center, axis=-1, keepdims=True)
+    inv = lax.rsqrt(spread + EPS)
+    return center * inv, inv
+
+
+def norm_pull(grad, normed, inv, gain):
+    scaled = grad * gain
+    mean_one = jnp.mean(scaled, axis=-1, keepdims=True)
+    mean_two = jnp.mean(scaled * normed, axis=-1, keepdims=True)
+    return (scaled - mean_one - normed * mean_two) * inv
+
+
+def live_rows(length, first, count):
+    rows = lax.broadcasted_iota(jnp.int32, (count, 1), 0) + first
+    return (rows < length).astype(F32)
+
+
+def spectral_loop(channels, body):
+    half = BLOCK // 2
+    for parity in range(2):
+        sign = 1.0 if parity == 0 else -1.0
+        for lane in range(channels // LANES):
+            lanes = slice(lane * LANES, (lane + 1) * LANES)
+
+            def step(index, carry, sign=sign, lanes=lanes, parity=parity):
+                low = pl.multiple_of(parity * half + index * CHUNK, CHUNK)
+                body(sign, pl.ds(low, CHUNK), pl.ds(low + BLOCK, CHUNK), lanes)
+                return carry
+
+            lax.fori_loop(0, half // CHUNK, step, 0)
+
+
+def multiply(ar, ai, br, bi):
+    return ar * br - ai * bi, ar * bi + ai * br
+
+
+def multiply_conj(ar, ai, br, bi):
+    return ar * br + ai * bi, ar * bi - ai * br
+
+
+def spectra_body(coef_ref, rate_ref, taps_ref, table_ref, kern_out, taps_out, near, far, taps_time, spec):
+    states, channels = coef_ref.shape
+    blocks = kern_out.shape[0]
+    length = blocks * BLOCK
+    step_count = 32
+    groups = length // step_count
+    together = 8
+    near_time = lax.broadcasted_iota(jnp.int32, (step_count, 1), 0).astype(F32)
+    far_time = lax.broadcasted_iota(jnp.int32, (groups, 1), 0).astype(F32) * step_count
+
+    def fill(n, carry):
+        rate = rate_ref[pl.ds(n, 1), :]
+        near[n] = jnp.exp(-rate * near_time)
+        steps = coef_ref[pl.ds(n, 1), :] * jnp.exp(-rate * far_time)
+        for g in range(groups // together):
+            far[g, n] = steps[g * together : (g + 1) * together, :]
+        return carry
+
+    lax.fori_loop(0, states, fill, 0)
+    for lane in range(channels // LANES):
+        lanes = slice(lane * LANES, (lane + 1) * LANES)
+
+        def group_step(g, carry, lanes=lanes):
+            def add(n, sums):
+                near_n = near[n, :, lanes]
+                return tuple(
+                    sums[i] + far[g, n, i : i + 1, lanes] * near_n for i in range(together)
+                )
+
+            zeros = tuple(jnp.zeros((step_count, LANES), F32) for _ in range(together))
+            sums = lax.fori_loop(0, states, add, zeros, unroll=4)
+            for i in range(together):
+                place = pl.multiple_of((g * together + i) * step_count, step_count)
+                taps_time[pl.ds(place, step_count), lanes] = sums[i].astype(BF16)
+            return carry
+
+        lax.fori_loop(0, groups // together, group_step, 0)
+    for j in range(blocks):
+        spec[j] = dot(table_ref[...], taps_time[j * BLOCK : (j + 1) * BLOCK, :])
+    scale = 1.0 / BLOCK
+
+    def combine(sign, re, im, lanes):
+        for j in range(blocks):
+            out_re = spec[j, re, lanes]
+            out_im = spec[j, im, lanes]
+            if j > 0:
+                out_re = out_re - sign * spec[j - 1, im, lanes]
+                out_im = out_im + sign * spec[j - 1, re, lanes]
+            kern_out[j, re, lanes] = out_re * scale
+            kern_out[j, im, lanes] = out_im * scale
+
+    spectral_loop(channels, combine)
+    taps_out[...] = dot(table_ref[:, : taps_ref.shape[0]], taps_ref[...].astype(BF16)) * scale
+
+
+def spectra_call(coef, rate, taps, table, length, tile):
+    states, channels = coef.shape
+    blocks = length // BLOCK
+    column = lambda j: (0, j)
+    return pl.pallas_call(
+        spectra_body,
+        grid=(channels // tile,),
+        in_specs=[
+            pl.BlockSpec((states, tile), column),
+            pl.BlockSpec((states, tile), column),
+            pl.BlockSpec((taps.shape[0], tile), column),
+            pl.BlockSpec(table.shape, lambda j: (0, 0)),
+        ],
+        out_specs=[
+            pl.BlockSpec((blocks, 2 * BLOCK, tile), lambda j: (0, 0, j)),
+            pl.BlockSpec((2 * BLOCK, tile), column),
+        ],
+        out_shape=[
+            jax.ShapeDtypeStruct((blocks, 2 * BLOCK, channels), F32),
+            jax.ShapeDtypeStruct((2 * BLOCK, channels), F32),
+        ],
+        scratch_shapes=[
+            pltpu.VMEM((states, 32, tile), F32),
+            pltpu.VMEM((length // 256, states, 8, tile), F32),
+            pltpu.VMEM((length, tile), BF16),
+            pltpu.VMEM((blocks, 2 * BLOCK, tile), F32),
+        ],
+        compiler_params=params(),
+        cost_estimate=cost(6e9, 20e6),
+        name="spectra",
+    )(coef, rate, taps, table)
+
+
+def mixer_body(
+    length_ref, x_ref, gain_one_ref, wq_ref, wk_ref, wv_ref, wout_ref, gain_two_ref, kern_ref, tapspec_ref,
+    table_ref, back_ref,
+    a_one_ref, q_ref, k_ref, v_ref, shifted_ref, mixed_ref, state_ref, gated_ref, hidden_ref, a_two_ref,
+    total, spec, prod,
+):
+    j = pl.program_id(0)
+    length, width = x_ref.shape
+    tile = q_ref.shape[1]
+    blocks = length // BLOCK
+    live = length_ref[0]
+
+    @pl.when(j == 0)
+    def _():
+        for b in range(blocks):
+            rows = slice(b * BLOCK, (b + 1) * BLOCK)
+            normed, _ = norm_stats(x_ref[rows, :].astype(F32))
+            a_one_ref[rows, :] = (normed * gain_one_ref[...]).astype(BF16)
+        total[...] = jnp.zeros_like(total)
+
+    for b in range(blocks):
+        rows = slice(b * BLOCK, (b + 1) * BLOCK)
+        mask = live_rows(live, b * BLOCK, BLOCK)
+        a_rows = a_one_ref[rows, :]
+        k_ref[rows, :] = (dot(a_rows, wk_ref[...]) * mask).astype(BF16)
+        v_ref[rows, :] = (dot(a_rows, wv_ref[...]) * mask).astype(BF16)
+        q_ref[rows, :] = dot(a_rows, wq_ref[...]).astype(BF16)
+        spec[b] = dot(table_ref[...], k_ref[rows, :])
+
+    def shift_product(sign, re, im, lanes):
+        tr = tapspec_ref[re, lanes]
+        ti = tapspec_ref[im, lanes]
+        before = None
+        for b in range(blocks):
+            xr = spec[b, re, lanes]
+            xi = spec[b, im, lanes]
+            if b == 0:
+                sr, si = xr, xi
+            else:
+                sr, si = xr - sign * before[1], xi + sign * before[0]
+            before = (xr, xi)
+            yr, yi = multiply(sr, si, tr, ti)
+            prod[b, re, lanes] = yr.astype(BF16)
+            prod[b, im, lanes] = yi.astype(BF16)
+
+    spectral_loop(tile, shift_product)
+    for b in range(blocks):
+        rows = slice(b * BLOCK, (b + 1) * BLOCK)
+        shifted = dot(back_ref[...], prod[b])
+        shifted_ref[rows, :] = shifted.astype(BF16)
+        mixed_ref[rows, :] = (shifted * v_ref[rows, :].astype(F32)).astype(BF16)
+        spec[b] = dot(table_ref[...], mixed_ref[rows, :])
+
+    def state_product(sign, re, im, lanes):
+        x = [(spec[b, re, lanes], spec[b, im, lanes]) for b in range(blocks)]
+        h = [(kern_ref[b, re, lanes], kern_ref[b, im, lanes]) for b in range(blocks)]
+        for i in range(blocks):
+            yr, yi = multiply(*x[i], *h[0])
+            for d in range(1, i + 1):
+                pr, pi = multiply(*x[i - d], *h[d])
+                yr, yi = yr + pr, yi + pi
+            prod[i, re, lanes] = yr.astype(BF16)
+            prod[i, im, lanes] = yi.astype(BF16)
+
+    spectral_loop(tile, state_product)
+    for b in range(blocks):
+        rows = slice(b * BLOCK, (b + 1) * BLOCK)
+        state = dot(back_ref[...], prod[b]).astype(BF16)
+        state_ref[rows, :] = state
+        gated_ref[rows, :] = (q_ref[rows, :].astype(F32) * state.astype(F32)).astype(BF16)
+        total[rows, :] += dot(gated_ref[rows, :], wout_ref[...])
+
+    @pl.when(j == pl.num_programs(0) - 1)
+    def _():
+        for b in range(blocks):
+            rows = slice(b * BLOCK, (b + 1) * BLOCK)
+            mask = live_rows(live, b * BLOCK, BLOCK)
+            hidden = x_ref[rows, :].astype(F32) + mask * total[rows, :]
+            hidden_ref[rows, :] = hidden
+            normed, _ = norm_stats(hidden)
+            a_two_ref[rows, :] = (normed * gain_two_ref[...]).astype(BF16)
+
+
+def mixer_call(live, x, gain_one, wq, wk, wv, wout, gain_two, kern, tapspec, tables, tile):
+    length, width = x.shape
+    blocks = length // BLOCK
+    table, back = tables
+    whole = lambda j, n: (0, 0)
+    column = lambda j, n: (0, j)
+    rows_full = pl.BlockSpec((length, width), whole)
+    rows_tile = pl.BlockSpec((length, tile), column)
+    gain_spec = pl.BlockSpec((1, width), whole)
+    low = jax.ShapeDtypeStruct((length, width), BF16)
+    return pl.pallas_call(
+        mixer_body,
+        grid_spec=pltpu.PrefetchScalarGridSpec(
+            num_scalar_prefetch=1,
+            grid=(width // tile,),
+            in_specs=[
+                rows_full,
+                gain_spec,
+                pl.BlockSpec((width, tile), column),
+                pl.BlockSpec((width, tile), column),
+                pl.BlockSpec((width, tile), column),
+                pl.BlockSpec((tile, width), lambda j, n: (j, 0)),
+                gain_spec,
+                pl.BlockSpec((blocks, 2 * BLOCK, tile), lambda j, n: (0, 0, j)),
+                pl.BlockSpec((2 * BLOCK, tile), column),
+                pl.BlockSpec(table.shape, whole),
+                pl.BlockSpec(back.shape, whole),
+            ],
+            out_specs=[rows_full] + [rows_tile] * 7 + [rows_full] * 2,
+            scratch_shapes=[
+                pltpu.VMEM((length, width), F32),
+                pltpu.VMEM((blocks, 2 * BLOCK, tile), F32),
+                pltpu.VMEM((blocks, 2 * BLOCK, tile), BF16),
+            ],
+        ),
+        out_shape=[low] * 8 + [jax.ShapeDtypeStruct((length, width), F32), low],
+        compiler_params=params(),
+        cost_estimate=cost(10e9, 30e6),
+        name="mixer_forward",
+    )(live, x, gain_one, wq, wk, wv, wout, gain_two, kern, tapspec, table, back)
+
+
+def gelu_pair(x):
+    bell = jnp.exp(x * x * -0.5)
+    size = jnp.abs(x)
+    t = 1.0 / (1.0 + (0.3275911 / math.sqrt(2.0)) * size)
+    poly = t * (
+        0.5 * 0.254829592
+        + t * (0.5 * -0.284496736 + t * (0.5 * 1.421413741 + t * (0.5 * -1.453152027 + t * (0.5 * 1.061405429))))
+    )
+    tail = poly * bell
+    phi = jnp.where(x >= 0.0, 1.0 - tail, tail)
+    return x * phi, phi + x * bell * (1.0 / math.sqrt(2.0 * math.pi))
+
+
+def share_out(grad, send_ref, keep_ref, mine, share):
+    bits = [send_ref.shape[i] for i in range(send_ref.ndim - 3)]
+    count = math.prod(bits)
+    for half, ref in ((0, keep_ref), (1, send_ref)):
+        for spot in range(count):
+            relative, left, place = 0, spot, []
+            for size in reversed(bits):
+                place.append(left % size)
+                left //= size
+            place = place[::-1]
+            for axis, bit in enumerate(place):
+                relative += bit << axis
+            owner = jnp.bitwise_xor(mine, 2 * relative + half)
+            low = pl.multiple_of(owner * share, share)
+            ref[(*place, 0)] = grad[pl.ds(low, share), :].astype(BF16)
+
+
+def ffn_body(
+    length_ref, place_ref, a_two_ref, cot_ref, hidden_ref, up_ref, down_ref,
+    out_ref, d_pre_ref, send_ref, keep_ref, total, act, d_down, grad,
+):
+    j = pl.program_id(0)
+    length, width = a_two_ref.shape
+    tile = up_ref.shape[1]
+    live = length_ref[0]
+    rows_count = 256
+
+    @pl.when(j == 0)
+    def _():
+        for low in range(0, length, rows_count):
+            rows = slice(low, low + rows_count)
+            d_down[rows, :] = (cot_ref[rows, :].astype(F32) * live_rows(live, low, rows_count)).astype(BF16)
+        total[...] = jnp.zeros_like(total)
+
+    for low in range(0, length, rows_count):
+        rows = slice(low, low + rows_count)
+        pre = dot(a_two_ref[rows, :], up_ref[...])
+        d_act = dot_nt(d_down[rows, :], down_ref[...])
+        value, slope = gelu_pair(pre)
+        act[rows, :] = value.astype(BF16)
+        d_pre_ref[rows, :] = (d_act * slope).astype(BF16)
+        total[rows, :] += dot(act[rows, :], down_ref[...])
+    grad[...] = dot_tn(act[...], d_down[...])
+    share = tile // 4
+    share_out(grad, send_ref.at[:, 0], keep_ref.at[:, 0], place_ref[0] & 3, share)
+
+    @pl.when(j == pl.num_programs(0) - 1)
+    def _():
+        for low in range(0, length, rows_count):
+            rows = slice(low, low + rows_count)
+            mask = live_rows(live, low, rows_count)
+            out_ref[rows, :] = (hidden_ref[rows, :] + mask * total[rows, :]).astype(BF16)
+
+
+def ffn_call(live, place, a_two, cot, hidden, up, down):
+    length, width = a_two.shape
+    hidden_units = up.shape[1]
+    tile = hidden_units // 4
+    share = tile // 4
+    whole = lambda j, n, p: (0, 0)
+    rows_full = pl.BlockSpec((length, width), whole)
+
+    def z_place(j, n, p):
+        z = jnp.bitwise_xor(j, p[0] >> 2)
+        return (0, z & 1, z >> 1, 0, 0)
+
+    half_spec = pl.BlockSpec((2, 1, 1, share, width), z_place)
+    half_shape = jax.ShapeDtypeStruct((2, 2, 2, share, width), BF16)
+    return pl.pallas_call(
+        ffn_body,
+        grid_spec=pltpu.PrefetchScalarGridSpec(
+            num_scalar_prefetch=2,
+            grid=(4,),
+            in_specs=[
+                rows_full,
+                rows_full,
+                rows_full,
+                pl.BlockSpec((width, tile), lambda j, n, p: (0, j)),
+                pl.BlockSpec((tile, width), lambda j, n, p: (j, 0)),
+            ],
+            out_specs=[
+                rows_full,
+                pl.BlockSpec((length, tile), lambda j, n, p: (0, j)),
+                half_spec,
+                half_spec,
+            ],
+            scratch_shapes=[
+                pltpu.VMEM((length, width), F32),
+                pltpu.VMEM((length, tile), BF16),
+                pltpu.VMEM((length, width), BF16),
+                pltpu.VMEM((tile, width), F32),
+            ],
+        ),
+        out_shape=[
+            jax.ShapeDtypeStruct((length, width), BF16),
+            jax.ShapeDtypeStruct((length, hidden_units), BF16),
+            half_shape,
+            half_shape,
+        ],
+        compiler_params=params(),
+        cost_estimate=cost(8 * length * width * hidden_units, 40e6),
+        name="feed_forward",
+    )(live, place, a_two, cot, hidden, up, down)
+
+
+def ffn_back_body(
+    length_ref, place_ref, a_two_ref, d_pre_ref, up_ref, cot_ref, hidden_ref, gain_ref,
+    d_hidden_ref, d_mixer_ref, gain_grad_ref, send_ref, keep_ref, total, grad,
+):
+    j = pl.program_id(0)
+    length, width = a_two_ref.shape
+    live = length_ref[0]
+    rows_count = 256
+    grad[...] = dot_tn(a_two_ref[...], d_pre_ref[...])
+    share_out(grad, send_ref, keep_ref, place_ref[0], send_ref.shape[-2])
+
+    @pl.when(j == 0)
+    def _():
+        total[...] = jnp.zeros_like(total)
+
+    for low in range(0, length, rows_count):
+        rows = slice(low, low + rows_count)
+        total[rows, :] += dot_nt(d_pre_ref[rows, :], up_ref[...])
+
+    @pl.when(j == pl.num_programs(0) - 1)
+    def _():
+        gain_sum = jnp.zeros((1, width), F32)
+        for low in range(0, length, rows_count):
+            rows = slice(low, low + rows_count)
+            mask = live_rows(live, low, rows_count)
+            normed, inv = norm_stats(hidden_ref[rows, :])
+            grad_in = total[rows, :]
+            gain_sum = gain_sum + jnp.sum(grad_in * normed, axis=0, keepdims=True)
+            d_hidden = cot_ref[rows, :].astype(F32) + norm_pull(grad_in, normed, inv, gain_ref[...])
+            d_hidden_ref[rows, :] = d_hidden
+            d_mixer_ref[rows, :] = (mask * d_hidden).astype(BF16)
+        gain_grad_ref[...] = gain_sum
+
+
+def ffn_back_call(live, place, a_two, d_pre, up, cot, hidden, gain):
+    length, width = a_two.shape
+    hidden_units = up.shape[1]
+    tile = hidden_units // 4
+    share = width // 16
+    whole = lambda j, n, p: (0, 0)
+    rows_full = pl.BlockSpec((length, width), whole)
+    half_spec = pl.BlockSpec((2, 2, 2, 1, share, tile), lambda j, n, p: (0, 0, 0, j, 0, 0))
+    half_shape = jax.ShapeDtypeStruct((2, 2, 2, 4, share, tile), BF16)
+    return pl.pallas_call(
+        ffn_back_body,
+        grid_spec=pltpu.PrefetchScalarGridSpec(
+            num_scalar_prefetch=2,
+            grid=(4,),
+            in_specs=[
+                rows_full,
+                pl.BlockSpec((length, tile), lambda j, n, p: (0, j)),
+                pl.BlockSpec((width, tile), lambda j, n, p: (0, j)),
+                rows_full,
+                rows_full,
+                pl.BlockSpec((1, width), whole),
+            ],
+            out_specs=[rows_full, rows_full, pl.BlockSpec((1, width), whole), half_spec, half_spec],
+            scratch_shapes=[pltpu.VMEM((length, width), F32), pltpu.VMEM((width, tile), F32)],
+        ),
+        out_shape=[
+            jax.ShapeDtypeStruct((length, width), F32),
+            jax.ShapeDtypeStruct((length, width), BF16),
+            jax.ShapeDtypeStruct((1, width), F32),
+            half_shape,
+            half_shape,
+        ],
+        compiler_params=params(),
+        cost_estimate=cost(4 * length * width * hidden_units, 40e6),
+        name="feed_forward_back",
+    )(live, place, a_two, d_pre, up, cot, hidden, gain)
+
+
+def gate_back_body(
+    place_ref, d_mixer_ref, wout_ref, state_ref, q_ref, gated_ref, a_one_ref,
+    d_query_ref, d_state_ref, send_ref, keep_ref, grad,
+):
+    length, width = d_mixer_ref.shape
+    rows_count = 256
+    share = width // 16
+    mine = place_ref[0]
+    grad[...] = dot_tn(gated_ref[...], d_mixer_ref[...])
+    share_out(grad, send_ref.at[:, :, :, 0:1], keep_ref.at[:, :, :, 0:1], mine, share)
+    for low in range(0, length, rows_count):
+        rows = slice(low, low + rows_count)
+        d_gated = dot_nt(d_mixer_ref[rows, :], wout_ref[...])
+        d_query_ref[rows, :] = (d_gated * state_ref[rows, :].astype(F32)).astype(BF16)
+        d_state_ref[rows, :] = (d_gated * q_ref[rows, :].astype(F32)).astype(BF16)
+    grad[...] = dot_tn(a_one_ref[...], d_query_ref[...])
+    share_out(grad, send_ref.at[:, :, :, 1:2], keep_ref.at[:, :, :, 1:2], mine, share)
+
+
+def gate_back_call(place, d_mixer, wout, state, q, gated, a_one):
+    length, width = d_mixer.shape
+    share = width // 16
+    whole = lambda i, p: (0, 0)
+    rows_full = pl.BlockSpec((length, width), whole)
+    half_spec = pl.BlockSpec((2, 2, 2, 2, share, width), lambda i, p: (0, 0, 0, 0, 0, 0))
+    half_shape = jax.ShapeDtypeStruct((2, 2, 2, 2, share, width), BF16)
+    low = jax.ShapeDtypeStruct((length, width), BF16)
+    return pl.pallas_call(
+        gate_back_body,
+        grid_spec=pltpu.PrefetchScalarGridSpec(
+            num_scalar_prefetch=1,
+            grid=(1,),
+            in_specs=[rows_full, pl.BlockSpec(wout.shape, whole)] + [rows_full] * 4,
+            out_specs=[rows_full, rows_full, half_spec, half_spec],
+            scratch_shapes=[pltpu.VMEM((width, width), F32)],
+        ),
+        out_shape=[low, low, half_shape, half_shape],
+        compiler_params=params(),
+        cost_estimate=cost(6 * length * width * width, 15e6),
+        name="gate_back",
+    )(place, d_mixer, wout, state, q, gated, a_one)
+
+
+def mixer_back_body(
+    length_ref, place_ref, d_state_ref, d_query_ref, mixed_ref, shifted_ref, k_ref, v_ref, a_one_ref,
+    wq_ref, wk_ref, wv_ref, kern_ref, tapspec_ref, table_ref, back_ref, x_ref, gain_ref, d_hidden_ref,
+    d_x_ref, gain_grad_ref, d_taps_ref, send_ref, keep_ref, dk_send_ref, dk_keep_ref,
+    total, spec_one, spec_two, prod, kern_prod, d_keys, d_values, grad, d_kern,
+):
+    j = pl.program_id(0)
+    length, width = a_one_ref.shape
+    tile = k_ref.shape[1]
+    blocks = length // BLOCK
+    live = length_ref[0]
+    mine = place_ref[0]
+
+    for b in range(blocks):
+        rows = slice(b * BLOCK, (b + 1) * BLOCK)
+        spec_one[b] = dot(table_ref[...], d_state_ref[rows, :])
+        spec_two[b] = dot(table_ref[...], mixed_ref[rows, :])
+
+    def state_product(sign, re, im, lanes):
+        s = [(spec_one[b, re, lanes], spec_one[b, im, lanes]) for b in range(blocks)]
+        h = [(kern_ref[b, re, lanes], kern_ref[b, im, lanes]) for b in range(blocks)]
+        for b in range(blocks):
+            yr, yi = multiply_conj(*h[0], *s[b])
+            for i in range(b + 1, blocks):
+                pr, pi = multiply_conj(*h[i - b], *s[i])
+                yr, yi = yr + pr, yi + pi
+            prod[b, re, lanes] = yr.astype(BF16)
+            prod[b, im, lanes] = yi.astype(BF16)
+
+    spectral_loop(tile, state_product)
+
+    def kernel_product(sign, re, im, lanes):
+        s = [(spec_one[b, re, lanes], spec_one[b, im, lanes]) for b in range(blocks)]
+        x = [(spec_two[b, re, lanes], spec_two[b, im, lanes]) for b in range(blocks)]
+        after = None
+        for d in range(blocks - 1, -1, -1):
+            yr, yi = multiply_conj(*x[0], *s[d])
+            for i in range(d + 1, blocks):
+                pr, pi = multiply_conj(*x[i - d], *s[i])
+                yr, yi = yr + pr, yi + pi
+            if after is None:
+                hr, hi = yr, yi
+            else:
+                hr, hi = yr + sign * after[1], yi - sign * after[0]
+            after = (yr, yi)
+            kern_prod[d, re, lanes] = hr.astype(BF16)
+            kern_prod[d, im, lanes] = hi.astype(BF16)
+
+    spectral_loop(tile, kernel_product)
+    for b in range(blocks):
+        rows = slice(b * BLOCK, (b + 1) * BLOCK)
+        mask = live_rows(live, b * BLOCK, BLOCK)
+        d_mixed = dot(back_ref[...], prod[b]).astype(BF16).astype(F32)
+        d_values[rows, :] = (mask * d_mixed * shifted_ref[rows, :].astype(F32)).astype(BF16)
+        d_shifted = (d_mixed * v_ref[rows, :].astype(F32)).astype(BF16)
+        spec_one[b] = dot(table_ref[...], d_shifted)
+        spec_two[b] = dot(table_ref[...], k_ref[rows, :])
+        d_kern[rows, :] = dot(back_ref[...], kern_prod[b]) * (1.0 / BLOCK)
+
+    def shift_product(sign, re, im, lanes):
+        tr = tapspec_ref[re, lanes]
+        ti = tapspec_ref[im, lanes]
+        s = [(spec_one[b, re, lanes], spec_one[b, im, lanes]) for b in range(blocks)]
+        x = [(spec_two[b, re, lanes], spec_two[b, im, lanes]) for b in range(blocks)]
+        u = [multiply_conj(tr, ti, *s[b]) for b in range(blocks)]
+        sum_re, sum_im = multiply_conj(*x[0], *s[0])
+        for b in range(blocks):
+            yr, yi = u[b]
+            if b < blocks - 1:
+                yr, yi = yr + sign * u[b + 1][1], yi - sign * u[b + 1][0]
+            prod[b, re, lanes] = yr.astype(BF16)
+            prod[b, im, lanes] = yi.astype(BF16)
+            if b > 0:
+                wr = x[b][0] - sign * x[b - 1][1]
+                wi = x[b][1] + sign * x[b - 1][0]
+                pr, pi = multiply_conj(wr, wi, *s[b])
+                sum_re, sum_im = sum_re + pr, sum_im + pi
+        kern_prod[0, re, lanes] = sum_re.astype(BF16)
+        kern_prod[0, im, lanes] = sum_im.astype(BF16)
+
+    spectral_loop(tile, shift_product)
+    for b in range(blocks):
+        rows = slice(b * BLOCK, (b + 1) * BLOCK)
+        mask = live_rows(live, b * BLOCK, BLOCK)
+        d_keys[rows, :] = (mask * dot(back_ref[...], prod[b])).astype(BF16)
+    taps = d_taps_ref.shape[0]
+    d_taps_ref[...] = dot(back_ref[:taps, :], kern_prod[0]) * (1.0 / BLOCK)
+
+    share_out(d_kern, dk_send_ref, dk_keep_ref, mine, length // 16)
+    share = width // 16
+    grad[...] = dot_tn(a_one_ref[...], d_keys[...])
+    share_out(grad, send_ref.at[:, :, :, 0:1], keep_ref.at[:, :, :, 0:1], mine, share)
+    grad[...] = dot_tn(a_one_ref[...], d_values[...])
+    share_out(grad, send_ref.at[:, :, :, 1:2], keep_ref.at[:, :, :, 1:2], mine, share)
+
+    @pl.when(j == 0)
+    def _():
+        total[...] = jnp.zeros_like(total)
+
+    for b in range(blocks):
+        rows = slice(b * BLOCK, (b + 1) * BLOCK)
+        total[rows, :] += (
+            dot_nt(d_query_ref[rows, :], wq_ref[...])
+            + dot_nt(d_keys[rows, :], wk_ref[...])
+            + dot_nt(d_values[rows, :], wv_ref[...])
+        )
+
+    @pl.when(j == pl.num_programs(0) - 1)
+    def _():
+        gain_sum = jnp.zeros((1, width), F32)
+        for b in range(blocks):
+            rows = slice(b * BLOCK, (b + 1) * BLOCK)
+            normed, inv = norm_stats(x_ref[rows, :].astype(F32))
+            grad_in = total[rows, :]
+            gain_sum = gain_sum + jnp.sum(grad_in * normed, axis=0, keepdims=True)
+            d_x_ref[rows, :] = (d_hidden_ref[rows, :] + norm_pull(grad_in, normed, inv, gain_ref[...])).astype(BF16)
+        gain_grad_ref[...] = gain_sum
+
+
+def mixer_back_call(
+    live, place, d_state, d_query, mixed, shifted, k, v, a_one, wq, wk, wv, kern, tapspec, tables, x, gain, d_hidden,
+    taps_count, tile
+):
+    length, width = a_one.shape
+    blocks = length // BLOCK
+    table, back = tables
+    share = width // 16
+    whole = lambda j, n, p: (0, 0)
+    column = lambda j, n, p: (0, j)
+    rows_full = pl.BlockSpec((length, width), whole)
+    rows_tile = pl.BlockSpec((length, tile), column)
+    weight = pl.BlockSpec((width, tile), column)
+    half_spec = pl.BlockSpec((2, 2, 2, 2, share, tile), lambda j, n, p: (0, 0, 0, 0, 0, j))
+    half_shape = jax.ShapeDtypeStruct((2, 2, 2, 2, share, width), BF16)
+    kern_spec = pl.BlockSpec((2, 2, 2, 1, length // 16, tile), lambda j, n, p: (0, 0, 0, 0, 0, j))
+    kern_shape = jax.ShapeDtypeStruct((2, 2, 2, 1, length // 16, width), BF16)
+    spectrum = pltpu.VMEM((blocks, 2 * BLOCK, tile), F32)
+    spectrum_low = pltpu.VMEM((blocks, 2 * BLOCK, tile), BF16)
+    return pl.pallas_call(
+        mixer_back_body,
+        grid_spec=pltpu.PrefetchScalarGridSpec(
+            num_scalar_prefetch=2,
+            grid=(width // tile,),
+            in_specs=[rows_tile] * 6
+            + [rows_full, weight, weight, weight]
+            + [
+                pl.BlockSpec((blocks, 2 * BLOCK, tile), lambda j, n, p: (0, 0, j)),
+                pl.BlockSpec((2 * BLOCK, tile), column),
+                pl.BlockSpec(table.shape, whole),
+                pl.BlockSpec(back.shape, whole),
+                rows_full,
+                pl.BlockSpec((1, width), whole),
+                rows_full,
+            ],
+            out_specs=[
+                rows_full,
+                pl.BlockSpec((1, width), whole),
+                pl.BlockSpec((taps_count, tile), column),
+                half_spec,
+                half_spec,
+                kern_spec,
+                kern_spec,
+            ],
+            scratch_shapes=[
+                pltpu.VMEM((length, width), F32),
+                spectrum,
+                spectrum,
+                spectrum_low,
+                spectrum_low,
+                pltpu.VMEM((length, tile), BF16),
+                pltpu.VMEM((length, tile), BF16),
+                pltpu.VMEM((width, tile), F32),
+                pltpu.VMEM((length, tile), F32),
+            ],
+        ),
+        out_shape=[
+            jax.ShapeDtypeStruct((length, width), BF16),
+            jax.ShapeDtypeStruct((1, width), F32),
+            jax.ShapeDtypeStruct((taps_count, width), F32),
+            half_shape,
+            half_shape,
+            kern_shape,
+            kern_shape,
+        ],
+        compiler_params=params(),
+        cost_estimate=cost(16e9, 40e6),
+        name="mixer_back",
+    )(
+        live, place, d_state, d_query, mixed, shifted, k, v, a_one, wq, wk, wv, kern, tapspec, table, back, x, gain,
+        d_hidden,
+    )
+
 
 MICRO = 2
 
@@ -103,7 +825,7 @@
     return first - second
 
 
-def per_device(
+def split_channels(
     tokens,
     lengths,
     gain_one,
@@ -308,6 +1030,159 @@
     )
 
 
+def add_low(a, b):
+    return (a.astype(F32) + b.astype(F32)).astype(BF16)
+
+
+def swap(value, axis_name, bit):
+    count = lax.axis_size(axis_name)
+    return lax.ppermute(value, axis_name, [(i, i ^ bit) for i in range(count)])
+
+
+def halve(value, axis, bit):
+    index = [slice(None)] * value.ndim
+    index[axis] = 1
+    given = swap(value[tuple(index)], "dp", bit)
+    index[axis] = 0
+    return add_low(value[tuple(index)], given)
+
+
+def reduce_shares(send, keep, cut):
+    joined = add_low(keep, swap(send, "dp", 1))
+    axis, low = cut
+    cuts = [slice(None)] * joined.ndim
+    results = []
+    for first in (True, False):
+        cuts[axis] = slice(0, low) if first else slice(low, None)
+        part = joined[tuple(cuts)]
+        if first:
+            part = halve(part, 0, 2)
+            part = halve(part, 0, 4)
+            part = halve(part, 0, 8)
+        else:
+            part = halve(part, 1, 4)
+            part = halve(part, 1, 8)
+            part = halve(part, 0, 2)
+        part = part.astype(F32) + swap(part, "seq", 1).astype(F32)
+        results.append(part)
+    return jnp.concatenate(results, axis=axis - 3)
+
+
+def reduce_small(value, place):
+    count = value.shape[0]
+    order = jnp.bitwise_xor(lax.iota(jnp.int32, count), place)
+    value = jnp.take(value, order, axis=0)
+    bit = count // 2
+    while bit >= 1:
+        value = value[:bit] + swap(value[bit:], "dp", bit)
+        bit //= 2
+    return value[0]
+
+
+def whole_row(own, given, side):
+    return jnp.where(
+        side == 0, jnp.concatenate([own, given], axis=0), jnp.concatenate([given, own], axis=0)
+    )
+
+
+def exchange_rows(rows, side):
+    own = lax.dynamic_index_in_dim(rows, side, 0, keepdims=False)
+    other = lax.dynamic_index_in_dim(rows, 1 - side, 0, keepdims=False)
+    return whole_row(own, swap(other, "seq", 1), side)
+
+
+def return_rows(row, side):
+    half = row.shape[0] // 2
+    own = lax.dynamic_slice_in_dim(row, side * half, half, 0)
+    other = lax.dynamic_slice_in_dim(row, (1 - side) * half, half, 0)
+    given = swap(other, "seq", 1)
+    return jnp.where(side == 0, jnp.stack([own, given]), jnp.stack([given, own]))
+
+
+def split_rows(
+    tokens, lengths, gain_one, w_query, w_key, w_value, w_out, gain_two, w_up, w_down,
+    shift_taps, diag_coef, diag_rate, cotangent,
+):
+    side = lax.axis_index("seq")
+    mine = lax.axis_index("dp")
+    devices = lax.axis_size("dp")
+    width = tokens.shape[2]
+    length = tokens.shape[1] * 2
+    channels, states = diag_coef.shape
+    tile = 256
+    tables = transform_tables()
+    place = jnp.reshape(mine, (1,)).astype(jnp.int32)
+    live = lax.dynamic_slice_in_dim(lengths, side, 1, 0)
+    x = exchange_rows(tokens, side)
+    packed = jnp.stack([diag_coef.T, diag_rate.T, shift_taps.T])
+    packed_other = swap(packed, "seq", 1)
+    packed_all = jnp.where(
+        side == 0,
+        jnp.concatenate([packed, packed_other], axis=2),
+        jnp.concatenate([packed_other, packed], axis=2),
+    )
+    coef, rate, taps = packed_all[0], packed_all[1], packed_all[2]
+    cot = exchange_rows(cotangent, side)
+    kern, tapspec = spectra_call(coef, rate, taps, tables[0], length, tile)
+    row_one = gain_one[None, :]
+    row_two = gain_two[None, :]
+    a_one, q, k, v, shifted, mixed, state, gated, hidden, a_two = mixer_call(
+        live, x, row_one, w_query, w_key, w_value, w_out, row_two, kern, tapspec, tables, tile
+    )
+    out_row, d_pre, down_send, down_keep = ffn_call(live, place, a_two, cot, hidden, w_up, w_down)
+    out = return_rows(out_row, side)
+    share = w_down.shape[0] // devices
+    down = reduce_shares(down_send[:, :, :, None], down_keep[:, :, :, None], (4, 112))
+    d_hidden, d_mixer, d_gain_two, up_send, up_keep = ffn_back_call(
+        live, place, a_two, d_pre, w_up, cot, hidden, row_two
+    )
+    up = reduce_shares(up_send, up_keep, (3, 2))
+    d_query, d_state, gate_send, gate_keep = gate_back_call(place, d_mixer, w_out, state, q, gated, a_one)
+    gate = reduce_shares(gate_send, gate_keep, (3, 1))
+    d_row, d_gain_one, d_taps, kv_send, kv_keep, kern_send, kern_keep = mixer_back_call(
+        live, place, d_state, d_query, mixed, shifted, k, v, a_one, w_query, w_key, w_value, kern, tapspec, tables,
+        x, row_one, d_hidden, states, tile,
+    )
+    d_tokens = return_rows(d_row, side)
+    d_kern = reduce_shares(kern_send, kern_keep, (4, 32))[0]
+    kv = reduce_shares(kv_send, kv_keep, (3, 1))
+
+    d_kern_half = lax.dynamic_slice_in_dim(d_kern, side * channels, channels, 1)
+    steps = (mine * d_kern.shape[0] + lax.iota(jnp.int32, d_kern.shape[0])).astype(F32)
+    decay = jnp.exp(-diag_rate.T[None] * steps[:, None, None]) * d_kern_half[:, None, :]
+    coef_part = jnp.sum(decay, axis=0)
+    rate_part = -diag_coef.T * jnp.sum(decay * steps[:, None, None], axis=0)
+    each = states // devices
+    pair = jnp.concatenate(
+        [coef_part.reshape(devices, each, channels), rate_part.reshape(devices, each, channels)], axis=1
+    )
+    pair = reduce_small(pair, mine)
+
+    gain_each = width // devices
+    gains = jnp.concatenate([d_gain_one.reshape(devices, 1, gain_each), d_gain_two.reshape(devices, 1, gain_each)], axis=2)
+    gains = jnp.pad(gains, ((0, 0), (0, 0), (0, width - 2 * gain_each)))
+    small = jnp.concatenate([d_taps.reshape(devices, each, width), gains], axis=1)
+    small = reduce_small(small, mine)
+    small = small + swap(small, "seq", 1)
+    taps_part = lax.dynamic_slice_in_dim(small[:each], side * channels, channels, 1)
+    up_share = jnp.transpose(up, (1, 0, 2)).reshape(up.shape[1], -1)
+    return (
+        out,
+        d_tokens,
+        small[each, :gain_each],
+        gate[1],
+        kv[0],
+        kv[1],
+        gate[0],
+        small[each, gain_each : 2 * gain_each],
+        up_share,
+        down.reshape(share, width),
+        taps_part.T,
+        pair[:each].T,
+        pair[each:].T,
+    )
+
+
 def solution(mesh):
     in_specs = (
         P("dp", "seq", None),
@@ -340,6 +1215,19 @@
         P("seq", "dp"),
         P("seq", "dp"),
     )
+
+    def per_device(*args):
+        tokens, shift_taps = args[0], args[10]
+        rows, positions, width = tokens.shape
+        fits = (
+            mesh.shape["seq"] == rows == 2
+            and mesh.shape["dp"] == 16
+            and positions * 2 % BLOCK == 0
+            and width % 256 == 0
+            and shift_taps.shape[1] <= BLOCK
+        )
+        return split_rows(*args) if fits else split_channels(*args)
+
     return jax.shard_map(
         per_device, mesh=mesh, in_specs=in_specs, out_specs=out_specs, check_vma=False
     )

time: 1370 us -> 430 us (0.31)
  matrix products: 732 us -> 0 us
  Pallas kernels: 0 us -> 160 us
  other arithmetic: 180 us -> 31.3 us
  local copies, waits for them, and re-layouts: 159 us -> 15 us
  waiting for transfers between devices: 215 us -> 143 us
  starting transfers between devices: 51.4 us -> 71.3 us
  between operations: 17.9 us -> 1.92 us
    dot_general x56 -> x0, matrix products: 678 us -> none  [the longest x4 114 us: inverse(): jnp.einsum('rfc,tf->rtc', imag_part, sin_weighted, precision=highest)]
    pallas_call x0 -> x6, Pallas kernels: none -> 160 us  [the longest x1 36.8 us: mixer_back_call(): pl.pallas_call(mixer_back_body, grid_spec=pltpu.PrefetchScalarGridSpec(nu...]
    ppermute x0 -> x59, waiting for transfers between devices: none -> 143 us  [swap(): return lax.ppermute(value, axis_name, [(i, i ^ bit) for i in range(count)])]
    reduce_scatter x6 -> x0, waiting for transfers between devices: 91 us -> none  [the longest x1 78.8 us: per_device(): lax.psum_scatter(grad_down.astype(jnp.bfloat16), 'dp', scatter_dimension=...]
    unnamed x9 -> x0, waiting for transfers between devices: 87.9 us -> none
    unnamed x345 -> x32, local copies, waits for them, and re-layouts: 83.3 us -> 0.25 us
    unnamed x13 -> x1, other arithmetic: 77.9 us -> 0.04 us
    ppermute x0 -> x59, starting transfers between devices: none -> 71.3 us  [swap(): return lax.ppermute(value, axis_name, [(i, i ^ bit) for i in range(count)])]
  transfers between devices with their start and end apart: 20 -> 59, of which waited for: 6 -> 36; matrix products, arithmetic and copies ran while one was open for 60% -> 9% of each run, Pallas kernels for 0% -> 13%
where the time goes in v1:
time: 430 us; the launch traced here: 423 us
  Pallas kernels  160 us (37%)
  waiting for transfers between devices  143 us (33%)
  starting transfers between devices  71.3 us (17%)
  other arithmetic  31.3 us (7%)
  local copies, waits for them, and re-layouts  15 us (3%)
    ppermute x59, waiting for transfers between devices, swap(): return lax.ppermute(value, axis_name, [(i, i ^ bit) for i in range(count)])  143 us
    ppermute x59, starting transfers between devices, swap(): return lax.ppermute(value, axis_name, [(i, i ^ bit) for i in range(count)])  71.3 us
    pallas_call x1, Pallas kernels, mixer_back_call(): pl.pallas_call(mixer_back_body, grid_spec=pltpu.PrefetchScalarGridSpec(nu...  36.8 us
    pallas_call x1, Pallas kernels, ffn_call(): pl.pallas_call(ffn_body, grid_spec=pltpu.PrefetchScalarGridSpec(num_scala...  34.1 us
    pallas_call x1, Pallas kernels, mixer_call(): pl.pallas_call(mixer_body, grid_spec=pltpu.PrefetchScalarGridSpec(num_sca...  28.1 us
    pallas_call x1, Pallas kernels, spectra_call(): pl.pallas_call(spectra_body, grid=(channels // tile,), in_specs=[pl.Block...  27.1 us
    pallas_call x1, Pallas kernels, ffn_back_call(): pl.pallas_call(ffn_back_body, grid_spec=pltpu.PrefetchScalarGridSpec(num_...  24.8 us
    pallas_call x1, Pallas kernels, gate_back_call(): pl.pallas_call(gate_back_body, grid_spec=pltpu.PrefetchScalarGridSpec(num...  9.12 us
  transfers between devices with their start and end apart: 59, of which 36 were waited for; matrix products, arithmetic and copies ran while one was open for 9% of the time, Pallas kernels for 13%

profile of v1, /device:TPU:0, one launch (start us, length us, event | category | flops | bytes accessed | tf_op | source)
XLA Modules:
  0.0 422.6 jit_solution(17277216092853379769)
XLA Ops:
  0.6 1.7 pad_maximum_fusion.1
  2.4 3.0 collective-permute-start.1
  5.3 1.6 dynamic-slice_bitcast_fusion.5
  7.3 1.9 collective-permute-start.2
  11.0 2.4 collective-permute-done.1
  15.5 27.1 %spectra.1 = (f32[4,512,768]{2,1,0:T(8,128)}, f32[512,768]{1,0:T(8,128)}) custom-call(f32[64,768]{1,0:T(8,128)} %get-tuple-element.95.coef_ref, f32[64,768]{1,0:T(8,128)} %get-tuple-element.94.rate_ref, f32[64,768]{1,0:T(8,128)} %get-tuple-element.93.taps_ref, bf16[512,256]{1,0:T(8,128)(2,1)} %constant.71.clone.table_ref), custom_call_target="tpu_custom_call" | custom-call | flops 6000000000 | bytes 20000000 | tf_op jit(solution)/shard_map/spectra/pallas_call | solution.py:150
  42.5 3.1 maximum_select_fusion.x_ref
  45.6 28.1 %mixer_forward.1 = (bf16[1024,768]{1,0:T(8,128)(2,1)}, bf16[1024,768]{1,0:T(8,128)(2,1)}, bf16[1024,768]{1,0:T(8,128)(2,1)}, bf16[1024,768]{1,0:T(8,128)(2,1)}, ...) custom-call(s32[1]{0:T(128)} %dynamic_slice.34.length_ref, ...), custom_call_target="tpu_custom_call" | custom-call | flops 10000000000 | bytes 30000000 | tf_op jit(solution)/shard_map/mixer_forward/pallas_call | solution.py:272
  73.7 3.1 maximum_select_fusion.1.cot_ref
  76.9 34.1 %feed_forward.1 = (bf16[1024,768]{1,0:T(8,128)(2,1)}, bf16[1024,3072]{1,0:T(8,128)(2,1)}, bf16[2,2,2,192,768]{4,3,2,1,0:T(8,128)(2,1)}, bf16[2,2,2,192,768]{4,3,2,1,0:T(8,128)(2,1)}) custom-call(s32[1]{0:T(128)} %dynamic_slice.34.length_ref, s32[1]{0:T(128)} %bitcast.place_ref, bf16[1024,768]{1,0:T(8,128)(2,1)} %get-tuple-element.47.a_two_ref, ...), custom_call_target="tpu_custom_call" | custom-call | flops 19327352832 | bytes 40000000 | tf_op jit(solution)/shard_map/feed_forward/pallas_call | solution.py:385
  110.9 24.8 %feed_forward_back.1 = (f32[1024,768]{1,0:T(8,128)}, bf16[1024,768]{1,0:T(8,128)(2,1)}, f32[1,768]{1,0:T(1,128)}, bf16[2,2,2,4,48,768]{5,4,3,2,1,0:T(8,128)(2,1)}, bf16[2,2,2,4,48,768]{5,4,3,2,1,0:T(8,128)(2,1)}) custom-call(s32[1]{0:T(128)} %dynamic_slice.34.length_ref, s32[1]{0:T(128)} %bitcast.place_ref, bf16[1024,768]{1,0:T(8,128)(2,1)} %get-tuple-element.47.a_two_ref, ...), custom_call_target="tpu_custom_call" | custom-call | flops 9663676416 | bytes 40000000 | tf_op jit(solution)/shard_map/feed_forward_back/pallas_call | solution.py:465
  135.7 9.1 %gate_back.1 = (bf16[1024,768]{1,0:T(8,128)(2,1)}, bf16[1024,768]{1,0:T(8,128)(2,1)}, bf16[2,2,2,2,48,768]{5,4,3,2,1,0:T(8,128)(2,1)}, bf16[2,2,2,2,48,768]{5,4,3,2,1,0:T(8,128)(2,1)}) custom-call(s32[1]{0:T(128)} %bitcast.place_ref, bf16[1024,768]{1,0:T(8,128)(2,1)} %get-tuple-element.51.d_mixer_ref, bf16[768,768]{1,0:T(8,128)(2,1)} %wout_ref.3, ...), custom_call_target="tpu_custom_call" | custom-call | flops 3623878656 | bytes 15000000 | tf_op jit(solution)/shard_map/gate_back/pallas_call | solution.py:521
  144.8 36.8 %mixer_back.1 = (bf16[1024,768]{1,0:T(8,128)(2,1)}, f32[1,768]{1,0:T(1,128)}, f32[64,768]{1,0:T(8,128)}, bf16[2,2,2,2,48,768]{5,4,3,2,1,0:T(8,128)(2,1)}, bf16[2...) custom-call(s32[1]{0:T(128)} %dynamic_slice.34.length_ref, ...), custom_call_target="tpu_custom_call" | custom-call | flops 16000000000 | bytes 40000000 | tf_op jit(solution)/shard_map/mixer_back/pallas_call | solution.py:675
  184.5 3.2 collective-permute-start.5
  187.6 7.3 %collective-permute-done.5 = f32[8,5,768]{2,1,0:T(8,128)S(1)} collective-permute-done((f32[8,5,768]{2,1,0:T(8,128)S(1)}, f32[8,5,768]{2,1,0:T(8,128)S(1)}, u32[]{:S(2)}, u32[]{:S(2)}) %collective-permute-start.5) | collective-permute-done | bytes 122912 | tf_op jit(solution)/shard_map/ppermute | solution.py:1039
  195.6 4.0 collective-permute-done.6
  201.2 2.6 collective-permute-done.7
  208.0 17.0 %collective-permute-done.9 = f32[5,768]{1,0:T(8,128)S(1)} collective-permute-done((f32[5,768]{1,0:T(8,128)S(1)}, f32[5,768]{1,0:T(8,128)S(1)}, u32[]{:S(2)}, u32[]{:S(2)}) %collective-permute-start.9) | collective-permute-done | bytes 15392 | tf_op jit(solution)/shard_map/ppermute | solution.py:1039
  228.9 12.5 %collective-permute-done.4 = bf16[512,768]{1,0:T(8,128)(2,1)S(1)} collective-permute-done((bf16[512,768]{1,0:T(8,128)(2,1)S(1)}, bf16[512,768]{1,0:T(8,128)(2,1)S(1)}, u32[]{:S(2)}, u32[]{:S(2)}) %collective-permute-start.4) | collective-permute-done | bytes 786464 | tf_op jit(solution)/shard_map/ppermute | solution.py:1039
  244.3 5.8 %collective-permute-done.47 = bf16[2,2,1,32,768]{4,3,1,2,0:T(8,128)(2,1)S(1)} collective-permute-done((bf16[2,2,1,32,768]{4,3,1,2,0:T(8,128)(2,1)S(1)}, bf16[2,2,1,32,768]{4,3,1,2,0:T(8,128)(2,1)S(1)}, u32[]{:S(2)}, u32[]{:S(2)}) %collective-permute-start.47) | collective-permute-done | bytes 196640 | tf_op jit(solution)/shard_map/ppermute | solution.py:1039
  250.1 1.9 collective-permute-start.52
  252.1 5.4 %collective-permute-done.52 = bf16[2,1,32,768]{3,2,0,1:T(8,128)(2,1)S(1)} collective-permute-done((bf16[2,1,32,768]{3,2,0,1:T(8,128)(2,1)S(1)}, bf16[2,1,32,768]{3,2,0,1:T(8,128)(2,1)S(1)}, u32[]{:S(2)}, u32[]{:S(2)}) %collective-permute-start.52) | collective-permute-done | bytes 98336 | tf_op jit(solution)/shard_map/ppermute | solution.py:1039
  257.6 4.6 %collective-permute-done.48 = bf16[2,1,32,768]{3,2,1,0:T(8,128)(2,1)S(1)} collective-permute-done((bf16[2,1,32,768]{3,2,1,0:T(8,128)(2,1)S(1)}, bf16[2,1,32,768]{3,2,1,0:T(8,128)(2,1)S(1)}, u32[]{:S(2)}, u32[]{:S(2)}) %collective-permute-start.48) | collective-permute-done | bytes 98336 | tf_op jit(solution)/shard_map/ppermute | solution.py:1039
  263.7 2.6 collective-permute-done.53
  266.2 1.6 collective-permute-start.49
  267.9 3.8 collective-permute-done.49
  273.2 2.6 collective-permute-done.54
  277.3 2.6 collective-permute-done.50
  279.9 2.3 fusion
  282.2 1.7 reshape.439
  283.8 1.6 fusion.34
  285.4 1.6 reshape.440
  287.0 1.7 pad_maximum_fusion.2
  288.6 2.2 gather_fusion.1
  293.1 1.6 add_convert_fusion.1
  294.8 1.6 add_convert_fusion.2
  296.4 1.8 collective-permute-done.55
  298.5 3.8 collective-permute-done.56
  302.4 1.6 collective-permute-start.57
  304.0 2.2 collective-permute-done.57
  306.7 1.6 collective-permute-start.16
  309.7 6.2 %collective-permute-done.20 = bf16[2,2,1,48,768]{4,3,1,0,2:T(8,128)(2,1)S(1)} collective-permute-done((bf16[2,2,1,48,768]{4,3,1,0,2:T(8,128)(2,1)S(1)}, bf16[2,2,1,48,768]{4,3,1,0,2:T(8,128)(2,1)S(1)}, u32[]{:S(2)}, u32[]{:S(2)}) %collective-permute-start.20) | collective-permute-done | bytes 294944 | tf_op jit(solution)/shard_map/ppermute | solution.py:1039
  316.7 1.9 collective-permute-start.17
  318.6 3.7 collective-permute-done.24
  322.3 2.6 collective-permute-start.21
  324.9 3.5 collective-permute-done.11
  328.6 2.3 collective-permute-done.17
  331.0 4.5 %collective-permute-done.21 = bf16[2,1,48,768]{3,2,0,1:T(8,128)(2,1)S(1)} collective-permute-done((bf16[2,1,48,768]{3,2,0,1:T(8,128)(2,1)S(1)}, bf16[2,1,48,768]{3,2,0,1:T(8,128)(2,1)S(1)}, u32[]{:S(2)}, u32[]{:S(2)}) %collective-permute-start.21) | collective-permute-done | bytes 147488 | tf_op jit(solution)/shard_map/ppermute | solution.py:1039
  335.6 4.1 collective-permute-done.12
  339.6 1.6 collective-permute-start.22
  342.0 2.0 collective-permute-done.22
  356.3 2.2 add_convert_fusion
  358.6 1.6 collective-permute-start.29
  362.0 10.1 %collective-permute-done.42 = bf16[2,2,1,80,768]{4,3,1,0,2:T(8,128)(2,1)S(1)} collective-permute-done((bf16[2,2,1,80,768]{4,3,1,0,2:T(8,128)(2,1)S(1)}, bf16[2,2,1,80,768]{4,3,1,0,2:T(8,128)(2,1)S(1)}, u32[]{:S(2)}, u32[]{:S(2)}) %collective-permute-start.42) | collective-permute-done | bytes 491552 | tf_op jit(solution)/shard_map/ppermute | solution.py:1039
  373.2 1.7 collective-permute-done.29
  374.9 9.9 %collective-permute-done.33 = bf16[2,2,2,48,768]{4,3,2,1,0:T(8,128)(2,1)S(1)} collective-permute-done((bf16[2,2,2,48,768]{4,3,2,1,0:T(8,128)(2,1)S(1)}, bf16[2,2,2,48,768]{4,3,2,1,0:T(8,128)(2,1)S(1)}, u32[]{:S(2)}, u32[]{:S(2)}) %collective-permute-start.33) | collective-permute-done | bytes 589856 | tf_op jit(solution)/shard_map/ppermute | solution.py:1039
  385.5 3.0 collective-permute-start.30
  388.8 1.6 collective-permute-start.44
  390.5 4.1 collective-permute-done.44
  397.0 3.2 collective-permute-start.35
  401.8 3.7 collective-permute-done.39
  406.2 5.8 %collective-permute-start.36 = (bf16[2,48,768]{2,1,0:T(8,128)(2,1)S(1)}, bf16[2,48,768]{2,1,0:T(8,128)(2,1)S(1)}, u32[]{:S(2)}, u32[]{:S(2)}) collective-permute-start(bf16[2,48,768]{2,1,0:T(8,128)(2,1)S(1)} %fusion.17), channel_id=1, source_target_pairs={{0,1},{1,0},{2,3},{3,2},{4,5},{5,4},{6,7},{7,6},{8,9},{9,8},{10,11... | collective-permute-start | bytes 442376 | tf_op jit(solution)/shard_map/ppermute | solution.py:1039
  412.1 3.5 collective-permute-start.32
  415.7 1.7 collective-permute-start.41
  (224 shorter events, 56.8 us)
Async XLA Ops:
  2.4 11.1 %collective-permute-start.1 = (f32[3,64,384]{2,1,0:T(8,128)}, f32[3,64,384]{2,1,0:T(8,128)}, u32[]{:S(2)}, u32[]{:S(2)}) collective-permute-start(f32[3,64,384]{2,1,0:T(8,128)} %pad_maximum_fusion.1), channel_id=1, source_target_pairs={{0,1},{1,0},{2,3},{3,2},{4,5},{5,4},{6,7},{7,6},{8,9},{9,8},{10,11... | collective-permute-start | bytes 884744 | tf_op jit(solution)/shard_map/ppermute | solution.py:1039
  7.0 35.5 %collective-permute-start = (bf16[512,768]{1,0:T(8,128)(2,1)S(1)}, bf16[512,768]{1,0:T(8,128)(2,1)}, u32[]{:S(2)}, u32[]{:S(2)}) collective-permute-start(bf16[512,768]{1,0:T(8,128)(2,1)S(1)} %get-tuple-element.88), channel_id=1, source_target_pairs={{0,1},{1,0},{2,3},{3,2},{4,5},{5,4},{6,7},{7,6},{8,9},{9,8},{10,11... | collective-permute-start | bytes 2359304 | tf_op jit(solution)/shard_map/ppermute | solution.py:1039
  7.3 66.4 %collective-permute-start.2 = (bf16[512,768]{1,0:T(8,128)(2,1)S(1)}, bf16[512,768]{1,0:T(8,128)(2,1)}, u32[]{:S(2)}, u32[]{:S(2)}) collective-permute-start(bf16[512,768]{1,0:T(8,128)(2,1)S(1)} %get-tuple-element.86), channel_id=1, source_target_pairs={{0,1},{1,0},{2,3},{3,2},{4,5},{5,4},{6,7},{7,6},{8,9},{9,8},{10,11... | collective-permute-start | bytes 2359304 | tf_op jit(solution)/shard_map/ppermute | solution.py:1039
  144.8 37.5 %copy-start.13 = (f32[1,768]{1,0:T(1,128)S(1)}, f32[1,768]{1,0:T(1,128)}, u32[]{:S(2)}) copy-start(f32[1,768]{1,0:T(1,128)} %get-tuple-element.66) | copy-start | bytes 9220
  183.7 17.5 %copy-start.14 = (bf16[2,2,2,1,64,768]{5,4,3,2,1,0:T(8,128)(2,1)S(1)}, bf16[2,2,2,1,64,768]{5,4,3,2,1,0:T(8,128)(2,1)}, u32[]{:S(2)}) copy-start(bf16[2,2,2,1,64,768]{5,4,3,2,1,0:T(8,128)(2,1)} %get-tuple-element.76) | copy-start | bytes 2359300
  184.3 19.6 %copy-start.3 = (bf16[1024,768]{1,0:T(8,128)(2,1)S(1)}, bf16[1024,768]{1,0:T(8,128)(2,1)}, u32[]{:S(2)}) copy-start(bf16[1024,768]{1,0:T(8,128)(2,1)} %get-tuple-element.49) | copy-start | bytes 4718596
  184.5 10.4 %collective-permute-start.5 = (f32[8,5,768]{2,1,0:T(8,128)S(1)}, f32[8,5,768]{2,1,0:T(8,128)S(1)}, u32[]{:S(2)}, u32[]{:S(2)}) collective-permute-start(f32[8,5,768]{2,1,0:T(8,128)S(1)} %slice.382), channel_id=1, source_target_pairs={{0,16},{2,18},{4,20},{6,22},{8,24},{10,26},{12,28},{14,30},{16,0},... | collective-permute-start | bytes 368648 | tf_op jit(solution)/shard_map/ppermute | solution.py:1039
  194.9 4.7 %collective-permute-start.6 = (f32[4,5,768]{2,1,0:T(8,128)S(1)}, f32[4,5,768]{2,1,0:T(8,128)S(1)}, u32[]{:S(2)}, u32[]{:S(2)}) collective-permute-start(f32[4,5,768]{2,1,0:T(8,128)S(1)} %slice.384), channel_id=1, source_target_pairs={{0,8},{2,10},{4,12},{6,14},{8,0},{10,2},{12,4},{14,6},{16,24},{18,... | collective-permute-start | bytes 184328 | tf_op jit(solution)/shard_map/ppermute | solution.py:1039
  199.6 4.2 collective-permute-start.7
  201.2 25.0 %collective-permute-start.46 = (bf16[2,2,2,1,64,768]{5,4,3,2,1,0:T(8,128)(2,1)S(1)}, bf16[2,2,2,1,64,768]{5,4,3,2,1,0:T(8,128)(2,1)S(1)}, u32[]{:S(2)}, u32[]{:S(2)}) collective-permute-start(bf16[2,2,2,1,64,768]{5,4,3,2,1,0:T(8,128)(2,1)S(1)} %copy-done.14), channel_id=1, source_target_pairs={{0,2},{2,0},{4,6},{6,4},{8,10},{10,8},{12,14},{14,12},{16,18},{18,... | collective-permute-start | bytes 2359304 | tf_op jit(solution)/shard_map/ppermute | solution.py:1039
  203.8 1.9 collective-permute-start.8
  204.0 22.9 %collective-permute-start.3 = (bf16[512,768]{1,0:T(8,128)(2,1)S(1)}, bf16[512,768]{1,0:T(8,128)(2,1)S(1)}, u32[]{:S(2)}, u32[]{:S(2)}) collective-permute-start(bf16[512,768]{1,0:T(8,128)(2,1)S(1)} %get-tuple-element.84), channel_id=1, source_target_pairs={{0,1},{1,0},{2,3},{3,2},{4,5},{5,4},{6,7},{7,6},{8,9},{9,8},{10,11... | collective-permute-start | bytes 2359304 | tf_op jit(solution)/shard_map/ppermute | solution.py:1039
  205.5 149.1 %collective-permute-start.37 = (bf16[2,2,2,1,192,768]{5,4,2,1,0,3:T(8,128)(2,1)}, bf16[2,2,2,1,192,768]{5,4,2,1,0,3:T(8,128)(2,1)S(1)}, u32[]{:S(2)}, u32[]{:S(2)}) collective-permute-start(bf16[2,2,2,1,192,768]{5,4,2,1,0,3:T(8,128)(2,1)} %bitcast.347), channel_id=1, source_target_pairs={{0,2},{2,0},{4,6},{6,4},{8,10},{10,8},{12,14},{14,12},{16,18},{18,... | collective-permute-start | bytes 7077896 | tf_op jit(solution)/shard_map/ppermute | solution.py:1039
  205.7 19.2 %collective-permute-start.9 = (f32[5,768]{1,0:T(8,128)S(1)}, f32[5,768]{1,0:T(8,128)S(1)}, u32[]{:S(2)}, u32[]{:S(2)}) collective-permute-start(f32[5,768]{1,0:T(8,128)S(1)} %fusion.36), channel_id=1, source_target_pairs={{0,1},{1,0},{2,3},{3,2},{4,5},{5,4},{6,7},{7,6},{8,9},{9,8},{10,11... | collective-permute-start | bytes 46088 | tf_op jit(solution)/shard_map/ppermute | solution.py:1039
  206.5 20.2 %copy-start.9 = (bf16[2,2,2,1,64,768]{5,4,3,2,1,0:T(8,128)(2,1)S(1)}, bf16[2,2,2,1,64,768]{5,4,3,2,1,0:T(8,128)(2,1)}, u32[]{:S(2)}) copy-start(bf16[2,2,2,1,64,768]{5,4,3,2,1,0:T(8,128)(2,1)} %get-tuple-element.75) | copy-start | bytes 2359300
  206.6 34.8 %collective-permute-start.4 = (bf16[512,768]{1,0:T(8,128)(2,1)S(1)}, bf16[512,768]{1,0:T(8,128)(2,1)S(1)}, u32[]{:S(2)}, u32[]{:S(2)}) collective-permute-start(bf16[512,768]{1,0:T(8,128)(2,1)S(1)} %get-tuple-element.82), channel_id=1, source_target_pairs={{0,1},{1,0},{2,3},{3,2},{4,5},{5,4},{6,7},{7,6},{8,9},{9,8},{10,11... | collective-permute-start | bytes 2359304 | tf_op jit(solution)/shard_map/ppermute | solution.py:1039
  225.0 68.2 %collective-permute-start.15 = (bf16[2,2,2,2,48,768]{5,4,3,2,1,0:T(8,128)(2,1)}, bf16[2,2,2,2,48,768]{5,4,3,2,1,0:T(8,128)(2,1)}, u32[]{:S(2)}, u32[]{:S(2)}) collective-permute-start(bf16[2,2,2,2,48,768]{5,4,3,2,1,0:T(8,128)(2,1)} %get-tuple-element.70), channel_id=1, source_target_pairs={{0,2},{2,0},{4,6},{6,4},{8,10},{10,8},{12,14},{14,12},{16,18},{18,... | collective-permute-start | bytes 3538952 | tf_op jit(solution)/shard_map/ppermute | solution.py:1039
  226.2 68.6 %collective-permute-start.10 = (bf16[2,2,2,2,48,768]{5,4,3,2,1,0:T(8,128)(2,1)}, bf16[2,2,2,2,48,768]{5,4,3,2,1,0:T(8,128)(2,1)}, u32[]{:S(2)}, u32[]{:S(2)}) collective-permute-start(bf16[2,2,2,2,48,768]{5,4,3,2,1,0:T(8,128)(2,1)} %get-tuple-element.68), channel_id=1, source_target_pairs={{0,2},{2,0},{4,6},{6,4},{8,10},{10,8},{12,14},{14,12},{16,18},{18,... | collective-permute-start | bytes 3538952 | tf_op jit(solution)/shard_map/ppermute | solution.py:1039
  226.9 15.9 %collective-permute-start.51 = (bf16[2,2,1,32,768]{4,3,1,0,2:T(8,128)(2,1)S(1)}, bf16[2,2,1,32,768]{4,3,1,0,2:T(8,128)(2,1)S(1)}, u32[]{:S(2)}, u32[]{:S(2)}) collective-permute-start(bf16[2,2,1,32,768]{4,3,1,0,2:T(8,128)(2,1)S(1)} %slice_bitcast_fusion.24), channel_id=1, source_target_pairs={{0,8},{2,10},{4,12},{6,14},{8,0},{10,2},{12,4},{14,6},{16,24},{18,... | collective-permute-start | bytes 589832 | tf_op jit(solution)/shard_map/ppermute | solution.py:1039
  241.4 114.8 %collective-permute-start.28 = (bf16[2,2,2,4,48,768]{5,4,3,2,1,0:T(8,128)(2,1)}, bf16[2,2,2,4,48,768]{5,4,3,2,1,0:T(8,128)(2,1)}, u32[]{:S(2)}, u32[]{:S(2)}) collective-permute-start(bf16[2,2,2,4,48,768]{5,4,3,2,1,0:T(8,128)(2,1)} %get-tuple-element.72), channel_id=1, source_target_pairs={{0,2},{2,0},{4,6},{6,4},{8,10},{10,8},{12,14},{14,12},{16,18},{18,... | collective-permute-start | bytes 7077896 | tf_op jit(solution)/shard_map/ppermute | solution.py:1039
  242.8 7.3 %collective-permute-start.47 = (bf16[2,2,1,32,768]{4,3,1,2,0:T(8,128)(2,1)S(1)}, bf16[2,2,1,32,768]{4,3,1,2,0:T(8,128)(2,1)S(1)}, u32[]{:S(2)}, u32[]{:S(2)}) collective-permute-start(bf16[2,2,1,32,768]{4,3,1,2,0:T(8,128)(2,1)S(1)} %slice_bitcast_fusion.26), channel_id=1, source_target_pairs={{0,4},{2,6},{4,0},{6,2},{8,12},{10,14},{12,8},{14,10},{16,20},{18,... | collective-permute-start | bytes 589832 | tf_op jit(solution)/shard_map/ppermute | solution.py:1039
  250.1 7.4 %collective-permute-start.52 = (bf16[2,1,32,768]{3,2,0,1:T(8,128)(2,1)S(1)}, bf16[2,1,32,768]{3,2,0,1:T(8,128)(2,1)S(1)}, u32[]{:S(2)}, u32[]{:S(2)}) collective-permute-start(bf16[2,1,32,768]{3,2,0,1:T(8,128)(2,1)S(1)} %slice_bitcast_fusion.47), channel_id=1, source_target_pairs={{0,16},{2,18},{4,20},{6,22},{8,24},{10,26},{12,28},{14,30},{16,0},... | collective-permute-start | bytes 294920 | tf_op jit(solution)/shard_map/ppermute | solution.py:1039
  257.5 4.6 %collective-permute-start.48 = (bf16[2,1,32,768]{3,2,1,0:T(8,128)(2,1)S(1)}, bf16[2,1,32,768]{3,2,1,0:T(8,128)(2,1)S(1)}, u32[]{:S(2)}, u32[]{:S(2)}) collective-permute-start(bf16[2,1,32,768]{3,2,1,0:T(8,128)(2,1)S(1)} %slice_bitcast_fusion.49), channel_id=1, source_target_pairs={{0,8},{2,10},{4,12},{6,14},{8,0},{10,2},{12,4},{14,6},{16,24},{18,... | collective-permute-start | bytes 294920 | tf_op jit(solution)/shard_map/ppermute | solution.py:1039
  262.2 4.1 collective-permute-start.53
  266.2 5.4 %collective-permute-start.49 = (bf16[1,32,768]{2,1,0:T(8,128)(2,1)S(1)}, bf16[1,32,768]{2,1,0:T(8,128)(2,1)S(1)}, u32[]{:S(2)}, u32[]{:S(2)}) collective-permute-start(bf16[1,32,768]{2,1,0:T(8,128)(2,1)S(1)} %slice_bitcast_fusion.61), channel_id=1, source_target_pairs={{0,16},{2,18},{4,20},{6,22},{8,24},{10,26},{12,28},{14,30},{16,0},... | collective-permute-start | bytes 147464 | tf_op jit(solution)/shard_map/ppermute | solution.py:1039
  271.7 4.1 collective-permute-start.54
  275.8 4.1 collective-permute-start.50
  291.8 6.4 %collective-permute-start.55 = (f32[8,8,384]{2,1,0:T(8,128)S(1)}, f32[8,8,384]{2,1,0:T(8,128)S(1)}, u32[]{:S(2)}, u32[]{:S(2)}) collective-permute-start(f32[8,8,384]{2,1,0:T(8,128)S(1)} %slice.453), channel_id=1, source_target_pairs={{0,16},{2,18},{4,20},{6,22},{8,24},{10,26},{12,28},{14,30},{16,0},... | collective-permute-start | bytes 294920 | tf_op jit(solution)/shard_map/ppermute | solution.py:1039
  298.2 4.2 collective-permute-start.56
  302.4 3.9 collective-permute-start.57
  306.3 2.0 collective-permute-start.58
  306.4 9.5 %collective-permute-start.20 = (bf16[2,2,1,48,768]{4,3,1,0,2:T(8,128)(2,1)S(1)}, bf16[2,2,1,48,768]{4,3,1,0,2:T(8,128)(2,1)S(1)}, u32[]{:S(2)}, u32[]{:S(2)}) collective-permute-start(bf16[2,2,1,48,768]{4,3,1,0,2:T(8,128)(2,1)S(1)} %slice_bitcast_fusion.16), channel_id=1, source_target_pairs={{0,8},{2,10},{4,12},{6,14},{8,0},{10,2},{12,4},{14,6},{16,24},{18,... | collective-permute-start | bytes 884744 | tf_op jit(solution)/shard_map/ppermute | solution.py:1039
  306.7 9.8 %collective-permute-start.16 = (bf16[2,2,1,48,768]{4,3,1,0,2:T(8,128)(2,1)S(1)}, bf16[2,2,1,48,768]{4,3,1,0,2:T(8,128)(2,1)S(1)}, u32[]{:S(2)}, u32[]{:S(2)}) collective-permute-start(bf16[2,2,1,48,768]{4,3,1,0,2:T(8,128)(2,1)S(1)} %slice_bitcast_fusion.18), channel_id=1, source_target_pairs={{0,4},{2,6},{4,0},{6,2},{8,12},{10,14},{12,8},{14,10},{16,20},{18,... | collective-permute-start | bytes 884744 | tf_op jit(solution)/shard_map/ppermute | solution.py:1039
  308.3 14.0 %collective-permute-start.24 = (bf16[2,2,1,48,768]{4,3,1,0,2:T(8,128)(2,1)S(1)}, bf16[2,2,1,48,768]{4,3,1,0,2:T(8,128)(2,1)S(1)}, u32[]{:S(2)}, u32[]{:S(2)}) collective-permute-start(bf16[2,2,1,48,768]{4,3,1,0,2:T(8,128)(2,1)S(1)} %slice_bitcast_fusion.14), channel_id=1, source_target_pairs={{0,4},{2,6},{4,0},{6,2},{8,12},{10,14},{12,8},{14,10},{16,20},{18,... | collective-permute-start | bytes 884744 | tf_op jit(solution)/shard_map/ppermute | solution.py:1039
  315.9 12.5 %collective-permute-start.11 = (bf16[2,2,1,48,768]{4,3,1,0,2:T(8,128)(2,1)S(1)}, bf16[2,2,1,48,768]{4,3,1,0,2:T(8,128)(2,1)S(1)}, u32[]{:S(2)}, u32[]{:S(2)}) collective-permute-start(bf16[2,2,1,48,768]{4,3,1,0,2:T(8,128)(2,1)S(1)} %slice_bitcast_fusion.20), channel_id=1, source_target_pairs={{0,8},{2,10},{4,12},{6,14},{8,0},{10,2},{12,4},{14,6},{16,24},{18,... | collective-permute-start | bytes 884744 | tf_op jit(solution)/shard_map/ppermute | solution.py:1039
  316.7 14.2 %collective-permute-start.17 = (bf16[2,1,48,768]{3,2,0,1:T(8,128)(2,1)S(1)}, bf16[2,1,48,768]{3,2,0,1:T(8,128)(2,1)S(1)}, u32[]{:S(2)}, u32[]{:S(2)}) collective-permute-start(bf16[2,1,48,768]{3,2,0,1:T(8,128)(2,1)S(1)} %slice_bitcast_fusion.41), channel_id=1, source_target_pairs={{0,8},{2,10},{4,12},{6,14},{8,0},{10,2},{12,4},{14,6},{16,24},{18,... | collective-permute-start | bytes 442376 | tf_op jit(solution)/shard_map/ppermute | solution.py:1039
  322.3 13.2 %collective-permute-start.21 = (bf16[2,1,48,768]{3,2,0,1:T(8,128)(2,1)S(1)}, bf16[2,1,48,768]{3,2,0,1:T(8,128)(2,1)S(1)}, u32[]{:S(2)}, u32[]{:S(2)}) collective-permute-start(bf16[2,1,48,768]{3,2,0,1:T(8,128)(2,1)S(1)} %slice_bitcast_fusion.39), channel_id=1, source_target_pairs={{0,16},{2,18},{4,20},{6,22},{8,24},{10,26},{12,28},{14,30},{16,0},... | collective-permute-start | bytes 442376 | tf_op jit(solution)/shard_map/ppermute | solution.py:1039
  328.5 11.1 %collective-permute-start.12 = (bf16[2,1,48,768]{3,2,0,1:T(8,128)(2,1)S(1)}, bf16[2,1,48,768]{3,2,0,1:T(8,128)(2,1)S(1)}, u32[]{:S(2)}, u32[]{:S(2)}) collective-permute-start(bf16[2,1,48,768]{3,2,0,1:T(8,128)(2,1)S(1)} %slice_bitcast_fusion.43), channel_id=1, source_target_pairs={{0,16},{2,18},{4,20},{6,22},{8,24},{10,26},{12,28},{14,30},{16,0},... | collective-permute-start | bytes 442376 | tf_op jit(solution)/shard_map/ppermute | solution.py:1039
  331.0 10.3 %collective-permute-start.25 = (bf16[2,1,48,768]{3,2,0,1:T(8,128)(2,1)S(1)}, bf16[2,1,48,768]{3,2,0,1:T(8,128)(2,1)S(1)}, u32[]{:S(2)}, u32[]{:S(2)}) collective-permute-start(bf16[2,1,48,768]{3,2,0,1:T(8,128)(2,1)S(1)} %slice_bitcast_fusion.37), channel_id=1, source_target_pairs={{0,8},{2,10},{4,12},{6,14},{8,0},{10,2},{12,4},{14,6},{16,24},{18,... | collective-permute-start | bytes 442376 | tf_op jit(solution)/shard_map/ppermute | solution.py:1039
  335.5 6.4 %collective-permute-start.18 = (bf16[1,48,768]{2,1,0:T(8,128)(2,1)S(1)}, bf16[1,48,768]{2,1,0:T(8,128)(2,1)S(1)}, u32[]{:S(2)}, u32[]{:S(2)}) collective-permute-start(bf16[1,48,768]{2,1,0:T(8,128)(2,1)S(1)} %slice_bitcast_fusion.55), channel_id=1, source_target_pairs={{0,16},{2,18},{4,20},{6,22},{8,24},{10,26},{12,28},{14,30},{16,0},... | collective-permute-start | bytes 221192 | tf_op jit(solution)/shard_map/ppermute | solution.py:1039
  335.6 19.1 %copy-start.1 = (bf16[2,2,2,192,768]{4,3,2,1,0:T(8,128)(2,1)S(1)}, bf16[2,2,2,192,768]{4,3,2,1,0:T(8,128)(2,1)}, u32[]{:S(2)}) copy-start(bf16[2,2,2,192,768]{4,3,2,1,0:T(8,128)(2,1)} %get-tuple-element.73) | copy-start | bytes 7077892
  339.6 4.4 %collective-permute-start.22 = (bf16[1,48,768]{2,1,0:T(8,128)(2,1)S(1)}, bf16[1,48,768]{2,1,0:T(8,128)(2,1)S(1)}, u32[]{:S(2)}, u32[]{:S(2)}) collective-permute-start(bf16[1,48,768]{2,1,0:T(8,128)(2,1)S(1)} %slice_bitcast_fusion.53), channel_id=1, source_target_pairs={{0,4},{2,6},{4,0},{6,2},{8,12},{10,14},{12,8},{14,10},{16,20},{18,... | collective-permute-start | bytes 221192 | tf_op jit(solution)/shard_map/ppermute | solution.py:1039
  341.3 4.4 %collective-permute-start.13 = (bf16[1,48,768]{2,1,0:T(8,128)(2,1)S(1)}, bf16[1,48,768]{2,1,0:T(8,128)(2,1)S(1)}, u32[]{:S(2)}, u32[]{:S(2)}) collective-permute-start(bf16[1,48,768]{2,1,0:T(8,128)(2,1)S(1)} %slice_bitcast_fusion.57), channel_id=1, source_target_pairs={{0,4},{2,6},{4,0},{6,2},{8,12},{10,14},{12,8},{14,10},{16,20},{18,... | collective-permute-start | bytes 221192 | tf_op jit(solution)/shard_map/ppermute | solution.py:1039
  341.9 6.1 %collective-permute-start.26 = (bf16[1,48,768]{2,1,0:T(8,128)(2,1)S(1)}, bf16[1,48,768]{2,1,0:T(8,128)(2,1)S(1)}, u32[]{:S(2)}, u32[]{:S(2)}) collective-permute-start(bf16[1,48,768]{2,1,0:T(8,128)(2,1)S(1)} %slice_bitcast_fusion.51), channel_id=1, source_target_pairs={{0,16},{2,18},{4,20},{6,22},{8,24},{10,26},{12,28},{14,30},{16,0},... | collective-permute-start | bytes 221192 | tf_op jit(solution)/shard_map/ppermute | solution.py:1039
  344.0 5.5 %collective-permute-start.19 = (bf16[1,48,768]{2,1,0:T(8,128)(2,1)S(1)}, bf16[1,48,768]{2,1,0:T(8,128)(2,1)S(1)}, u32[]{:S(2)}, u32[]{:S(2)}) collective-permute-start(bf16[1,48,768]{2,1,0:T(8,128)(2,1)S(1)} %fusion.28), channel_id=1, source_target_pairs={{0,1},{1,0},{2,3},{3,2},{4,5},{5,4},{6,7},{7,6},{8,9},{9,8},{10,11... | collective-permute-start | bytes 221192 | tf_op jit(solution)/shard_map/ppermute | solution.py:1039
  345.7 5.6 %collective-permute-start.23 = (bf16[1,48,768]{2,1,0:T(8,128)(2,1)S(1)}, bf16[1,48,768]{2,1,0:T(8,128)(2,1)S(1)}, u32[]{:S(2)}, u32[]{:S(2)}) collective-permute-start(bf16[1,48,768]{2,1,0:T(8,128)(2,1)S(1)} %fusion.27), channel_id=1, source_target_pairs={{0,1},{1,0},{2,3},{3,2},{4,5},{5,4},{6,7},{7,6},{8,9},{9,8},{10,11... | collective-permute-start | bytes 221192 | tf_op jit(solution)/shard_map/ppermute | solution.py:1039
  348.0 4.4 %collective-permute-start.14 = (bf16[1,48,768]{2,1,0:T(8,128)(2,1)S(1)}, bf16[1,48,768]{2,1,0:T(8,128)(2,1)S(1)}, u32[]{:S(2)}, u32[]{:S(2)}) collective-permute-start(bf16[1,48,768]{2,1,0:T(8,128)(2,1)S(1)} %fusion.29), channel_id=1, source_target_pairs={{0,1},{1,0},{2,3},{3,2},{4,5},{5,4},{6,7},{7,6},{8,9},{9,8},{10,11... | collective-permute-start | bytes 221192 | tf_op jit(solution)/shard_map/ppermute | solution.py:1039
  349.5 4.4 %collective-permute-start.27 = (bf16[1,48,768]{2,1,0:T(8,128)(2,1)S(1)}, bf16[1,48,768]{2,1,0:T(8,128)(2,1)S(1)}, u32[]{:S(2)}, u32[]{:S(2)}) collective-permute-start(bf16[1,48,768]{2,1,0:T(8,128)(2,1)S(1)} %fusion.26), channel_id=1, source_target_pairs={{0,1},{1,0},{2,3},{3,2},{4,5},{5,4},{6,7},{7,6},{8,9},{9,8},{10,11... | collective-permute-start | bytes 221192 | tf_op jit(solution)/shard_map/ppermute | solution.py:1039
  355.2 16.9 %collective-permute-start.42 = (bf16[2,2,1,80,768]{4,3,1,0,2:T(8,128)(2,1)S(1)}, bf16[2,2,1,80,768]{4,3,1,0,2:T(8,128)(2,1)S(1)}, u32[]{:S(2)}, u32[]{:S(2)}) collective-permute-start(bf16[2,2,1,80,768]{4,3,1,0,2:T(8,128)(2,1)S(1)} %slice_bitcast_fusion.6), channel_id=1, source_target_pairs={{0,8},{2,10},{4,12},{6,14},{8,0},{10,2},{12,4},{14,6},{16,24},{18,... | collective-permute-start | bytes 1474568 | tf_op jit(solution)/shard_map/ppermute | solution.py:1039
  358.6 16.3 %collective-permute-start.29 = (bf16[2,2,2,48,768]{4,3,2,1,0:T(8,128)(2,1)S(1)}, bf16[2,2,2,48,768]{4,3,2,1,0:T(8,128)(2,1)S(1)}, u32[]{:S(2)}, u32[]{:S(2)}) collective-permute-start(bf16[2,2,2,48,768]{4,3,2,1,0:T(8,128)(2,1)S(1)} %slice_bitcast_fusion.4), channel_id=1, source_target_pairs={{0,4},{2,6},{4,0},{6,2},{8,12},{10,14},{12,8},{14,10},{16,20},{18,... | collective-permute-start | bytes 1769480 | tf_op jit(solution)/shard_map/ppermute | solution.py:1039
  360.3 24.5 %collective-permute-start.33 = (bf16[2,2,2,48,768]{4,3,2,1,0:T(8,128)(2,1)S(1)}, bf16[2,2,2,48,768]{4,3,2,1,0:T(8,128)(2,1)S(1)}, u32[]{:S(2)}, u32[]{:S(2)}) collective-permute-start(bf16[2,2,2,48,768]{4,3,2,1,0:T(8,128)(2,1)S(1)} %slice_bitcast_fusion.2), channel_id=1, source_target_pairs={{0,8},{2,10},{4,12},{6,14},{8,0},{10,2},{12,4},{14,6},{16,24},{18,... | collective-permute-start | bytes 1769480 | tf_op jit(solution)/shard_map/ppermute | solution.py:1039
  361.4 27.1 %collective-permute-start.38 = (bf16[2,2,1,112,768]{4,3,1,0,2:T(8,128)(2,1)S(1)}, bf16[2,2,1,112,768]{4,3,1,0,2:T(8,128)(2,1)S(1)}, u32[]{:S(2)}, u32[]{:S(2)}) collective-permute-start(bf16[2,2,1,112,768]{4,3,1,0,2:T(8,128)(2,1)S(1)} %slice_bitcast_fusion), channel_id=1, source_target_pairs={{0,4},{2,6},{4,0},{6,2},{8,12},{10,14},{12,8},{14,10},{16,20},{18,... | collective-permute-start | bytes 2064392 | tf_op jit(solution)/shard_map/ppermute | solution.py:1039
  372.2 16.5 %collective-permute-start.43 = (bf16[2,1,80,768]{3,2,0,1:T(8,128)(2,1)S(1)}, bf16[2,1,80,768]{3,2,0,1:T(8,128)(2,1)S(1)}, u32[]{:S(2)}, u32[]{:S(2)}) collective-permute-start(bf16[2,1,80,768]{3,2,0,1:T(8,128)(2,1)S(1)} %slice_bitcast_fusion.22), channel_id=1, source_target_pairs={{0,16},{2,18},{4,20},{6,22},{8,24},{10,26},{12,28},{14,30},{16,0},... | collective-permute-start | bytes 737288 | tf_op jit(solution)/shard_map/ppermute | solution.py:1039
  385.1 11.8 %collective-permute-start.34 = (bf16[2,2,48,768]{3,2,1,0:T(8,128)(2,1)S(1)}, bf16[2,2,48,768]{3,2,1,0:T(8,128)(2,1)S(1)}, u32[]{:S(2)}, u32[]{:S(2)}) collective-permute-start(bf16[2,2,48,768]{3,2,1,0:T(8,128)(2,1)S(1)} %slice_bitcast_fusion.10), channel_id=1, source_target_pairs={{0,16},{2,18},{4,20},{6,22},{8,24},{10,26},{12,28},{14,30},{16,0},... | collective-permute-start | bytes 884744 | tf_op jit(solution)/shard_map/ppermute | solution.py:1039
  385.5 14.7 %collective-permute-start.30 = (bf16[2,2,48,768]{3,2,1,0:T(8,128)(2,1)S(1)}, bf16[2,2,48,768]{3,2,1,0:T(8,128)(2,1)S(1)}, u32[]{:S(2)}, u32[]{:S(2)}) collective-permute-start(bf16[2,2,48,768]{3,2,1,0:T(8,128)(2,1)S(1)} %slice_bitcast_fusion.12), channel_id=1, source_target_pairs={{0,8},{2,10},{4,12},{6,14},{8,0},{10,2},{12,4},{14,6},{16,24},{18,... | collective-permute-start | bytes 884744 | tf_op jit(solution)/shard_map/ppermute | solution.py:1039
  388.8 5.8 %collective-permute-start.44 = (bf16[1,80,768]{2,1,0:T(8,128)(2,1)S(1)}, bf16[1,80,768]{2,1,0:T(8,128)(2,1)S(1)}, u32[]{:S(2)}, u32[]{:S(2)}) collective-permute-start(bf16[1,80,768]{2,1,0:T(8,128)(2,1)S(1)} %slice_bitcast_fusion.45), channel_id=1, source_target_pairs={{0,4},{2,6},{4,0},{6,2},{8,12},{10,14},{12,8},{14,10},{16,20},{18,... | collective-permute-start | bytes 368648 | tf_op jit(solution)/shard_map/ppermute | solution.py:1039
  390.4 15.1 %collective-permute-start.39 = (bf16[2,1,112,768]{3,2,0,1:T(8,128)(2,1)S(1)}, bf16[2,1,112,768]{3,2,0,1:T(8,128)(2,1)S(1)}, u32[]{:S(2)}, u32[]{:S(2)}) collective-permute-start(bf16[2,1,112,768]{3,2,0,1:T(8,128)(2,1)S(1)} %slice_bitcast_fusion.8), channel_id=1, source_target_pairs={{0,8},{2,10},{4,12},{6,14},{8,0},{10,2},{12,4},{14,6},{16,24},{18,... | collective-permute-start | bytes 1032200 | tf_op jit(solution)/shard_map/ppermute | solution.py:1039
  394.6 7.2 %collective-permute-start.45 = (bf16[1,80,768]{2,1,0:T(8,128)(2,1)S(1)}, bf16[1,80,768]{2,1,0:T(8,128)(2,1)S(1)}, u32[]{:S(2)}, u32[]{:S(2)}) collective-permute-start(bf16[1,80,768]{2,1,0:T(8,128)(2,1)S(1)} %fusion.23), channel_id=1, source_target_pairs={{0,1},{1,0},{2,3},{3,2},{4,5},{5,4},{6,7},{7,6},{8,9},{9,8},{10,11... | collective-permute-start | bytes 368648 | tf_op jit(solution)/shard_map/ppermute | solution.py:1039
  397.0 9.2 %collective-permute-start.35 = (bf16[2,48,768]{2,1,0:T(8,128)(2,1)S(1)}, bf16[2,48,768]{2,1,0:T(8,128)(2,1)S(1)}, u32[]{:S(2)}, u32[]{:S(2)}) collective-permute-start(bf16[2,48,768]{2,1,0:T(8,128)(2,1)S(1)} %slice_bitcast_fusion.33), channel_id=1, source_target_pairs={{0,4},{2,6},{4,0},{6,2},{8,12},{10,14},{12,8},{14,10},{16,20},{18,... | collective-permute-start | bytes 442376 | tf_op jit(solution)/shard_map/ppermute | solution.py:1039
  400.3 11.8 %collective-permute-start.31 = (bf16[2,48,768]{2,1,0:T(8,128)(2,1)S(1)}, bf16[2,48,768]{2,1,0:T(8,128)(2,1)S(1)}, u32[]{:S(2)}, u32[]{:S(2)}) collective-permute-start(bf16[2,48,768]{2,1,0:T(8,128)(2,1)S(1)} %slice_bitcast_fusion.35), channel_id=1, source_target_pairs={{0,16},{2,18},{4,20},{6,22},{8,24},{10,26},{12,28},{14,30},{16,0},... | collective-permute-start | bytes 442376 | tf_op jit(solution)/shard_map/ppermute | solution.py:1039
  405.6 10.1 %collective-permute-start.40 = (bf16[1,112,768]{2,1,0:T(8,128)(2,1)S(1)}, bf16[1,112,768]{2,1,0:T(8,128)(2,1)S(1)}, u32[]{:S(2)}, u32[]{:S(2)}) collective-permute-start(bf16[1,112,768]{2,1,0:T(8,128)(2,1)S(1)} %slice_bitcast_fusion.31), channel_id=1, source_target_pairs={{0,16},{2,18},{4,20},{6,22},{8,24},{10,26},{12,28},{14,30},{16,0},... | collective-permute-start | bytes 516104 | tf_op jit(solution)/shard_map/ppermute | solution.py:1039
  406.2 9.4 %collective-permute-start.36 = (bf16[2,48,768]{2,1,0:T(8,128)(2,1)S(1)}, bf16[2,48,768]{2,1,0:T(8,128)(2,1)S(1)}, u32[]{:S(2)}, u32[]{:S(2)}) collective-permute-start(bf16[2,48,768]{2,1,0:T(8,128)(2,1)S(1)} %fusion.17), channel_id=1, source_target_pairs={{0,1},{1,0},{2,3},{3,2},{4,5},{5,4},{6,7},{7,6},{8,9},{9,8},{10,11... | collective-permute-start | bytes 442376 | tf_op jit(solution)/shard_map/ppermute | solution.py:1039
  412.1 6.6 %collective-permute-start.32 = (bf16[2,48,768]{2,1,0:T(8,128)(2,1)S(1)}, bf16[2,48,768]{2,1,0:T(8,128)(2,1)S(1)}, u32[]{:S(2)}, u32[]{:S(2)}) collective-permute-start(bf16[2,48,768]{2,1,0:T(8,128)(2,1)S(1)} %fusion.18), channel_id=1, source_target_pairs={{0,1},{1,0},{2,3},{3,2},{4,5},{5,4},{6,7},{7,6},{8,9},{9,8},{10,11... | collective-permute-start | bytes 442376 | tf_op jit(solution)/shard_map/ppermute | solution.py:1039
  415.7 5.5 %collective-permute-start.41 = (bf16[1,112,768]{2,1,0:T(8,128)(2,1)S(1)}, bf16[1,112,768]{2,1,0:T(8,128)(2,1)S(1)}, u32[]{:S(2)}, u32[]{:S(2)}) collective-permute-start(bf16[1,112,768]{2,1,0:T(8,128)(2,1)S(1)} %fusion.16), channel_id=1, source_target_pairs={{0,1},{1,0},{2,3},{3,2},{4,5},{5,4},{6,7},{7,6},{8,9},{9,8},{10,11... | collective-permute-start | bytes 516104 | tf_op jit(solution)/shard_map/ppermute | solution.py:1039
  (11 other events, 47.1 us)

commit v2 on v1

--- a/solution.py
+++ b/solution.py
@@ -136,8 +136,8 @@
             if j > 0:
                 out_re = out_re - sign * spec[j - 1, im, lanes]
                 out_im = out_im + sign * spec[j - 1, re, lanes]
-            kern_out[j, re, lanes] = out_re * scale
-            kern_out[j, im, lanes] = out_im * scale
+            kern_out[j, re, lanes] = (out_re * scale).astype(BF16)
+            kern_out[j, im, lanes] = (out_im * scale).astype(BF16)
 
     spectral_loop(channels, combine)
     taps_out[...] = dot(table_ref[:, : taps_ref.shape[0]], taps_ref[...].astype(BF16)) * scale
@@ -161,7 +161,7 @@
             pl.BlockSpec((2 * BLOCK, tile), column),
         ],
         out_shape=[
-            jax.ShapeDtypeStruct((blocks, 2 * BLOCK, channels), F32),
+            jax.ShapeDtypeStruct((blocks, 2 * BLOCK, channels), BF16),
             jax.ShapeDtypeStruct((2 * BLOCK, channels), F32),
         ],
         scratch_shapes=[
@@ -231,7 +231,7 @@
 
     def state_product(sign, re, im, lanes):
         x = [(spec[b, re, lanes], spec[b, im, lanes]) for b in range(blocks)]
-        h = [(kern_ref[b, re, lanes], kern_ref[b, im, lanes]) for b in range(blocks)]
+        h = [(kern_ref[b, re, lanes].astype(F32), kern_ref[b, im, lanes].astype(F32)) for b in range(blocks)]
         for i in range(blocks):
             yr, yi = multiply(*x[i], *h[0])
             for d in range(1, i + 1):
@@ -314,247 +314,451 @@
     return x * phi, phi + x * bell * (1.0 / math.sqrt(2.0 * math.pi))
 
 
-def share_out(grad, send_ref, keep_ref, mine, share):
-    bits = [send_ref.shape[i] for i in range(send_ref.ndim - 3)]
-    count = math.prod(bits)
-    for half, ref in ((0, keep_ref), (1, send_ref)):
-        for spot in range(count):
-            relative, left, place = 0, spot, []
-            for size in reversed(bits):
-                place.append(left % size)
-                left //= size
-            place = place[::-1]
-            for axis, bit in enumerate(place):
-                relative += bit << axis
-            owner = jnp.bitwise_xor(mine, 2 * relative + half)
-            low = pl.multiple_of(owner * share, share)
-            ref[(*place, 0)] = grad[pl.ds(low, share), :].astype(BF16)
+def bit_of(index, bit):
+    return lax.rem(index // bit, 2)
+
+
+def partner(axis, bit):
+    index = lax.axis_index(axis)
+    return {axis: index + bit * (1 - 2 * bit_of(index, bit))}
+
+
+CORE, MIDDLE, NEAR, FAR, SIDE = ("dp", 1), ("dp", 2), ("dp", 4), ("dp", 8), ("seq", 1)
+
+
+def greet(partners):
+    barrier = pltpu.get_barrier_semaphore()
+    for axis, bit in partners:
+        pl.semaphore_signal(barrier, inc=1, device_id=partner(axis, bit), device_id_type=pl.DeviceIdType.MESH)
+    pl.semaphore_wait(barrier, len(partners))
+
+
+def transfer(source, target, sems, to):
+    return pltpu.make_async_remote_copy(
+        src_ref=source,
+        dst_ref=target,
+        send_sem=sems.at[0],
+        recv_sem=sems.at[1],
+        device_id=partner(*to),
+        device_id_type=pl.DeviceIdType.MESH,
+    )
+
+
+def add_into(target, other):
+    target[...] = target[...] + other[...]
+
+
+def owner_bits(mine, relative):
+    total = 0
+    for bit, differs in relative.items():
+        own = bit_of(mine, bit)
+        total = total + bit * (1 - own if differs else own)
+    return total
+
+
+def share_all(grad, send, keep, rows, share):
+    mine = lax.axis_index("dp")
+    for core, ref in ((0, keep), (1, send)):
+        for x in range(2):
+            for near in range(2):
+                for far in range(2):
+                    owner = owner_bits(mine, {1: core, 2: x, 4: near, 8: far})
+                    low = pl.multiple_of(owner * share, 8)
+                    ref[x, near, far, rows, :] = grad[pl.ds(low, share), :].astype(BF16)
+
+
+class Sum:
+    def __init__(self, send, keep, chain, sems, outer, start=0):
+        self.send, self.keep, self.chain, self.sems = send, keep, chain, sems
+        self.outer, self.start = outer, start
+
+    def given(self, step, half):
+        ref = self.chain[step]
+        if step == 3:
+            return ref
+        if self.outer and step in (0, 1):
+            return ref.at[:, half]
+        return ref.at[half]
+
+    def copy(self, step):
+        order = (CORE, NEAR, FAR, MIDDLE, SIDE) if self.outer else (CORE, MIDDLE, NEAR, FAR, SIDE)
+        source = self.send if step == self.start else self.given(step - 1, 1)
+        return transfer(source, self.chain[step], self.sems.at[step], order[step])
+
+    def begin(self):
+        self.copy(self.start).start()
+
+    def add(self, step):
+        self.copy(step).wait()
+        kept = self.keep if step == self.start else self.given(step - 1, 0)
+        add_into(self.chain[step], kept)
+
+    def advance(self, step):
+        self.add(step)
+        self.copy(step + 1).start()
+
+    def finish(self):
+        self.copy(4).wait()
+        return self.chain[3][...].astype(F32) + self.chain[4][...].astype(F32)
+
+
+class Gather:
+    def __init__(self, z, source, first, chain, sems):
+        self.z, self.source, self.first, self.chain, self.sems = z, source, first, chain, sems
+        mine = lax.axis_index("dp")
+        self.near = bit_of(mine, 4) == bit_of(z, 1)
+        self.far = bit_of(mine, 8) == bit_of(z, 2)
+
+    def copy(self, step):
+        if step == self.first:
+            source = self.source if step else self.source.at[1]
+        else:
+            source = self.chain[step - 1]
+        return transfer(source, self.chain[step], self.sems.at[step], (MIDDLE, NEAR, FAR, SIDE)[step])
+
+    def both(self):
+        return jnp.logical_and(self.near, self.far)
+
+    def step_x(self):
+        self.copy(0).wait()
+        add_into(self.chain[0], self.source.at[0])
+
+    def send_near(self):
+        @pl.when(jnp.logical_not(self.near))
+        def _():
+            self.copy(1).start()
+
+    def step_near(self):
+        kept = self.source if self.first == 1 else self.chain[0]
+
+        @pl.when(jnp.logical_not(self.near))
+        def _():
+            self.copy(1).wait_send()
+
+        @pl.when(self.near)
+        def _():
+            self.copy(1).wait_recv()
+            add_into(self.chain[1], kept)
+
+        @pl.when(jnp.logical_and(self.near, jnp.logical_not(self.far)))
+        def _():
+            self.copy(2).start()
+
+    def step_far(self):
+        @pl.when(jnp.logical_and(self.near, jnp.logical_not(self.far)))
+        def _():
+            self.copy(2).wait_send()
+
+        @pl.when(self.both())
+        def _():
+            self.copy(2).wait_recv()
+            add_into(self.chain[2], self.chain[1])
+            self.copy(3).start()
+
+    def finish(self, out):
+        @pl.when(self.both())
+        def _():
+            self.copy(3).wait()
+            out[...] = self.chain[2][...].astype(F32) + self.chain[3][...].astype(F32)
 
 
 def ffn_body(
-    length_ref, place_ref, a_two_ref, cot_ref, hidden_ref, up_ref, down_ref,
-    out_ref, d_pre_ref, send_ref, keep_ref, total, act, d_down, grad,
+    length_ref, a_two_ref, cot_ref, hidden_ref, gain_ref, up_ref, down_ref,
+    out_ref, d_hidden_ref, d_mixer_ref, gain_grad_ref, up_out, down_out, up_two, up_three, down_two, down_three,
+    total, back, act, d_pre, d_down, grad,
+    up_send, up_keep, up_r0, up_r1, up_r2, up_r3, up_r4, up_sems,
+    down_send, down_keep, down_r0, down_r1, down_r2, down_r3, down_r4, down_sems, down_core_sems,
 ):
     j = pl.program_id(0)
+    last = pl.num_programs(0) - 1
     length, width = a_two_ref.shape
     tile = up_ref.shape[1]
     live = length_ref[0]
     rows_count = 256
+    share_up, share_down = width // 16, tile // 4
+
+    def early(t):
+        return min(t, 1) if isinstance(t, int) else t
+
+    def up_sum(t):
+        r1 = up_r1.at[min(t, 2) if isinstance(t, int) else t]
+        chain = [up_r0.at[t], r1, up_r2.at[early(t)], up_r3.at[early(t)], up_r4.at[early(t)]]
+        return Sum(up_send, up_keep, chain, up_sems.at[t], True)
+
+    def down_core(t):
+        return transfer(down_send, down_r0.at[t], down_core_sems.at[t], CORE)
+
+    def down_sum(t):
+        chain = [down_r1.at[t], down_r2.at[early(t)], down_r3.at[early(t)], down_r4.at[early(t)]]
+        return Gather(t, down_r0.at[t], 0, chain, down_sems.at[t])
 
     @pl.when(j == 0)
     def _():
+        greet((CORE, MIDDLE, NEAR, FAR, SIDE))
         for low in range(0, length, rows_count):
             rows = slice(low, low + rows_count)
             d_down[rows, :] = (cot_ref[rows, :].astype(F32) * live_rows(live, low, rows_count)).astype(BF16)
         total[...] = jnp.zeros_like(total)
-
-    for low in range(0, length, rows_count):
+        back[...] = jnp.zeros_like(back)
+        down_out[...] = jnp.zeros_like(down_out)
+
+    def chunk(low):
         rows = slice(low, low + rows_count)
         pre = dot(a_two_ref[rows, :], up_ref[...])
         d_act = dot_nt(d_down[rows, :], down_ref[...])
         value, slope = gelu_pair(pre)
         act[rows, :] = value.astype(BF16)
-        d_pre_ref[rows, :] = (d_act * slope).astype(BF16)
+        d_pre[rows, :] = (d_act * slope).astype(BF16)
         total[rows, :] += dot(act[rows, :], down_ref[...])
+        back[rows, :] += dot_nt(d_pre[rows, :], up_ref[...])
+
+    def join_core(t):
+        up_sum(t).add(0)
+        down_core(t).wait()
+        add_into(down_r0.at[t], down_keep)
+
+    chunk(0)
+
+    @pl.when(j >= 1)
+    def _():
+        join_core(j - 1)
+        up_sum(j - 1).copy(1).start()
+        down_sum(j - 1).copy(0).start()
+
+    @pl.when(j >= 2)
+    def _():
+        up_sum(j - 2).advance(2)
+        down_sum(j - 2).step_near()
+
+    chunk(rows_count)
+
+    @pl.when(j >= 2)
+    def _():
+        up_sum(j - 2).advance(3)
+
+    chunk(2 * rows_count)
+
+    @pl.when(j >= 2)
+    def _():
+        down_sum(j - 2).step_far()
+
+    chunk(3 * rows_count)
+
+    @pl.when(jnp.logical_and(j >= 1, j < last))
+    def _():
+        up_sum(j - 1).advance(1)
+        down_sum(j - 1).step_x()
+        down_sum(j - 1).send_near()
+
+    @pl.when(j == last)
+    def _():
+        up_sum(2).add(1)
+        down_sum(2).step_x()
+        up_two[...] = up_r1[2]
+        down_two[...] = down_r1[2]
+
+    @pl.when(j >= 2)
+    def _():
+        up_out[j - 2] = up_sum(j - 2).finish()
+        down_sum(j - 2).finish(down_out)
+
     grad[...] = dot_tn(act[...], d_down[...])
-    share = tile // 4
-    share_out(grad, send_ref.at[:, 0], keep_ref.at[:, 0], place_ref[0] & 3, share)
-
-    @pl.when(j == pl.num_programs(0) - 1)
-    def _():
-        for low in range(0, length, rows_count):
-            rows = slice(low, low + rows_count)
-            mask = live_rows(live, low, rows_count)
-            out_ref[rows, :] = (hidden_ref[rows, :] + mask * total[rows, :]).astype(BF16)
-
-
-def ffn_call(live, place, a_two, cot, hidden, up, down):
-    length, width = a_two.shape
-    hidden_units = up.shape[1]
-    tile = hidden_units // 4
-    share = tile // 4
-    whole = lambda j, n, p: (0, 0)
-    rows_full = pl.BlockSpec((length, width), whole)
-
-    def z_place(j, n, p):
-        z = jnp.bitwise_xor(j, p[0] >> 2)
-        return (0, z & 1, z >> 1, 0, 0)
-
-    half_spec = pl.BlockSpec((2, 1, 1, share, width), z_place)
-    half_shape = jax.ShapeDtypeStruct((2, 2, 2, share, width), BF16)
-    return pl.pallas_call(
-        ffn_body,
-        grid_spec=pltpu.PrefetchScalarGridSpec(
-            num_scalar_prefetch=2,
-            grid=(4,),
-            in_specs=[
-                rows_full,
-                rows_full,
-                rows_full,
-                pl.BlockSpec((width, tile), lambda j, n, p: (0, j)),
-                pl.BlockSpec((tile, width), lambda j, n, p: (j, 0)),
-            ],
-            out_specs=[
-                rows_full,
-                pl.BlockSpec((length, tile), lambda j, n, p: (0, j)),
-                half_spec,
-                half_spec,
-            ],
-            scratch_shapes=[
-                pltpu.VMEM((length, width), F32),
-                pltpu.VMEM((length, tile), BF16),
-                pltpu.VMEM((length, width), BF16),
-                pltpu.VMEM((tile, width), F32),
-            ],
-        ),
-        out_shape=[
-            jax.ShapeDtypeStruct((length, width), BF16),
-            jax.ShapeDtypeStruct((length, hidden_units), BF16),
-            half_shape,
-            half_shape,
-        ],
-        compiler_params=params(),
-        cost_estimate=cost(8 * length * width * hidden_units, 40e6),
-        name="feed_forward",
-    )(live, place, a_two, cot, hidden, up, down)
-
-
-def ffn_back_body(
-    length_ref, place_ref, a_two_ref, d_pre_ref, up_ref, cot_ref, hidden_ref, gain_ref,
-    d_hidden_ref, d_mixer_ref, gain_grad_ref, send_ref, keep_ref, total, grad,
-):
-    j = pl.program_id(0)
-    length, width = a_two_ref.shape
-    live = length_ref[0]
-    rows_count = 256
-    grad[...] = dot_tn(a_two_ref[...], d_pre_ref[...])
-    share_out(grad, send_ref, keep_ref, place_ref[0], send_ref.shape[-2])
-
-    @pl.when(j == 0)
-    def _():
-        total[...] = jnp.zeros_like(total)
-
-    for low in range(0, length, rows_count):
-        rows = slice(low, low + rows_count)
-        total[rows, :] += dot_nt(d_pre_ref[rows, :], up_ref[...])
-
-    @pl.when(j == pl.num_programs(0) - 1)
+    mine = lax.axis_index("dp")
+    for core, ref in ((0, down_keep), (1, down_send)):
+        for x in range(2):
+            low = pl.multiple_of(owner_bits(mine, {1: core, 2: x}) * share_down, 8)
+            ref[x] = grad[pl.ds(low, share_down), :].astype(BF16)
+    down_core(j).start()
+    grad[...] = dot_tn(a_two_ref[...], d_pre[...])
+    share_all(grad, up_send, up_keep, slice(None), share_up)
+    up_sum(j).begin()
+
+    @pl.when(j == last)
     def _():
         gain_sum = jnp.zeros((1, width), F32)
         for low in range(0, length, rows_count):
             rows = slice(low, low + rows_count)
             mask = live_rows(live, low, rows_count)
-            normed, inv = norm_stats(hidden_ref[rows, :])
-            grad_in = total[rows, :]
+            hidden = hidden_ref[rows, :]
+            out_ref[rows, :] = (hidden + mask * total[rows, :]).astype(BF16)
+            normed, inv = norm_stats(hidden)
+            grad_in = back[rows, :]
             gain_sum = gain_sum + jnp.sum(grad_in * normed, axis=0, keepdims=True)
             d_hidden = cot_ref[rows, :].astype(F32) + norm_pull(grad_in, normed, inv, gain_ref[...])
             d_hidden_ref[rows, :] = d_hidden
             d_mixer_ref[rows, :] = (mask * d_hidden).astype(BF16)
         gain_grad_ref[...] = gain_sum
-
-
-def ffn_back_call(live, place, a_two, d_pre, up, cot, hidden, gain):
+        join_core(3)
+        up_three[...] = up_r0[3]
+        down_three[...] = down_r0[3]
+
+
+def once(shape, index=None):
+    zeros = (0,) * len(shape)
+    return pl.BlockSpec(shape, index or (lambda *_: zeros), pipeline_mode=pl.Buffered(1))
+
+
+def ffn_call(live, a_two, cot, hidden, gain, up, down):
     length, width = a_two.shape
     hidden_units = up.shape[1]
     tile = hidden_units // 4
-    share = width // 16
-    whole = lambda j, n, p: (0, 0)
-    rows_full = pl.BlockSpec((length, width), whole)
-    half_spec = pl.BlockSpec((2, 2, 2, 1, share, tile), lambda j, n, p: (0, 0, 0, j, 0, 0))
-    half_shape = jax.ShapeDtypeStruct((2, 2, 2, 4, share, tile), BF16)
+    su, sd = width // 16, tile // 4
+    rows_full = once((length, width))
+    low = lambda *shape: jax.ShapeDtypeStruct(shape, BF16)
+    full = lambda *shape: jax.ShapeDtypeStruct(shape, F32)
+    vmem = lambda *shape: pltpu.VMEM(shape, BF16)
+    out_shape = [
+        low(length, width),
+        full(length, width),
+        low(length, width),
+        full(1, width),
+        full(2, su, tile),
+        full(sd, width),
+        low(2, 2, su, tile),
+        low(2, 2, 2, su, tile),
+        low(sd, width),
+        low(2, sd, width),
+    ]
     return pl.pallas_call(
-        ffn_back_body,
-        grid_spec=pltpu.PrefetchScalarGridSpec(
-            num_scalar_prefetch=2,
-            grid=(4,),
-            in_specs=[
-                rows_full,
-                pl.BlockSpec((length, tile), lambda j, n, p: (0, j)),
-                pl.BlockSpec((width, tile), lambda j, n, p: (0, j)),
-                rows_full,
-                rows_full,
-                pl.BlockSpec((1, width), whole),
-            ],
-            out_specs=[rows_full, rows_full, pl.BlockSpec((1, width), whole), half_spec, half_spec],
-            scratch_shapes=[pltpu.VMEM((length, width), F32), pltpu.VMEM((width, tile), F32)],
-        ),
-        out_shape=[
-            jax.ShapeDtypeStruct((length, width), F32),
-            jax.ShapeDtypeStruct((length, width), BF16),
-            jax.ShapeDtypeStruct((1, width), F32),
-            half_shape,
-            half_shape,
+        ffn_body,
+        grid=(4,),
+        in_specs=[
+            pl.BlockSpec(memory_space=pltpu.SMEM),
+            rows_full,
+            rows_full,
+            rows_full,
+            once((1, width)),
+            pl.BlockSpec((width, tile), lambda j: (0, j)),
+            pl.BlockSpec((tile, width), lambda j: (j, 0)),
         ],
-        compiler_params=params(),
-        cost_estimate=cost(4 * length * width * hidden_units, 40e6),
-        name="feed_forward_back",
-    )(live, place, a_two, d_pre, up, cot, hidden, gain)
-
-
-def gate_back_body(
-    place_ref, d_mixer_ref, wout_ref, state_ref, q_ref, gated_ref, a_one_ref,
-    d_query_ref, d_state_ref, send_ref, keep_ref, grad,
-):
-    length, width = d_mixer_ref.shape
-    rows_count = 256
-    share = width // 16
-    mine = place_ref[0]
-    grad[...] = dot_tn(gated_ref[...], d_mixer_ref[...])
-    share_out(grad, send_ref.at[:, :, :, 0:1], keep_ref.at[:, :, :, 0:1], mine, share)
-    for low in range(0, length, rows_count):
-        rows = slice(low, low + rows_count)
-        d_gated = dot_nt(d_mixer_ref[rows, :], wout_ref[...])
-        d_query_ref[rows, :] = (d_gated * state_ref[rows, :].astype(F32)).astype(BF16)
-        d_state_ref[rows, :] = (d_gated * q_ref[rows, :].astype(F32)).astype(BF16)
-    grad[...] = dot_tn(a_one_ref[...], d_query_ref[...])
-    share_out(grad, send_ref.at[:, :, :, 1:2], keep_ref.at[:, :, :, 1:2], mine, share)
-
-
-def gate_back_call(place, d_mixer, wout, state, q, gated, a_one):
-    length, width = d_mixer.shape
-    share = width // 16
-    whole = lambda i, p: (0, 0)
-    rows_full = pl.BlockSpec((length, width), whole)
-    half_spec = pl.BlockSpec((2, 2, 2, 2, share, width), lambda i, p: (0, 0, 0, 0, 0, 0))
-    half_shape = jax.ShapeDtypeStruct((2, 2, 2, 2, share, width), BF16)
-    low = jax.ShapeDtypeStruct((length, width), BF16)
-    return pl.pallas_call(
-        gate_back_body,
-        grid_spec=pltpu.PrefetchScalarGridSpec(
-            num_scalar_prefetch=1,
-            grid=(1,),
-            in_specs=[rows_full, pl.BlockSpec(wout.shape, whole)] + [rows_full] * 4,
-            out_specs=[rows_full, rows_full, half_spec, half_spec],
-            scratch_shapes=[pltpu.VMEM((width, width), F32)],
-        ),
-        out_shape=[low, low, half_shape, half_shape],
-        compiler_params=params(),
-        cost_estimate=cost(6 * length * width * width, 15e6),
-        name="gate_back",
-    )(place, d_mixer, wout, state, q, gated, a_one)
+        out_specs=[once(s.shape) for s in out_shape],
+        out_shape=out_shape,
+        scratch_shapes=[
+            pltpu.VMEM((length, width), F32),
+            pltpu.VMEM((length, width), F32),
+            vmem(length, tile),
+            vmem(length, tile),
+            vmem(length, width),
+            pltpu.VMEM((tile, width), F32),
+            vmem(2, 2, 2, su, tile),
+            vmem(2, 2, 2, su, tile),
+            vmem(4, 2, 2, 2, su, tile),
+            vmem(3, 2, 2, su, tile),
+            vmem(2, 2, su, tile),
+            vmem(2, su, tile),
+            vmem(2, su, tile),
+            pltpu.SemaphoreType.DMA((4, 5, 2)),
+            vmem(2, sd, width),
+            vmem(2, sd, width),
+            vmem(4, 2, sd, width),
+            vmem(3, sd, width),
+            vmem(2, sd, width),
+            vmem(2, sd, width),
+            vmem(2, sd, width),
+            pltpu.SemaphoreType.DMA((4, 4, 2)),
+            pltpu.SemaphoreType.DMA((4, 2)),
+        ],
+        compiler_params=pltpu.CompilerParams(vmem_limit_bytes=VMEM_BYTES, collective_id=1, has_side_effects=True),
+        cost_estimate=cost(12 * length * width * hidden_units, 40e6),
+        name="feed_forward",
+    )(live, a_two, cot, hidden, gain, up, down)
 
 
 def mixer_back_body(
-    length_ref, place_ref, d_state_ref, d_query_ref, mixed_ref, shifted_ref, k_ref, v_ref, a_one_ref,
-    wq_ref, wk_ref, wv_ref, kern_ref, tapspec_ref, table_ref, back_ref, x_ref, gain_ref, d_hidden_ref,
-    d_x_ref, gain_grad_ref, d_taps_ref, send_ref, keep_ref, dk_send_ref, dk_keep_ref,
-    total, spec_one, spec_two, prod, kern_prod, d_keys, d_values, grad, d_kern,
+    length_ref, out_row_ref, d_mixer_ref, wout_ref, state_ref, q_ref, gated_ref, a_one_ref,
+    mixed_ref, shifted_ref, k_ref, v_ref, wq_ref, wk_ref, wv_ref, kern_ref, tapspec_ref, table_ref, back_ref,
+    x_ref, gain_ref, d_hidden_ref, up_two_ref, up_three_ref, down_two_ref, down_three_ref, up_part_ref, down_part_ref,
+    out_ref, d_tokens_ref, gain_grad_ref, d_taps_ref, up_ref, down_ref, gate_ref, kv_ref, d_kern_ref,
+    total, spec_one, spec_two, prod, kern_prod, d_keys, d_values, d_query, d_state, grad, d_kern, d_x,
+    up_two_r1, up_two_r2, up_two_r3, up_two_r4, up_three_r1, up_three_r2, up_three_r3, up_three_r4, up_sems,
+    down_two_r, down_three_r, down_sems,
+    gate_send, gate_keep, gate_r0, gate_r1, gate_r2, gate_r3, gate_r4, gate_sems,
+    kv_send, kv_keep, kv_r0, kv_r1, kv_r2, kv_r3, kv_r4, kv_sems,
+    out_sems, row_sems, own_sems,
 ):
     j = pl.program_id(0)
+    tiles = pl.num_programs(0)
     length, width = a_one_ref.shape
+    half = length // 2
     tile = k_ref.shape[1]
     blocks = length // BLOCK
+    share = width // 16
+    kern_share = length // 16
     live = length_ref[0]
-    mine = place_ref[0]
+    side = lax.axis_index("seq")
+    columns = pl.ds(pl.multiple_of(j * tile, tile), tile)
+    own_rows = pl.ds(pl.multiple_of(side * half, half), half)
+    other_rows = pl.ds(pl.multiple_of((1 - side) * half, half), half)
+
+    up_two = Sum(up_two_ref.at[:, 1], up_two_ref.at[:, 0], [None, None, up_two_r2, up_two_r3, up_two_r4], up_sems.at[0], True, 2)
+    up_three = Sum(
+        up_three_ref.at[:, 1], up_three_ref.at[:, 0], [None, up_three_r1, up_three_r2, up_three_r3, up_three_r4],
+        up_sems.at[1], True, 1,
+    )
+    down_two = Gather(2, down_two_ref, 1, [None] + [down_two_r.at[i] for i in range(1, 4)], down_sems.at[0])
+    down_three = Gather(3, down_three_ref, 0, [down_three_r.at[i] for i in range(4)], down_sems.at[1])
+    gate = Sum(gate_send, gate_keep, [gate_r0, gate_r1, gate_r2, gate_r3, gate_r4], gate_sems, False)
+
+    def kv(t):
+        chain = [kv_r0.at[t], kv_r1.at[t], kv_r2.at[t], kv_r3.at[t], kv_r4.at[t]]
+        return Sum(kv_send, kv_keep, chain, kv_sems.at[t], False)
+
+    def kv_finish(t):
+        value = kv(t).finish()
+        place = slice(t * tile, (t + 1) * tile)
+        kv_ref[0, :, place] = value[:share]
+        kv_ref[1, :, place] = value[share : 2 * share]
+        d_kern_ref[:, place] = value[2 * share :]
+
+    def send_out():
+        return transfer(out_row_ref.at[other_rows], out_ref.at[side], out_sems, SIDE)
+
+    def keep_out():
+        return pltpu.make_async_copy(out_row_ref.at[own_rows], out_ref.at[side], own_sems.at[0])
+
+    def send_row():
+        return transfer(d_x.at[0], d_tokens_ref.at[side], row_sems, SIDE)
+
+    def keep_row():
+        return pltpu.make_async_copy(d_x.at[1], d_tokens_ref.at[side], own_sems.at[1])
+
+    @pl.when(j == 0)
+    def _():
+        greet((CORE, MIDDLE, NEAR, FAR, SIDE))
+        up_three.begin()
+        up_two.begin()
+        down_three.copy(0).start()
+        down_two.send_near()
+        send_out().start()
+        keep_out().start()
+        total[:width, :] = dot_tn(gated_ref[...], d_mixer_ref[...])
+        share_all(total, gate_send, gate_keep, slice(0, share), share)
+        for b in range(blocks):
+            rows = slice(b * BLOCK, (b + 1) * BLOCK)
+            d_gated = dot_nt(d_mixer_ref[rows, :], wout_ref[...])
+            low_query = (d_gated * state_ref[rows, :].astype(F32)).astype(BF16)
+            low_state = (d_gated * q_ref[rows, :].astype(F32)).astype(BF16)
+            d_query[rows, :] = low_query
+            for t in range(width // tile):
+                d_state[t, rows, :] = low_state[:, t * tile : (t + 1) * tile]
+        total[:width, :] = dot_tn(a_one_ref[...], d_query[...])
+        share_all(total, gate_send, gate_keep, slice(share, 2 * share), share)
+        total[...] = jnp.zeros_like(total)
+        gate.begin()
+        up_three.advance(1)
+        up_two.advance(2)
+        down_three.step_x()
+        down_three.send_near()
+        down_two.step_near()
 
     for b in range(blocks):
         rows = slice(b * BLOCK, (b + 1) * BLOCK)
-        spec_one[b] = dot(table_ref[...], d_state_ref[rows, :])
+        spec_one[b] = dot(table_ref[...], d_state[j, rows, :])
         spec_two[b] = dot(table_ref[...], mixed_ref[rows, :])
 
     def state_product(sign, re, im, lanes):
         s = [(spec_one[b, re, lanes], spec_one[b, im, lanes]) for b in range(blocks)]
-        h = [(kern_ref[b, re, lanes], kern_ref[b, im, lanes]) for b in range(blocks)]
+        h = [(kern_ref[b, re, lanes].astype(F32), kern_ref[b, im, lanes].astype(F32)) for b in range(blocks)]
         for b in range(blocks):
             yr, yi = multiply_conj(*h[0], *s[b])
             for i in range(b + 1, blocks):
@@ -583,6 +787,29 @@
             kern_prod[d, im, lanes] = hi.astype(BF16)
 
     spectral_loop(tile, kernel_product)
+
+    @pl.when(j == 0)
+    def _():
+        gate.advance(0)
+        up_three.advance(2)
+        up_two.advance(3)
+        down_three.step_near()
+        down_two.step_far()
+
+    @pl.when(j >= 1)
+    def _():
+        kv(j - 1).advance(0)
+
+    @pl.when(j == 1)
+    def _():
+        gate.advance(3)
+        up_ref[:, 2 * width : 3 * width] = up_two.finish()
+        up_ref[:, 3 * width : 4 * width] = up_three.finish()
+
+    @pl.when(j == 2)
+    def _():
+        kv_finish(0)
+
     for b in range(blocks):
         rows = slice(b * BLOCK, (b + 1) * BLOCK)
         mask = live_rows(live, b * BLOCK, BLOCK)
@@ -592,6 +819,26 @@
         spec_one[b] = dot(table_ref[...], d_shifted)
         spec_two[b] = dot(table_ref[...], k_ref[rows, :])
         d_kern[rows, :] = dot(back_ref[...], kern_prod[b]) * (1.0 / BLOCK)
+
+    @pl.when(j == 0)
+    def _():
+        gate.advance(1)
+        up_three.advance(3)
+        down_three.step_far()
+
+    @pl.when(j >= 1)
+    def _():
+        kv(j - 1).advance(1)
+
+    @pl.when(j == 1)
+    def _():
+        for i in range(2):
+            up_ref[:, i * width : (i + 1) * width] = up_part_ref[i]
+        down_ref[...] = down_part_ref[...]
+        down_two.finish(down_ref)
+        down_three.finish(down_ref)
+        send_out().wait()
+        keep_out().wait()
 
     def shift_product(sign, re, im, lanes):
         tr = tapspec_ref[re, lanes]
@@ -620,110 +867,183 @@
         mask = live_rows(live, b * BLOCK, BLOCK)
         d_keys[rows, :] = (mask * dot(back_ref[...], prod[b])).astype(BF16)
     taps = d_taps_ref.shape[0]
-    d_taps_ref[...] = dot(back_ref[:taps, :], kern_prod[0]) * (1.0 / BLOCK)
-
-    share_out(d_kern, dk_send_ref, dk_keep_ref, mine, length // 16)
-    share = width // 16
-    grad[...] = dot_tn(a_one_ref[...], d_keys[...])
-    share_out(grad, send_ref.at[:, :, :, 0:1], keep_ref.at[:, :, :, 0:1], mine, share)
-    grad[...] = dot_tn(a_one_ref[...], d_values[...])
-    share_out(grad, send_ref.at[:, :, :, 1:2], keep_ref.at[:, :, :, 1:2], mine, share)
+    d_taps_ref[:, columns] = dot(back_ref[:taps, :], kern_prod[0]) * (1.0 / BLOCK)
 
     @pl.when(j == 0)
     def _():
-        total[...] = jnp.zeros_like(total)
-
-    for b in range(blocks):
-        rows = slice(b * BLOCK, (b + 1) * BLOCK)
-        total[rows, :] += (
-            dot_nt(d_query_ref[rows, :], wq_ref[...])
+        gate.advance(2)
+
+    @pl.when(j >= 1)
+    def _():
+        kv(j - 1).advance(2)
+
+    @pl.when(j == 1)
+    def _():
+        value = gate.finish()
+        gate_ref[0] = value[:share]
+        gate_ref[1] = value[share:]
+
+    def token_grad(rows):
+        return (
+            total[rows, :]
+            + dot_nt(d_query[rows, columns], wq_ref[...])
             + dot_nt(d_keys[rows, :], wk_ref[...])
             + dot_nt(d_values[rows, :], wv_ref[...])
         )
 
-    @pl.when(j == pl.num_programs(0) - 1)
-    def _():
-        gain_sum = jnp.zeros((1, width), F32)
+    def key_value_grads():
+        grad[...] = dot_tn(a_one_ref[...], d_keys[...])
+        share_all(grad, kv_send, kv_keep, slice(0, share), share)
+        grad[...] = dot_tn(a_one_ref[...], d_values[...])
+        share_all(grad, kv_send, kv_keep, slice(share, 2 * share), share)
+        share_all(d_kern, kv_send, kv_keep, slice(2 * share, 2 * share + kern_share), kern_share)
+        kv(j).begin()
+
+    @pl.when(j < tiles - 1)
+    def _():
+        key_value_grads()
         for b in range(blocks):
             rows = slice(b * BLOCK, (b + 1) * BLOCK)
-            normed, inv = norm_stats(x_ref[rows, :].astype(F32))
-            grad_in = total[rows, :]
-            gain_sum = gain_sum + jnp.sum(grad_in * normed, axis=0, keepdims=True)
-            d_x_ref[rows, :] = (d_hidden_ref[rows, :] + norm_pull(grad_in, normed, inv, gain_ref[...])).astype(BF16)
+            total[rows, :] = token_grad(rows)
+
+    @pl.when(jnp.logical_and(j >= 1, j < tiles))
+    def _():
+        kv(j - 1).advance(3)
+
+    @pl.when(j == tiles - 1)
+    def _():
+        def norm_rows(place, low, gain_sum):
+            for b in range(half // BLOCK):
+                rows = pl.ds(pl.multiple_of(low + b * BLOCK, BLOCK), BLOCK)
+                normed, inv = norm_stats(x_ref[rows, :].astype(F32))
+                grad_in = token_grad(rows)
+                gain_sum = gain_sum + jnp.sum(grad_in * normed, axis=0, keepdims=True)
+                pulled = d_hidden_ref[rows, :] + norm_pull(grad_in, normed, inv, gain_ref[...])
+                d_x[place, b * BLOCK : (b + 1) * BLOCK, :] = pulled.astype(BF16)
+            return gain_sum
+
+        key_value_grads()
+        gain_sum = norm_rows(0, (1 - side) * half, jnp.zeros((1, width), F32))
+        send_row().start()
+        kv(2).advance(0)
+        gain_sum = norm_rows(1, side * half, gain_sum)
+        keep_row().start()
         gain_grad_ref[...] = gain_sum
+        kv(2).advance(1)
+        kv_finish(1)
+        kv(2).advance(2)
+        kv(2).advance(3)
+        kv_finish(2)
+        keep_row().wait()
+        send_row().wait()
 
 
 def mixer_back_call(
-    live, place, d_state, d_query, mixed, shifted, k, v, a_one, wq, wk, wv, kern, tapspec, tables, x, gain, d_hidden,
-    taps_count, tile
+    live, out_row, d_mixer, wout, state, q, gated, a_one, mixed, shifted, k, v, wq, wk, wv, kern, tapspec, tables,
+    x, gain, d_hidden, ffn_sums, taps_count, tile,
 ):
     length, width = a_one.shape
     blocks = length // BLOCK
+    half = length // 2
     table, back = tables
     share = width // 16
-    whole = lambda j, n, p: (0, 0)
-    column = lambda j, n, p: (0, j)
-    rows_full = pl.BlockSpec((length, width), whole)
+    part_rows = 2 * share + length // 16
+    count = width // tile
+    column = lambda j: (0, j)
+    rows_full = once((length, width))
     rows_tile = pl.BlockSpec((length, tile), column)
     weight = pl.BlockSpec((width, tile), column)
-    half_spec = pl.BlockSpec((2, 2, 2, 2, share, tile), lambda j, n, p: (0, 0, 0, 0, 0, j))
-    half_shape = jax.ShapeDtypeStruct((2, 2, 2, 2, share, width), BF16)
-    kern_spec = pl.BlockSpec((2, 2, 2, 1, length // 16, tile), lambda j, n, p: (0, 0, 0, 0, 0, j))
-    kern_shape = jax.ShapeDtypeStruct((2, 2, 2, 1, length // 16, width), BF16)
-    spectrum = pltpu.VMEM((blocks, 2 * BLOCK, tile), F32)
-    spectrum_low = pltpu.VMEM((blocks, 2 * BLOCK, tile), BF16)
+    anywhere = pl.BlockSpec(memory_space=pl.ANY)
+    low = lambda *shape: jax.ShapeDtypeStruct(shape, BF16)
+    full = lambda *shape: jax.ShapeDtypeStruct(shape, F32)
+    vmem = lambda *shape: pltpu.VMEM(shape, BF16)
+    wide = lambda *shape: pltpu.VMEM(shape, F32)
+    sems = lambda *shape: pltpu.SemaphoreType.DMA(shape)
+    up_two, up_three, down_two, down_three, up_part, down_part = ffn_sums
+    su, sd = up_two.shape[2], down_two.shape[0]
+    out_shape = [
+        low(2, half, width),
+        low(2, half, width),
+        full(1, width),
+        full(taps_count, width),
+        full(su, 4 * width),
+        full(sd, width),
+        full(2, share, width),
+        full(2, share, width),
+        full(length // 16, width),
+    ]
     return pl.pallas_call(
         mixer_back_body,
-        grid_spec=pltpu.PrefetchScalarGridSpec(
-            num_scalar_prefetch=2,
-            grid=(width // tile,),
-            in_specs=[rows_tile] * 6
-            + [rows_full, weight, weight, weight]
-            + [
-                pl.BlockSpec((blocks, 2 * BLOCK, tile), lambda j, n, p: (0, 0, j)),
-                pl.BlockSpec((2 * BLOCK, tile), column),
-                pl.BlockSpec(table.shape, whole),
-                pl.BlockSpec(back.shape, whole),
-                rows_full,
-                pl.BlockSpec((1, width), whole),
-                rows_full,
-            ],
-            out_specs=[
-                rows_full,
-                pl.BlockSpec((1, width), whole),
-                pl.BlockSpec((taps_count, tile), column),
-                half_spec,
-                half_spec,
-                kern_spec,
-                kern_spec,
-            ],
-            scratch_shapes=[
-                pltpu.VMEM((length, width), F32),
-                spectrum,
-                spectrum,
-                spectrum_low,
-                spectrum_low,
-                pltpu.VMEM((length, tile), BF16),
-                pltpu.VMEM((length, tile), BF16),
-                pltpu.VMEM((width, tile), F32),
-                pltpu.VMEM((length, tile), F32),
-            ],
+        grid=(count,),
+        in_specs=[pl.BlockSpec(memory_space=pltpu.SMEM), anywhere, rows_full, once(wout.shape)]
+        + [rows_full] * 4
+        + [rows_tile] * 4
+        + [weight] * 3
+        + [
+            pl.BlockSpec((blocks, 2 * BLOCK, tile), lambda j: (0, 0, j)),
+            pl.BlockSpec((2 * BLOCK, tile), column),
+            once(table.shape),
+            once(back.shape),
+            rows_full,
+            once((1, width)),
+            rows_full,
+        ]
+        + [once(s.shape) for s in ffn_sums],
+        out_specs=[anywhere, anywhere] + [once(s.shape) for s in out_shape[2:]],
+        out_shape=out_shape,
+        scratch_shapes=[
+            wide(length, width),
+            wide(blocks, 2 * BLOCK, tile),
+            wide(blocks, 2 * BLOCK, tile),
+            vmem(blocks, 2 * BLOCK, tile),
+            vmem(blocks, 2 * BLOCK, tile),
+            vmem(length, tile),
+            vmem(length, tile),
+            vmem(length, width),
+            vmem(count, length, tile),
+            wide(width, tile),
+            wide(length, tile),
+            vmem(2, half, width),
+            vmem(16, LANES),
+            vmem(2, su, width),
+            vmem(su, width),
+            vmem(su, width),
+            vmem(2, 2, su, width),
+            vmem(2, su, width),
+            vmem(su, width),
+            vmem(su, width),
+            sems(2, 5, 2),
+            vmem(4, sd, width),
+            vmem(4, sd, width),
+            sems(2, 4, 2),
+            vmem(2, 2, 2, 2 * share, width),
+            vmem(2, 2, 2, 2 * share, width),
+            vmem(2, 2, 2, 2 * share, width),
+            vmem(2, 2, 2 * share, width),
+            vmem(2, 2 * share, width),
+            vmem(2 * share, width),
+            vmem(2 * share, width),
+            sems(5, 2),
+            vmem(2, 2, 2, part_rows, tile),
+            vmem(2, 2, 2, part_rows, tile),
+            vmem(count, 2, 2, 2, part_rows, tile),
+            vmem(count, 2, 2, part_rows, tile),
+            vmem(count, 2, part_rows, tile),
+            vmem(count, part_rows, tile),
+            vmem(count, part_rows, tile),
+            sems(count, 5, 2),
+            sems(2),
+            sems(2),
+            sems(2),
+        ],
+        compiler_params=pltpu.CompilerParams(
+            vmem_limit_bytes=62 * 1024 * 1024, collective_id=2, has_side_effects=True
         ),
-        out_shape=[
-            jax.ShapeDtypeStruct((length, width), BF16),
-            jax.ShapeDtypeStruct((1, width), F32),
-            jax.ShapeDtypeStruct((taps_count, width), F32),
-            half_shape,
-            half_shape,
-            kern_shape,
-            kern_shape,
-        ],
-        compiler_params=params(),
-        cost_estimate=cost(16e9, 40e6),
+        cost_estimate=cost(26e9, 40e6),
         name="mixer_back",
     )(
-        live, place, d_state, d_query, mixed, shifted, k, v, a_one, wq, wk, wv, kern, tapspec, table, back, x, gain,
-        d_hidden,
+        live, out_row, d_mixer, wout, state, q, gated, a_one, mixed, shifted, k, v, wq, wk, wv, kern, tapspec,
+        table, back, x, gain, d_hidden, up_two, up_three, down_two, down_three, up_part, down_part,
     )
 
 
@@ -1030,42 +1350,9 @@
     )
 
 
-def add_low(a, b):
-    return (a.astype(F32) + b.astype(F32)).astype(BF16)
-
-
 def swap(value, axis_name, bit):
     count = lax.axis_size(axis_name)
     return lax.ppermute(value, axis_name, [(i, i ^ bit) for i in range(count)])
-
-
-def halve(value, axis, bit):
-    index = [slice(None)] * value.ndim
-    index[axis] = 1
-    given = swap(value[tuple(index)], "dp", bit)
-    index[axis] = 0
-    return add_low(value[tuple(index)], given)
-
-
-def reduce_shares(send, keep, cut):
-    joined = add_low(keep, swap(send, "dp", 1))
-    axis, low = cut
-    cuts = [slice(None)] * joined.ndim
-    results = []
-    for first in (True, False):
-        cuts[axis] = slice(0, low) if first else slice(low, None)
-        part = joined[tuple(cuts)]
-        if first:
-            part = halve(part, 0, 2)
-            part = halve(part, 0, 4)
-            part = halve(part, 0, 8)
-        else:
-            part = halve(part, 1, 4)
-            part = halve(part, 1, 8)
-            part = halve(part, 0, 2)
-        part = part.astype(F32) + swap(part, "seq", 1).astype(F32)
-        results.append(part)
-    return jnp.concatenate(results, axis=axis - 3)
 
 
 def reduce_small(value, place):
@@ -1089,14 +1376,6 @@
     own = lax.dynamic_index_in_dim(rows, side, 0, keepdims=False)
     other = lax.dynamic_index_in_dim(rows, 1 - side, 0, keepdims=False)
     return whole_row(own, swap(other, "seq", 1), side)
-
-
-def return_rows(row, side):
-    half = row.shape[0] // 2
-    own = lax.dynamic_slice_in_dim(row, side * half, half, 0)
-    other = lax.dynamic_slice_in_dim(row, (1 - side) * half, half, 0)
-    given = swap(other, "seq", 1)
-    return jnp.where(side == 0, jnp.stack([own, given]), jnp.stack([given, own]))
 
 
 def split_rows(
@@ -1111,7 +1390,6 @@
     channels, states = diag_coef.shape
     tile = 256
     tables = transform_tables()
-    place = jnp.reshape(mine, (1,)).astype(jnp.int32)
     live = lax.dynamic_slice_in_dim(lengths, side, 1, 0)
     x = exchange_rows(tokens, side)
     packed = jnp.stack([diag_coef.T, diag_rate.T, shift_taps.T])
@@ -1129,23 +1407,13 @@
     a_one, q, k, v, shifted, mixed, state, gated, hidden, a_two = mixer_call(
         live, x, row_one, w_query, w_key, w_value, w_out, row_two, kern, tapspec, tables, tile
     )
-    out_row, d_pre, down_send, down_keep = ffn_call(live, place, a_two, cot, hidden, w_up, w_down)
-    out = return_rows(out_row, side)
-    share = w_down.shape[0] // devices
-    down = reduce_shares(down_send[:, :, :, None], down_keep[:, :, :, None], (4, 112))
-    d_hidden, d_mixer, d_gain_two, up_send, up_keep = ffn_back_call(
-        live, place, a_two, d_pre, w_up, cot, hidden, row_two
-    )
-    up = reduce_shares(up_send, up_keep, (3, 2))
-    d_query, d_state, gate_send, gate_keep = gate_back_call(place, d_mixer, w_out, state, q, gated, a_one)
-    gate = reduce_shares(gate_send, gate_keep, (3, 1))
-    d_row, d_gain_one, d_taps, kv_send, kv_keep, kern_send, kern_keep = mixer_back_call(
-        live, place, d_state, d_query, mixed, shifted, k, v, a_one, w_query, w_key, w_value, kern, tapspec, tables,
-        x, row_one, d_hidden, states, tile,
-    )
-    d_tokens = return_rows(d_row, side)
-    d_kern = reduce_shares(kern_send, kern_keep, (4, 32))[0]
-    kv = reduce_shares(kv_send, kv_keep, (3, 1))
+    out_row, d_hidden, d_mixer, d_gain_two, up_part, down_part, *parts = ffn_call(
+        live, a_two, cot, hidden, row_two, w_up, w_down
+    )
+    out, d_tokens, d_gain_one, d_taps, up, down, gate, kv, d_kern = mixer_back_call(
+        live, out_row, d_mixer, w_out, state, q, gated, a_one, mixed, shifted, k, v, w_query, w_key, w_value, kern,
+        tapspec, tables, x, row_one, d_hidden, (*parts, up_part, down_part), states, tile,
+    )
 
     d_kern_half = lax.dynamic_slice_in_dim(d_kern, side * channels, channels, 1)
     steps = (mine * d_kern.shape[0] + lax.iota(jnp.int32, d_kern.shape[0])).astype(F32)
@@ -1165,7 +1433,6 @@
     small = reduce_small(small, mine)
     small = small + swap(small, "seq", 1)
     taps_part = lax.dynamic_slice_in_dim(small[:each], side * channels, channels, 1)
-    up_share = jnp.transpose(up, (1, 0, 2)).reshape(up.shape[1], -1)
     return (
         out,
         d_tokens,
@@ -1175,8 +1442,8 @@
         kv[1],
         gate[0],
         small[each, gain_each : 2 * gain_each],
-        up_share,
-        down.reshape(share, width),
+        up,
+        down,
         taps_part.T,
         pair[:each].T,
         pair[each:].T,

time: 430 us -> 360 us (0.84); the launches traced: 423 us -> 358 us
  Pallas kernels: 160 us -> 281 us
  waiting for transfers between devices: 143 us -> 35.6 us
  starting transfers between devices: 71.3 us -> 15.5 us
  other arithmetic: 31.3 us -> 10.1 us
    pallas_call x4 -> x2, Pallas kernels: 105 us -> 226 us  [the longest x1 138 us: mixer_back_call(): pl.pallas_call(mixer_back_body, grid=(count,), in_specs=[pl.BlockSpec(mem...]
    ppermute x59 -> x12, waiting for transfers between devices: 143 us -> 35.6 us  [swap(): return lax.ppermute(value, axis_name, [(i, i ^ bit) for i in range(count)])]
    ppermute x59 -> x12, starting transfers between devices: 71.3 us -> 15.5 us  [swap(): return lax.ppermute(value, axis_name, [(i, i ^ bit) for i in range(count)])]
    convert_element_type x32 -> x0, other arithmetic: 7.99 us -> none  [add_low(): return (a.astype(F32) + b.astype(F32)).astype(BF16)]
    unnamed x32 -> x36, local copies, waits for them, and re-layouts: 0.25 us -> 5.1 us
  transfers between devices with their start and end apart: 59 -> 12, of which waited for: 36 -> 8; matrix products, arithmetic and copies ran while one was open for 9% -> 3% of each run, Pallas kernels for 13% -> 15%
where the time goes in v2:
time: 360 us; the launch traced here: 358 us
  Pallas kernels  281 us (78%)
  waiting for transfers between devices  35.6 us (10%)
  starting transfers between devices  15.5 us (4%)
  local copies, waits for them, and re-layouts  14.4 us (4%)
  other arithmetic  10.1 us (3%)
    pallas_call x1, Pallas kernels, mixer_back_call(): pl.pallas_call(mixer_back_body, grid=(count,), in_specs=[pl.BlockSpec(mem...  138 us
    pallas_call x1, Pallas kernels, ffn_call(): pl.pallas_call(ffn_body, grid=(4,), in_specs=[pl.BlockSpec(memory_space=p...  87.3 us
    ppermute x12, waiting for transfers between devices, swap(): return lax.ppermute(value, axis_name, [(i, i ^ bit) for i in range(count)])  35.6 us
    pallas_call x1, Pallas kernels, mixer_call(): pl.pallas_call(mixer_body, grid_spec=pltpu.PrefetchScalarGridSpec(num_sca...  28.4 us
    pallas_call x1, Pallas kernels, spectra_call(): pl.pallas_call(spectra_body, grid=(channels // tile,), in_specs=[pl.Block...  27 us
    ppermute x12, starting transfers between devices, swap(): return lax.ppermute(value, axis_name, [(i, i ^ bit) for i in range(count)])  15.5 us
  transfers between devices with their start and end apart: 12, of which 8 were waited for; matrix products, arithmetic and copies ran while one was open for 3% of the time, Pallas kernels for 15%

profile of v2, /device:TPU:0, one launch (start us, length us, event | category | flops | bytes accessed | tf_op | source)
XLA Modules:
  0.0 358.1 jit_solution(16539108613161073498)
XLA Ops:
  0.7 0.0 copy-start.3
  0.7 0.0 copy-start.4
  0.7 0.0 copy-start.7
  0.7 0.0 copy-start
  0.7 1.6 dynamic-slice_bitcast_fusion.3
  2.3 3.0 collective-permute-start
  5.3 0.0 copy-done.4
  5.3 0.7 pad_maximum_fusion.1
  6.1 0.0 collective-permute-start.1
  6.1 0.1 dynamic-slice_bitcast_fusion.1
  6.2 2.1 collective-permute-start.2
  8.3 0.6 dynamic_slice.22.length_ref
  8.9 0.6 broadcast_in_dim.30.gain_one_ref.gain_ref
  9.5 0.6 broadcast_in_dim.31.gain_two_ref.gain_ref
  10.1 20.0 %collective-permute-done.1 = f32[3,64,384]{2,1,0:T(8,128)} collective-permute-done((f32[3,64,384]{2,1,0:T(8,128)}, f32[3,64,384]{2,1,0:T(8,128)}, u32[]{:S(2)}, u32[]{:S(2)}) %collective-permute-start.1) | collective-permute-done | bytes 294944 | tf_op jit(solution)/shard_map/ppermute | solution.py:1355
  30.1 1.1 maximum_select_fusion.2
  31.2 0.8 slice_bitcast_fusion
  32.1 27.0 %spectra.1 = (bf16[4,512,768]{2,1,0:T(8,128)(2,1)}, f32[512,768]{1,0:T(8,128)}) custom-call(f32[64,768]{1,0:T(8,128)} %get-tuple-element.83.coef_ref, f32[64,768]{1,0:T(8,128)} %get-tuple-element.82.rate_ref, f32[64,768]{1,0:T(8,128)} %get-tuple-element.81.taps_ref, bf16[512,256]{1,0:T(8,128)(2,1)} %constant.66.clone.table_ref), custom_call_target="tpu_custom_call" | custom-call | flops 6000000000 | bytes 20000000 | tf_op jit(solution)/shard_map/spectra/pallas_call | solution.py:150
  59.1 0.0 collective-permute-done
  59.1 3.1 maximum_select_fusion.x_ref
  62.2 28.4 %mixer_forward.1 = (bf16[1024,768]{1,0:T(8,128)(2,1)}, bf16[1024,768]{1,0:T(8,128)(2,1)}, bf16[1024,768]{1,0:T(8,128)(2,1)}, bf16[1024,768]{1,0:T(8,128)(2,1)}, ...) custom-call(s32[1]{0:T(128)} %dynamic_slice.22.length_ref, ...), custom_call_target="tpu_custom_call" | custom-call | flops 10000000000 | bytes 30000000 | tf_op jit(solution)/shard_map/mixer_forward/pallas_call | solution.py:272
  90.6 0.0 collective-permute-done.2
  90.6 3.1 maximum_select_fusion.1.cot_ref
  93.7 87.3 %feed_forward.1 = (bf16[1024,768]{1,0:T(8,128)(2,1)}, f32[1024,768]{1,0:T(8,128)}, bf16[1024,768]{1,0:T(8,128)(2,1)}, f32[1,768]{1,0:T(1,128)}, f32[2,48,768]{2,...) custom-call(s32[1]{0:T(128)} %dynamic_slice.22.length_ref, ...), custom_call_target="tpu_custom_call" | custom-call | flops 28991029248 | bytes 40000000 | tf_op jit(solution)/shard_map/feed_forward/pallas_call | solution.py:622
  181.0 138.5 %mixer_back.1 = (bf16[2,512,768]{2,1,0:T(8,128)(2,1)}, bf16[2,512,768]{2,1,0:T(8,128)(2,1)}, f32[1,768]{1,0:T(1,128)}, f32[64,768]{1,0:T(8,128)}, f32[48,3072]{1...) custom-call(s32[1]{0:T(128)} %dynamic_slice.22.length_ref, ...), custom_call_target="tpu_custom_call" | custom-call | flops 25999998976 | bytes 40000000 | tf_op jit(solution)/shard_map/mixer_back/pallas_call | solution.py:975
  319.5 0.9 constant_dynamic-slice_fusion
  320.4 1.6 fusion
  322.1 0.6 gather_fusion.1
  322.7 0.1 broadcast_select_fusion.1
  322.8 0.1 collective-permute-start.8
  322.9 0.1 reshape.73
  323.0 0.1 reshape.74
  323.1 0.1 reshape.72
  323.2 0.1 fusion.2
  323.3 0.1 pad_maximum_fusion
  323.4 0.6 gather_fusion
  323.9 0.1 broadcast_select_fusion
  324.1 3.0 collective-permute-start.3
  327.0 0.8 slice_bitcast_fusion.3
  327.9 5.9 %collective-permute-done.8 = f32[8,8,384]{2,1,0:T(8,128)S(1)} collective-permute-done((f32[8,8,384]{2,1,0:T(8,128)S(1)}, f32[8,8,384]{2,1,0:T(8,128)S(1)}, u32[]{:S(2)}, u32[]{:S(2)}) %collective-permute-start.8) | collective-permute-done | bytes 98336 | tf_op jit(solution)/shard_map/ppermute | solution.py:1355
  333.8 0.1 collective-permute-start.9
  333.9 3.3 collective-permute-done.3
  337.2 0.1 collective-permute-start.4
  337.3 0.6 collective-permute-done.9
  338.0 2.5 collective-permute-start.10
  340.5 1.4 collective-permute-done.4
  341.9 2.4 collective-permute-start.5
  344.4 0.0 collective-permute-done.10
  344.4 0.1 collective-permute-start.11
  344.5 2.0 collective-permute-done.5
  346.5 0.1 collective-permute-start.6
  346.5 0.0 collective-permute-done.11
  346.6 1.2 collective-permute-done.6
  347.7 2.1 collective-permute-start.7
  349.8 0.6 slice_bitcast_fusion.7
  350.4 1.2 collective-permute-done.7
  351.6 0.6 slice_bitcast_fusion.9
  352.2 0.6 dynamic-slice_bitcast_fusion.4
  352.8 1.1 copy.37
  353.9 0.8 copy-done.1
  354.8 1.1 copy.38
  355.9 0.3 copy-done.6
  356.2 0.8 copy.39
  357.0 0.8 copy.40
  (54 shorter events, 0.4 us)
Async XLA Ops:
  0.7 4.7 %copy-start.3 = (f32[384,64]{0,1:T(8,128)S(1)}, f32[384,64]{0,1:T(8,128)}, u32[]{:S(2)}) copy-start(f32[384,64]{0,1:T(8,128)} %param.28) | copy-start | bytes 294916
  0.7 4.7 %copy-start.4 = (f32[384,64]{0,1:T(8,128)S(1)}, f32[384,64]{0,1:T(8,128)}, u32[]{:S(2)}) copy-start(f32[384,64]{0,1:T(8,128)} %param.27) | copy-start | bytes 294916
  0.7 4.7 %copy-start.7 = (f32[384,64]{0,1:T(8,128)S(1)}, f32[384,64]{0,1:T(8,128)}, u32[]{:S(2)}) copy-start(f32[384,64]{0,1:T(8,128)} %param.26) | copy-start | bytes 294916
  0.7 5.4 %copy-start = (bf16[2,512,768]{2,1,0:T(8,128)(2,1)S(1)}, bf16[2,512,768]{2,1,0:T(8,128)(2,1)}, u32[]{:S(2)}) copy-start(bf16[2,512,768]{2,1,0:T(8,128)(2,1)} %param.29) | copy-start | bytes 4718596
  2.3 56.8 %collective-permute-start = (bf16[512,768]{1,0:T(8,128)(2,1)S(1)}, bf16[512,768]{1,0:T(8,128)(2,1)}, u32[]{:S(2)}, u32[]{:S(2)}) collective-permute-start(bf16[512,768]{1,0:T(8,128)(2,1)S(1)} %get-tuple-element.80), channel_id=1, source_target_pairs={{0,1},{1,0},{2,3},{3,2},{4,5},{5,4},{6,7},{7,6},{8,9},{9,8},{10,11... | collective-permute-start | bytes 2359304 | tf_op jit(solution)/shard_map/ppermute | solution.py:1355
  6.1 2.2 copy-start.15
  6.1 2.8 copy-start.11
  6.1 3.4 copy-start.12
  6.1 24.0 %collective-permute-start.1 = (f32[3,64,384]{2,1,0:T(8,128)}, f32[3,64,384]{2,1,0:T(8,128)}, u32[]{:S(2)}, u32[]{:S(2)}) collective-permute-start(f32[3,64,384]{2,1,0:T(8,128)} %pad_maximum_fusion.1), channel_id=1, source_target_pairs={{0,1},{1,0},{2,3},{3,2},{4,5},{5,4},{6,7},{7,6},{8,9},{9,8},{10,11... | collective-permute-start | bytes 884744 | tf_op jit(solution)/shard_map/ppermute | solution.py:1355
  6.2 84.4 %collective-permute-start.2 = (bf16[512,768]{1,0:T(8,128)(2,1)S(1)}, bf16[512,768]{1,0:T(8,128)(2,1)}, u32[]{:S(2)}, u32[]{:S(2)}) collective-permute-start(bf16[512,768]{1,0:T(8,128)(2,1)S(1)} %get-tuple-element.78), channel_id=1, source_target_pairs={{0,1},{1,0},{2,3},{3,2},{4,5},{5,4},{6,7},{7,6},{8,9},{9,8},{10,11... | collective-permute-start | bytes 2359304 | tf_op jit(solution)/shard_map/ppermute | solution.py:1355
  322.0 1.0 copy-start.14
  322.0 1.1 copy-start.13
  322.0 1.1 copy-start.10
  322.8 4.2 %copy-start.8 = (f32[2,48,768]{2,1,0:T(8,128)S(1)}, f32[2,48,768]{2,1,0:T(8,128)}, u32[]{:S(2)}) copy-start(f32[2,48,768]{2,1,0:T(8,128)} %get-tuple-element.70) | copy-start | bytes 884740
  322.8 4.2 %copy-start.9 = (f32[2,48,768]{2,1,0:T(8,128)S(1)}, f32[2,48,768]{2,1,0:T(8,128)}, u32[]{:S(2)}) copy-start(f32[2,48,768]{2,1,0:T(8,128)} %get-tuple-element.71) | copy-start | bytes 884740
  322.8 10.9 %collective-permute-start.8 = (f32[8,8,384]{2,1,0:T(8,128)S(1)}, f32[8,8,384]{2,1,0:T(8,128)S(1)}, u32[]{:S(2)}, u32[]{:S(2)}) collective-permute-start(f32[8,8,384]{2,1,0:T(8,128)S(1)} %slice.139), channel_id=1, source_target_pairs={{0,16},{2,18},{4,20},{6,22},{8,24},{10,26},{12,28},{14,30},{16,0},... | collective-permute-start | bytes 294920 | tf_op jit(solution)/shard_map/ppermute | solution.py:1355
  324.1 13.1 %collective-permute-start.3 = (f32[8,5,768]{2,1,0:T(8,128)S(1)}, f32[8,5,768]{2,1,0:T(8,128)S(1)}, u32[]{:S(2)}, u32[]{:S(2)}) collective-permute-start(f32[8,5,768]{2,1,0:T(8,128)S(1)} %slice.128), channel_id=1, source_target_pairs={{0,16},{2,18},{4,20},{6,22},{8,24},{10,26},{12,28},{14,30},{16,0},... | collective-permute-start | bytes 368648 | tf_op jit(solution)/shard_map/ppermute | solution.py:1355
  327.0 25.8 %copy-start.2 = (bf16[2,512,768]{2,1,0:T(8,128)(2,1)S(1)}, bf16[2,512,768]{2,1,0:T(8,128)(2,1)}, u32[]{:S(2)}) copy-start(bf16[2,512,768]{2,1,0:T(8,128)(2,1)} %get-tuple-element.107) | copy-start | bytes 4718596
  333.8 4.2 %collective-permute-start.9 = (f32[4,8,384]{2,1,0:T(8,128)S(1)}, f32[4,8,384]{2,1,0:T(8,128)S(1)}, u32[]{:S(2)}, u32[]{:S(2)}) collective-permute-start(f32[4,8,384]{2,1,0:T(8,128)S(1)} %slice.141), channel_id=1, source_target_pairs={{0,8},{2,10},{4,12},{6,14},{8,0},{10,2},{12,4},{14,6},{16,24},{18,... | collective-permute-start | bytes 147464 | tf_op jit(solution)/shard_map/ppermute | solution.py:1355
  337.2 4.7 %collective-permute-start.4 = (f32[4,5,768]{2,1,0:T(8,128)S(1)}, f32[4,5,768]{2,1,0:T(8,128)S(1)}, u32[]{:S(2)}, u32[]{:S(2)}) collective-permute-start(f32[4,5,768]{2,1,0:T(8,128)S(1)} %slice.130), channel_id=1, source_target_pairs={{0,8},{2,10},{4,12},{6,14},{8,0},{10,2},{12,4},{14,6},{16,24},{18,... | collective-permute-start | bytes 184328 | tf_op jit(solution)/shard_map/ppermute | solution.py:1355
  338.0 6.4 %collective-permute-start.10 = (f32[2,8,384]{2,1,0:T(8,128)S(1)}, f32[2,8,384]{2,1,0:T(8,128)S(1)}, u32[]{:S(2)}, u32[]{:S(2)}) collective-permute-start(f32[2,8,384]{2,1,0:T(8,128)S(1)} %slice.143), channel_id=1, source_target_pairs={{0,4},{2,6},{4,0},{6,2},{8,12},{10,14},{12,8},{14,10},{16,20},{18,... | collective-permute-start | bytes 73736 | tf_op jit(solution)/shard_map/ppermute | solution.py:1355
  341.9 4.5 %collective-permute-start.5 = (f32[2,5,768]{2,1,0:T(8,128)S(1)}, f32[2,5,768]{2,1,0:T(8,128)S(1)}, u32[]{:S(2)}, u32[]{:S(2)}) collective-permute-start(f32[2,5,768]{2,1,0:T(8,128)S(1)} %slice.132), channel_id=1, source_target_pairs={{0,4},{2,6},{4,0},{6,2},{8,12},{10,14},{12,8},{14,10},{16,20},{18,... | collective-permute-start | bytes 92168 | tf_op jit(solution)/shard_map/ppermute | solution.py:1355
  344.4 2.1 collective-permute-start.11
  346.5 1.3 collective-permute-start.6
  347.7 3.9 %collective-permute-start.7 = (f32[5,768]{1,0:T(8,128)S(1)}, f32[5,768]{1,0:T(8,128)S(1)}, u32[]{:S(2)}, u32[]{:S(2)}) collective-permute-start(f32[5,768]{1,0:T(8,128)S(1)} %fusion.3), channel_id=1, source_target_pairs={{0,1},{1,0},{2,3},{3,2},{4,5},{5,4},{6,7},{7,6},{8,9},{9,8},{10,11... | collective-permute-start | bytes 46088 | tf_op jit(solution)/shard_map/ppermute | solution.py:1355
  352.8 2.0 copy-start.1
  354.8 1.4 copy-start.6
  354.8 2.3 copy-start.5

commit v3 on v0

--- a/solution.py
+++ b/solution.py
@@ -1,9 +1,1479 @@
+import functools
 import math
 
 import jax
 import jax.numpy as jnp
+import numpy as np
 from jax import lax
+from jax.experimental import pallas as pl
+from jax.experimental.pallas import tpu as pltpu
 from jax.sharding import PartitionSpec as P
+
+BLOCK = 256
+CHUNK = 16
+LANES = 128
+EPS = 1e-05
+F32 = jnp.float32
+BF16 = jnp.bfloat16
+VMEM_BYTES = 60 * 1024 * 1024
+
+
+def dot(a, b):
+    return lax.dot_general(a, b, (((1,), (0,)), ((), ())), preferred_element_type=F32)
+
+
+def dot_nt(a, b):
+    return lax.dot_general(a, b, (((1,), (1,)), ((), ())), preferred_element_type=F32)
+
+
+def dot_tn(a, b):
+    return lax.dot_general(a, b, (((0,), (0,)), ((), ())), preferred_element_type=F32)
+
+
+def params():
+    return pltpu.CompilerParams(vmem_limit_bytes=VMEM_BYTES)
+
+
+def cost(flops, byte_count):
+    return pl.CostEstimate(flops=int(flops), bytes_accessed=int(byte_count), transcendentals=0)
+
+
+def transform_tables():
+    freq = np.concatenate([np.arange(0, BLOCK, 2), np.arange(1, BLOCK, 2)]).astype(np.float64)
+    time = np.arange(BLOCK, dtype=np.float64)
+    angle = (2.0 * math.pi / (2 * BLOCK)) * (freq[:, None] + 0.5) * time[None, :]
+    table = np.concatenate([np.cos(angle), -np.sin(angle)], axis=0)
+    return jnp.asarray(table, dtype=BF16), jnp.asarray(table.T.copy(), dtype=BF16)
+
+
+def norm_stats(rows):
+    center = rows - jnp.mean(rows, axis=-1, keepdims=True)
+    spread = jnp.mean(center * center, axis=-1, keepdims=True)
+    inv = lax.rsqrt(spread + EPS)
+    return center * inv, inv
+
+
+def norm_pull(grad, normed, inv, gain):
+    scaled = grad * gain
+    mean_one = jnp.mean(scaled, axis=-1, keepdims=True)
+    mean_two = jnp.mean(scaled * normed, axis=-1, keepdims=True)
+    return (scaled - mean_one - normed * mean_two) * inv
+
+
+def live_rows(length, first, count):
+    rows = lax.broadcasted_iota(jnp.int32, (count, 1), 0) + first
+    return (rows < length).astype(F32)
+
+
+def spectral_loop(channels, body):
+    half = BLOCK // 2
+    for parity in range(2):
+        sign = 1.0 if parity == 0 else -1.0
+        for lane in range(channels // LANES):
+            lanes = slice(lane * LANES, (lane + 1) * LANES)
+
+            def step(index, carry, sign=sign, lanes=lanes, parity=parity):
+                low = pl.multiple_of(parity * half + index * CHUNK, CHUNK)
+                body(sign, pl.ds(low, CHUNK), pl.ds(low + BLOCK, CHUNK), lanes)
+                return carry
+
+            lax.fori_loop(0, half // CHUNK, step, 0)
+
+
+def multiply(ar, ai, br, bi):
+    return ar * br - ai * bi, ar * bi + ai * br
+
+
+def multiply_conj(ar, ai, br, bi):
+    return ar * br + ai * bi, ar * bi - ai * br
+
+
+def gelu_pair(x):
+    bell = jnp.exp(x * x * -0.5)
+    size = jnp.abs(x)
+    t = 1.0 / (1.0 + (0.3275911 / math.sqrt(2.0)) * size)
+    poly = t * (
+        0.5 * 0.254829592
+        + t * (0.5 * -0.284496736 + t * (0.5 * 1.421413741 + t * (0.5 * -1.453152027 + t * (0.5 * 1.061405429))))
+    )
+    tail = poly * bell
+    phi = jnp.where(x >= 0.0, 1.0 - tail, tail)
+    return x * phi, phi + x * bell * (1.0 / math.sqrt(2.0 * math.pi))
+
+
+def bit_of(index, bit):
+    return lax.rem(index // bit, 2)
+
+
+def partner(axis, bit):
+    index = lax.axis_index(axis)
+    return {axis: index + bit * (1 - 2 * bit_of(index, bit))}
+
+
+UP, DOWN, GATE, KERN, KEY, VALUE, KV, OUT, ROW, COEF, TAPS, GAIN = range(12)
+CORE, MIDDLE, NEAR, FAR, SIDE = ("dp", 1), ("dp", 2), ("dp", 4), ("dp", 8), ("seq", 1)
+
+
+def greet(partners):
+    barrier = pltpu.get_barrier_semaphore()
+    for axis, bit in partners:
+        pl.semaphore_signal(barrier, inc=1, device_id=partner(axis, bit), device_id_type=pl.DeviceIdType.MESH)
+    pl.semaphore_wait(barrier, len(partners))
+
+
+def transfer(source, target, sems, to):
+    return pltpu.make_async_remote_copy(
+        src_ref=source,
+        dst_ref=target,
+        send_sem=sems.at[0],
+        recv_sem=sems.at[1],
+        device_id=partner(*to),
+        device_id_type=pl.DeviceIdType.MESH,
+    )
+
+
+def add_into(target, other):
+    *lead, rows, _ = target.shape
+    for place in np.ndindex(*lead):
+        for low in range(0, rows, 48):
+            piece = (*place, slice(low, min(low + 48, rows)))
+            target[piece] = target[piece] + other[piece]
+
+
+def places(mine, owners, bits):
+    own = [bit_of(mine, bit) for bit in bits]
+    return [
+        tuple(1 - own[i] if (owner // bit) % 2 else own[i] for i, bit in enumerate(bits)) for owner in range(owners)
+    ]
+
+
+def spread(value, base, sideways=False):
+    value = value.astype(BF16)
+    share = value.shape[0] // 16
+    half = value.shape[1] // 2
+    side = lax.axis_index("seq")
+    for owner, (core, *place) in enumerate(places(lax.axis_index("dp"), 16, (1, 2, 4, 8))):
+        rows = value[owner * share : (owner + 1) * share]
+        if sideways:
+            base[(core, side, *place)] = rows[:, :half]
+            base[(core, 1 - side, *place)] = rows[:, half:]
+        else:
+            base[(core, *place)] = rows
+
+
+class Sum:
+    def __init__(self, refs, sems, order, final=None, across=True):
+        self.refs, self.sems, self.final = refs, sems, final
+        self.outer, self.sideways = order in "zZ", order in "XZ"
+        self.lead = 2 if self.sideways else 1
+        self.last = self.lead + 3
+        self.across = across
+
+    def part(self, step, half):
+        ref = self.refs[step]
+        if step == self.last:
+            return ref
+        if self.outer and self.lead <= step < self.lead + 2:
+            return ref.at[:, half]
+        return ref.at[half]
+
+    def copy(self, step):
+        order = (NEAR, FAR, MIDDLE) if self.outer else (MIDDLE, NEAR, FAR)
+        order = (CORE, *((SIDE,) if self.sideways else ()), *order, SIDE)
+        return transfer(self.part(step, 1), self.refs[step + 1], self.sems.at[step], order[step])
+
+    def start(self, step):
+        self.copy(step).start()
+
+    def wait(self, step):
+        self.copy(step).wait()
+        if step < self.last:
+            add_into(self.refs[step + 1], self.part(step, 0))
+            if step == self.last - 1 and not self.across:
+                self.final(self.refs[step + 1][...])
+        else:
+            self.final(self.refs[step][...], self.refs[step + 1][...], self.sideways)
+
+
+class Whole:
+    def __init__(self, refs, lands, sems):
+        self.refs, self.lands, self.sems = refs, lands, sems
+
+    def copy(self, step):
+        return transfer(self.refs.at[step], self.lands.at[step], self.sems.at[step], (CORE, MIDDLE, NEAR, FAR, SIDE)[step])
+
+    def start(self, step):
+        self.copy(step).start()
+
+    def wait(self, step):
+        self.copy(step).wait()
+        self.refs[step + 1] = self.refs[step] + self.lands[step]
+
+
+class Gather:
+    def __init__(self, z, refs, sems, sideways, final=None):
+        self.refs, self.sems, self.final, self.sideways = refs, sems, final, sideways
+        self.lead = 3 if sideways else 2
+        self.last = self.lead + 2
+        mine = lax.axis_index("dp")
+        near = bit_of(mine, 4) == z % 2
+        far = bit_of(mine, 8) == z // 2
+        both = jnp.logical_and(near, far)
+        self.gives = (jnp.logical_not(near), jnp.logical_and(near, jnp.logical_not(far)), both)
+        self.takes = (near, both, both)
+
+    def part(self, step, half):
+        return self.refs[step].at[half] if step < self.lead else self.refs[step]
+
+    def copy(self, step):
+        order = (CORE, *((SIDE,) if self.sideways else ()), MIDDLE, NEAR, FAR, SIDE)
+        return transfer(self.part(step, 1), self.refs[step + 1], self.sems.at[step], order[step])
+
+    def start(self, step):
+        if step < self.lead:
+            self.copy(step).start()
+        else:
+
+            @pl.when(self.gives[step - self.lead])
+            def _():
+                self.copy(step).start()
+
+    def wait(self, step):
+        if step < self.lead:
+            self.copy(step).wait()
+            add_into(self.refs[step + 1], self.part(step, 0))
+            return
+
+        @pl.when(self.gives[step - self.lead])
+        def _():
+            self.copy(step).wait_send()
+
+        @pl.when(self.takes[step - self.lead])
+        def _():
+            self.copy(step).wait_recv()
+            if step < self.last:
+                add_into(self.refs[step + 1], self.part(step, 0))
+            else:
+                self.final(self.refs[step][...], self.refs[step + 1][...], self.sideways)
+
+
+class Rows:
+    def __init__(self, source, target, sems):
+        self.copy = transfer(source, target, sems, SIDE)
+
+    def start(self, _):
+        self.copy.start()
+
+    def wait(self, _):
+        self.copy.wait()
+
+
+def follow(sums, events):
+    for name, index, exchange, begin in events:
+        if begin:
+            sums[name, index].start(exchange)
+        else:
+            sums[name, index].wait(exchange)
+
+
+def put(target, low, own, given, sideways):
+    if sideways:
+        side = lax.axis_index("seq")
+        half = own.shape[-1]
+        target[:, pl.ds(pl.multiple_of(low + side * half, LANES), half)] = own.astype(F32)
+        target[:, pl.ds(pl.multiple_of(low + (1 - side) * half, LANES), half)] = given.astype(F32)
+    else:
+        target[:, low : low + own.shape[-1]] = own.astype(F32) + given.astype(F32)
+
+
+def base_shape(rows, columns, order):
+    return (2, 2, 2, 2, 2, rows, columns // 2) if order in "XZ" else (2, 2, 2, 2, rows, columns)
+
+
+def landings(rows, columns, order):
+    *bits, rows, columns = base_shape(rows, columns, order)
+    return [pltpu.VMEM((*bits[n + 1 :], rows, columns), BF16) for n in range(len(bits))] + [pltpu.VMEM((rows, columns), BF16)]
+
+
+def gather_landings(rows, columns, sideways):
+    bits = (2, 2) if sideways else (2,)
+    columns = columns // 2 if sideways else columns
+    return [pltpu.VMEM((*bits[n:], rows, columns), BF16) for n in range(len(bits) + 1)] + [
+        pltpu.VMEM((rows, columns), BF16) for _ in range(3)
+    ]
+
+
+def once(shape):
+    zeros = (0,) * len(shape)
+    return pl.BlockSpec(shape, lambda *_: zeros, pipeline_mode=pl.Buffered(1))
+
+
+def mixer_body(
+    length_ref, tokens_hbm, cot_hbm, own_ref, taps_ref, gain_one_ref, gain_two_ref, wq_hbm, wk_hbm, wv_hbm, wout_hbm,
+    table_ref, back_ref,
+    x_hbm, cot_out, a_one_hbm, q_hbm, k_hbm, v_hbm, kern_hbm, tapspec_hbm, hidden_hbm, a_two_hbm,
+    shifted_ref, mixed_ref, state_ref,
+    x, a_one, q, k, v, total, a_two, wq, wk, wv, wout, kern, tapspec, taps, other, current, kern_time, near, far,
+    spec, prod, in_sems, own_sems, out_sems, token_sems, cot_sems, other_sems, taps_sems, unit_sems,
+):
+    j = pl.program_id(0)
+    steps = pl.num_programs(0)
+    length, width = x.shape
+    half = length // 2
+    tile = shifted_ref.shape[1]
+    blocks = length // BLOCK
+    states, channels = own_ref.shape[1:]
+    live = length_ref[0]
+    side = lax.axis_index("seq")
+    core = bit_of(lax.axis_index("dp"), 1)
+    own_rows = pl.ds(pl.multiple_of(side * half, half), half)
+
+    weights = [
+        pltpu.make_async_copy(source, target, in_sems.at[i])
+        for i, (source, target) in enumerate(((wq_hbm, wq), (wk_hbm, wk), (wv_hbm, wv), (wout_hbm, wout)))
+    ]
+    outs = [
+        pltpu.make_async_copy(source, target, out_sems.at[i])
+        for i, (source, target) in enumerate(
+            (
+                (x, x_hbm), (a_one, a_one_hbm), (q, q_hbm), (k, k_hbm), (v, v_hbm), (kern, kern_hbm),
+                (tapspec, tapspec_hbm), (total, hidden_hbm), (a_two, a_two_hbm),
+            )
+        )
+    ]
+    own_x = pltpu.make_async_copy(tokens_hbm.at[side], x.at[own_rows], own_sems.at[0])
+    own_cot = pltpu.make_async_copy(cot_hbm.at[side], cot_out.at[own_rows], own_sems.at[1])
+    other_x = transfer(tokens_hbm.at[1 - side], x.at[own_rows], token_sems, SIDE)
+    other_cot = transfer(cot_hbm.at[1 - side], cot_out.at[own_rows], cot_sems, SIDE)
+    wanted = pl.ds(pl.multiple_of(core * LANES, LANES), 2 * LANES)
+    other_params = transfer(own_ref.at[:, :, wanted], other, other_sems, SIDE)
+    own_lanes = pl.ds(pl.multiple_of(side * channels, LANES), channels)
+    other_taps = transfer(taps_ref, taps.at[:, own_lanes], taps_sems, SIDE)
+
+    def unit_columns(number, of_core):
+        tile_of = (2 * of_core, 1, 2 * of_core)[number]
+        half_of = (side, side + of_core - 2 * side * of_core, 1 - side)[number]
+        return pl.ds(pl.multiple_of(half_of * channels + tile_of * LANES, LANES), LANES)
+
+    def unit_copy(number):
+        columns = unit_columns(number, core)
+        return transfer(kern_time.at[:, columns], kern_time.at[:, columns], unit_sems.at[number], CORE)
+
+    def unit(number):
+        if number == 0:
+            for part in range(2):
+                current[part] = own_ref[part, :, pl.ds(pl.multiple_of(core * 2 * LANES, LANES), LANES)]
+        elif number == 1:
+
+            @pl.when(core == 0)
+            def _():
+                for part in range(2):
+                    current[part] = own_ref[part, :, LANES : 2 * LANES]
+
+            @pl.when(core == 1)
+            def _():
+                other_params.wait()
+                for part in range(2):
+                    current[part] = other[part, :, :LANES]
+
+        else:
+
+            @pl.when(core == 0)
+            def _():
+                other_params.wait()
+                for part in range(2):
+                    current[part] = other[part, :, :LANES]
+
+            @pl.when(core == 1)
+            def _():
+                for part in range(2):
+                    current[part] = other[part, :, LANES:]
+
+        columns = unit_columns(number, core)
+        step_count, together = 32, 8
+        groups = length // step_count
+        near_time = lax.broadcasted_iota(jnp.int32, (step_count, 1), 0).astype(F32)
+        far_time = lax.broadcasted_iota(jnp.int32, (groups, 1), 0).astype(F32) * step_count
+
+        def fill(n, carry):
+            rate = current[1, pl.ds(n, 1), :]
+            near[n] = jnp.exp(-rate * near_time)
+            far_n = current[0, pl.ds(n, 1), :] * jnp.exp(-rate * far_time)
+            for g in range(groups // together):
+                far[g, n] = far_n[g * together : (g + 1) * together, :]
+            return carry
+
+        lax.fori_loop(0, states, fill, 0)
+
+        def group(g, carry):
+            def add(n, sums):
+                near_n = near[n]
+                return tuple(sums[i] + far[g, n, i : i + 1, :] * near_n for i in range(together))
+
+            zeros = tuple(jnp.zeros((step_count, LANES), F32) for _ in range(together))
+            sums = lax.fori_loop(0, states, add, zeros, unroll=4)
+            for i in range(together):
+                place = pl.multiple_of((g * together + i) * step_count, step_count)
+                kern_time[pl.ds(place, step_count), columns] = sums[i].astype(BF16)
+            return carry
+
+        lax.fori_loop(0, groups // together, group, 0)
+        unit_copy(number).start()
+
+    def project_rows(low):
+        def block(b, carry):
+            rows = pl.ds(pl.multiple_of(low + b * BLOCK, BLOCK), BLOCK)
+            normed, _ = norm_stats(x[rows, :].astype(F32))
+            a_rows = (normed * gain_one_ref[...]).astype(BF16)
+            a_one[rows, :] = a_rows
+            mask = live_rows(live, low + b * BLOCK, BLOCK)
+            k[rows, :] = (dot(a_rows, wk[...]) * mask).astype(BF16)
+            v[rows, :] = (dot(a_rows, wv[...]) * mask).astype(BF16)
+            q[rows, :] = dot(a_rows, wq[...]).astype(BF16)
+            return carry
+
+        lax.fori_loop(0, half // BLOCK, block, 0)
+
+    @pl.when(j == 0)
+    def _():
+        own_x.start()
+        own_cot.start()
+        for copy in weights:
+            copy.start()
+        greet((CORE, SIDE))
+        other_params.start()
+        other_taps.start()
+        other_x.start()
+        taps[:, own_lanes] = taps_ref[...]
+        total[...] = jnp.zeros_like(total)
+        unit(0)
+        unit(1)
+        unit(2)
+        for copy in weights:
+            copy.wait()
+        own_x.wait()
+        project_rows(side * half)
+        other_taps.wait()
+        for number in range(3):
+            unit_copy(number).wait()
+
+        def tile_spectra(t, carry):
+            columns = pl.ds(pl.multiple_of(t * tile, tile), tile)
+            for b in range(blocks):
+                spec[b] = dot(table_ref[...], kern_time[b * BLOCK : (b + 1) * BLOCK, columns])
+
+            def combine(sign, re, im, lanes):
+                to = pl.ds(pl.multiple_of(t * tile + lanes.start, LANES), LANES)
+                for b in range(blocks):
+                    out_re = spec[b, re, lanes]
+                    out_im = spec[b, im, lanes]
+                    if b > 0:
+                        out_re = out_re - sign * spec[b - 1, im, lanes]
+                        out_im = out_im + sign * spec[b - 1, re, lanes]
+                    kern[b, re, to] = (out_re * (1.0 / BLOCK)).astype(BF16)
+                    kern[b, im, to] = (out_im * (1.0 / BLOCK)).astype(BF16)
+
+            spectral_loop(tile, combine)
+            tapspec[:, columns] = dot(table_ref[:, : taps.shape[0]], taps[:, columns]) * (1.0 / BLOCK)
+            return carry
+
+        lax.fori_loop(0, width // tile, tile_spectra, 0)
+        outs[5].start()
+        outs[6].start()
+        other_x.wait()
+        other_cot.start()
+        outs[0].start()
+        project_rows((1 - side) * half)
+        for copy in outs[1:5]:
+            copy.start()
+
+    @pl.when(j > 0)
+    def _():
+        t = j - 1
+        columns = pl.ds(pl.multiple_of(t * tile, tile), tile)
+        for b in range(blocks):
+            spec[b] = dot(table_ref[...], k[b * BLOCK : (b + 1) * BLOCK, columns])
+
+        def shift_product(sign, re, im, lanes):
+            at = pl.ds(pl.multiple_of(t * tile + lanes.start, LANES), LANES)
+            tr = tapspec[re, at]
+            ti = tapspec[im, at]
+            before = None
+            for b in range(blocks):
+                xr = spec[b, re, lanes]
+                xi = spec[b, im, lanes]
+                if b == 0:
+                    sr, si = xr, xi
+                else:
+                    sr, si = xr - sign * before[1], xi + sign * before[0]
+                before = (xr, xi)
+                yr, yi = multiply(sr, si, tr, ti)
+                prod[b, re, lanes] = yr.astype(BF16)
+                prod[b, im, lanes] = yi.astype(BF16)
+
+        spectral_loop(tile, shift_product)
+        for b in range(blocks):
+            rows = slice(b * BLOCK, (b + 1) * BLOCK)
+            shifted = dot(back_ref[...], prod[b])
+            shifted_ref[rows, :] = shifted.astype(BF16)
+            mixed_ref[rows, :] = (shifted * v[rows, columns].astype(F32)).astype(BF16)
+            spec[b] = dot(table_ref[...], mixed_ref[rows, :])
+
+        def state_product(sign, re, im, lanes):
+            at = pl.ds(pl.multiple_of(t * tile + lanes.start, LANES), LANES)
+            s = [(spec[b, re, lanes], spec[b, im, lanes]) for b in range(blocks)]
+            h = [(kern[b, re, at].astype(F32), kern[b, im, at].astype(F32)) for b in range(blocks)]
+            for i in range(blocks):
+                yr, yi = multiply(*s[i], *h[0])
+                for d in range(1, i + 1):
+                    pr, pi = multiply(*s[i - d], *h[d])
+                    yr, yi = yr + pr, yi + pi
+                prod[i, re, lanes] = yr.astype(BF16)
+                prod[i, im, lanes] = yi.astype(BF16)
+
+        spectral_loop(tile, state_product)
+        for b in range(blocks):
+            rows = slice(b * BLOCK, (b + 1) * BLOCK)
+            state = dot(back_ref[...], prod[b]).astype(BF16)
+            state_ref[rows, :] = state
+            gated = (q[rows, columns].astype(F32) * state.astype(F32)).astype(BF16)
+            total[rows, :] += dot(gated, wout[columns, :])
+
+    @pl.when(j == steps - 1)
+    def _():
+        def block(b, carry):
+            rows = pl.ds(pl.multiple_of(b * BLOCK, BLOCK), BLOCK)
+            mask = live_rows(live, b * BLOCK, BLOCK)
+            hidden = x[rows, :].astype(F32) + mask * total[rows, :]
+            total[rows, :] = hidden
+            normed, _ = norm_stats(hidden)
+            a_two[rows, :] = (normed * gain_two_ref[...]).astype(BF16)
+            return carry
+
+        lax.fori_loop(0, blocks, block, 0)
+        outs[7].start()
+        outs[8].start()
+        for copy in outs:
+            copy.wait()
+        own_cot.wait()
+        other_cot.wait()
+
+
+def mixer_call(live, tokens, cot, own, taps, gain_one, gain_two, wq, wk, wv, wout, tables, tile):
+    _, half, width = tokens.shape
+    length = 2 * half
+    blocks = length // BLOCK
+    table, back = tables
+    states, channels = taps.shape
+    anywhere = pl.BlockSpec(memory_space=pl.ANY)
+    rows_tile = pl.BlockSpec((length, tile), lambda j: (0, jnp.maximum(j - 1, 0)))
+    low = lambda *shape: jax.ShapeDtypeStruct(shape, BF16)
+    full = lambda *shape: jax.ShapeDtypeStruct(shape, F32)
+    vmem = lambda *shape: pltpu.VMEM(shape, BF16)
+    wide = lambda *shape: pltpu.VMEM(shape, F32)
+    sems = lambda *shape: pltpu.SemaphoreType.DMA(shape)
+    rows = low(length, width)
+    return pl.pallas_call(
+        mixer_body,
+        grid=(1 + width // tile,),
+        in_specs=[
+            pl.BlockSpec(memory_space=pltpu.SMEM),
+            anywhere,
+            anywhere,
+            once(own.shape),
+            once(taps.shape),
+            once((1, width)),
+            once((1, width)),
+            anywhere,
+            anywhere,
+            anywhere,
+            anywhere,
+            once(table.shape),
+            once(back.shape),
+        ],
+        out_specs=[anywhere] * 10 + [rows_tile] * 3,
+        out_shape=[
+            rows, rows, rows, rows, rows, rows,
+            low(blocks, 2 * BLOCK, width), full(2 * BLOCK, width), full(length, width), rows,
+            rows, rows, rows,
+        ],
+        scratch_shapes=[
+            vmem(length, width),
+            vmem(length, width),
+            vmem(length, width),
+            vmem(length, width),
+            vmem(length, width),
+            wide(length, width),
+            vmem(length, width),
+            vmem(*wq.shape),
+            vmem(*wk.shape),
+            vmem(*wv.shape),
+            vmem(*wout.shape),
+            vmem(blocks, 2 * BLOCK, width),
+            wide(2 * BLOCK, width),
+            vmem(states, width),
+            wide(2, states, 2 * LANES),
+            wide(2, states, LANES),
+            vmem(length, width),
+            wide(states, 32, LANES),
+            wide(length // 256, states, 8, LANES),
+            wide(blocks, 2 * BLOCK, tile),
+            vmem(blocks, 2 * BLOCK, tile),
+            sems(4),
+            sems(2),
+            sems(9),
+            sems(2),
+            sems(2),
+            sems(2),
+            sems(2),
+            sems(3, 2),
+        ],
+        compiler_params=pltpu.CompilerParams(vmem_limit_bytes=VMEM_BYTES, collective_id=3, has_side_effects=True),
+        cost_estimate=cost(16e9, 40e6),
+        name="mixer_forward",
+    )(live, tokens, cot, own, taps, gain_one, gain_two, wq, wk, wv, wout, table, back)
+
+
+ORDER = {UP: "zxxz", DOWN: "YYYY", GATE: "xx", KERN: "x", KV: "xX"}
+FEED_PLAN = {
+    (0, 4): ((DOWN, 0, 0, 1),),
+    (0, 5): ((UP, 0, 0, 1),),
+    (1, 1): ((DOWN, 0, 0, 0), (UP, 0, 0, 0), (DOWN, 0, 1, 1), (UP, 0, 1, 1)),
+    (1, 4): ((DOWN, 1, 0, 1),),
+    (1, 5): ((UP, 1, 0, 1),),
+    (2, 1): ((DOWN, 1, 0, 0), (DOWN, 0, 1, 0), (UP, 0, 1, 0), (UP, 1, 0, 0), (DOWN, 1, 1, 1), (UP, 1, 1, 1), (UP, 0, 2, 1)),
+    (2, 4): ((DOWN, 2, 0, 1),),
+    (2, 5): ((UP, 2, 0, 1), (DOWN, 0, 2, 1)),
+    (3, 1): ((DOWN, 2, 0, 0), (DOWN, 1, 1, 0), (UP, 1, 1, 0), (UP, 0, 2, 0), (UP, 2, 0, 0), (DOWN, 2, 1, 1), (UP, 2, 1, 1), (UP, 1, 2, 1)),
+    (3, 3): ((DOWN, 0, 2, 0), (DOWN, 0, 3, 1)),
+    (3, 4): ((DOWN, 3, 0, 1),),
+    (3, 5): ((UP, 1, 2, 0), (UP, 3, 0, 1), (DOWN, 1, 2, 1)),
+    (4, 1): ((UP, 1, 3, 1),),
+    (4, 4): ((DOWN, 3, 0, 0), (DOWN, 2, 1, 0), (UP, 2, 1, 0)),
+    (4, 5): ((DOWN, 0, 3, 0), (UP, 3, 0, 0), (GATE, 0, 0, 1), (UP, 0, 3, 1)),
+    (4, 7): ((DOWN, 1, 2, 0), (GATE, 1, 0, 1)),
+}
+FEED_LEFT = (
+    (DOWN, 3, 0, True),
+    (UP, 3, 0, True),
+    (DOWN, 2, 1, True),
+    (DOWN, 1, 2, True),
+    (UP, 2, 1, True),
+    (DOWN, 0, 3, True),
+    (UP, 1, 3, False),
+    (GATE, 0, 0, False),
+    (UP, 0, 3, False),
+    (GATE, 1, 0, False),
+)
+
+
+def ffn_body(
+    length_ref, a_two_ref, cot_ref, gain_ref, up_ref, down_ref, hidden_hbm, wout_hbm, state_hbm, q_hbm, a_one_hbm,
+    out_hbm, d_hidden_hbm, d_query_hbm, d_state_hbm, gain_grad_ref, up_out, down_out, *rest,
+):
+    left = rest[: len(FEED_LEFT)]
+    (
+        total, back, act, d_pre, d_down, hidden, wout, state, q, a_one, in_sems, out_sems,
+        up_flat, up_side, down_flat, down_side, gate_base, up_sems, down_sems, gate_sems, *lands,
+    ) = rest[len(FEED_LEFT) :]
+    j = pl.program_id(0)
+    quarters = 4
+    length, width = a_two_ref.shape
+    tile = up_ref.shape[1]
+    live = length_ref[0]
+    rows_count = 256
+
+    sums = {}
+    lands = list(lands)
+    up_bases, down_bases = (up_flat, up_side), (down_flat, down_side)
+
+    def take(count):
+        taken = lands[:count]
+        del lands[:count]
+        return taken
+
+    for t in range(quarters):
+        order, sideways = ORDER[UP][t], ORDER[DOWN][t] == "Y"
+
+        def keep_up(own, given, sideways, t=t):
+            put(up_out, t * tile, own, given, sideways)
+
+        def keep_down(own, given, sideways):
+            put(down_out, 0, own, given, sideways)
+
+        refs = [up_bases[order in "XZ"]] + take(6 if order in "XZ" else 5)
+        sums[UP, t] = Sum(refs, up_sems.at[t], order, keep_up)
+        refs = [down_bases[sideways]] + take(6 if sideways else 5)
+        sums[DOWN, t] = Gather(t, refs, down_sems.at[t], sideways, keep_down)
+    for i in range(2):
+        sums[GATE, i] = Sum([gate_base.at[i]] + take(5), gate_sems.at[i], ORDER[GATE][i])
+
+    def run(step, number):
+        follow(sums, FEED_PLAN.get((step, number), ()))
+
+    def slot(step, number):
+        if FEED_PLAN.get((step, number)):
+
+            @pl.when(j == step)
+            def _():
+                run(step, number)
+
+    def slots(number):
+        for step in range(quarters):
+            slot(step, number)
+
+    late = [
+        pltpu.make_async_copy(source, target, in_sems.at[i])
+        for i, (source, target) in enumerate(
+            ((hidden_hbm, hidden), (q_hbm, q), (state_hbm, state), (wout_hbm, wout), (a_one_hbm, a_one))
+        )
+    ]
+
+    @pl.when(j == 0)
+    def _():
+        for copy in late:
+            copy.start()
+        greet((CORE, MIDDLE, NEAR, FAR, SIDE))
+        for low in range(0, length, rows_count):
+            rows = slice(low, low + rows_count)
+            d_down[rows, :] = (cot_ref[rows, :].astype(F32) * live_rows(live, low, rows_count)).astype(BF16)
+        total[...] = jnp.zeros_like(total)
+        back[...] = jnp.zeros_like(back)
+        down_out[...] = jnp.zeros_like(down_out)
+        up_out[...] = jnp.zeros_like(up_out)
+
+    def chunk(low):
+        rows = pl.ds(low, rows_count)
+        pre = dot(a_two_ref[rows, :], up_ref[...])
+        d_act = dot_nt(d_down[rows, :], down_ref[...])
+        value, slope = gelu_pair(pre)
+        act[rows, :] = value.astype(BF16)
+        d_pre[rows, :] = (d_act * slope).astype(BF16)
+        total[rows, :] += dot(act[rows, :], down_ref[...])
+        back[rows, :] += dot_nt(d_pre[rows, :], up_ref[...])
+
+    @pl.when(j < quarters)
+    def _():
+        def step(part, carry):
+            chunk(pl.multiple_of(part * rows_count, rows_count))
+            for t in range(1, quarters):
+                for number in range(4):
+                    if FEED_PLAN.get((t, number)):
+                        pl.when(jnp.logical_and(j == t, part == number))(functools.partial(run, t, number))
+            return carry
+
+        lax.fori_loop(0, 4, step, 0)
+
+    share = tile // 4
+    for sideways in (False, True):
+        steps = [t for t in range(quarters) if (ORDER[DOWN][t] == "Y") == sideways]
+
+        @pl.when(functools.reduce(jnp.logical_or, [j == t for t in steps], False))
+        def _(sideways=sideways):
+            value = dot_tn(act[...], d_down[...]).astype(BF16)
+            side = lax.axis_index("seq")
+            for owner, (core, x) in enumerate(places(lax.axis_index("dp"), 4, (1, 2))):
+                rows = value[owner * share : (owner + 1) * share]
+                if sideways:
+                    down_side[core, side, x] = rows[:, : width // 2]
+                    down_side[core, 1 - side, x] = rows[:, width // 2 :]
+                else:
+                    down_flat[core, x] = rows
+
+    slots(4)
+
+    for sideways in (False, True):
+        steps = [t for t in range(quarters) if (ORDER[UP][t] in "XZ") == sideways]
+
+        @pl.when(functools.reduce(jnp.logical_or, [j == t for t in steps], False))
+        def _(sideways=sideways):
+            spread(dot_tn(a_two_ref[...], d_pre[...]), up_bases[sideways], sideways)
+
+    slots(5)
+
+    def send(source, target, number):
+        return pltpu.make_async_copy(source, target, out_sems.at[number])
+
+    @pl.when(j == quarters)
+    def _():
+        run(4, 0)
+        late[0].wait()
+        late[1].wait()
+        late[2].wait()
+        gain_sum = jnp.zeros((1, width), F32)
+        for low in range(0, length, rows_count):
+            rows = slice(low, low + rows_count)
+            mask = live_rows(live, low, rows_count)
+            before = hidden[rows, :]
+            d_pre[rows, :] = (before + mask * total[rows, :]).astype(BF16)
+            normed, inv = norm_stats(before)
+            grad_in = back[rows, :]
+            gain_sum = gain_sum + jnp.sum(grad_in * normed, axis=0, keepdims=True)
+            d_hidden = cot_ref[rows, :].astype(F32) + norm_pull(grad_in, normed, inv, gain_ref[...])
+            back[rows, :] = d_hidden
+            d_down[rows, :] = (mask * d_hidden).astype(BF16)
+            gated = q[rows, :].astype(F32) * state[rows, :].astype(F32)
+            act[rows, :] = gated.astype(BF16)
+            run(4, 1 + low // rows_count)
+        gain_grad_ref[...] = gain_sum
+        copies = [send(d_pre, out_hbm, 0), send(back, d_hidden_hbm, 1)]
+        for copy in copies:
+            copy.start()
+        spread(dot_tn(act[...], d_down[...]), gate_base.at[0])
+        run(4, 5)
+        late[3].wait()
+        late[4].wait()
+        for low in range(0, length, rows_count):
+            rows = slice(low, low + rows_count)
+            d_gated = dot_nt(d_down[rows, :], wout[...])
+            total[rows, :] = d_gated
+            act[rows, :] = (d_gated * state[rows, :].astype(F32)).astype(BF16)
+        copies.append(send(act, d_query_hbm, 2))
+        copies[2].start()
+        run(4, 6)
+        spread(dot_tn(a_one[...], act[...]), gate_base.at[1])
+        run(4, 7)
+        for low in range(0, length, rows_count):
+            rows = slice(low, low + rows_count)
+            d_down[rows, :] = (total[rows, :] * q[rows, :].astype(F32)).astype(BF16)
+        copies.append(send(d_down, d_state_hbm, 3))
+        copies[3].start()
+        run(4, 8)
+        for i, (name, index, exchange, waited) in enumerate(FEED_LEFT):
+            if not waited:
+                sums[name, index].wait(exchange)
+            copies.append(send(sums[name, index].refs[exchange + 1], left[i], 4 + i))
+            copies[-1].start()
+        for copy in copies:
+            copy.wait()
+
+
+def ffn_call(live, a_two, cot, hidden, gain, up, down, wout, state, q, a_one):
+    length, width = a_two.shape
+    hidden_units = up.shape[1]
+    tile = hidden_units // 4
+    su, sd = width // 16, tile // 4
+    rows_full = once((length, width))
+    anywhere = pl.BlockSpec(memory_space=pl.ANY)
+    low = lambda *shape: jax.ShapeDtypeStruct(shape, BF16)
+    full = lambda *shape: jax.ShapeDtypeStruct(shape, F32)
+    vmem = lambda *shape: pltpu.VMEM(shape, BF16)
+    wide = lambda *shape: pltpu.VMEM(shape, F32)
+    sems = lambda *shape: pltpu.SemaphoreType.DMA(shape)
+    shape_of = {}
+    for t in range(4):
+        shape_of[UP, t] = landings(su, tile, ORDER[UP][t])
+        shape_of[DOWN, t] = gather_landings(sd, width, ORDER[DOWN][t] == "Y")
+    for i in range(2):
+        shape_of[GATE, i] = landings(su, width, ORDER[GATE][i])
+    left = [low(*shape_of[name, index][exchange].shape) for name, index, exchange, _ in FEED_LEFT]
+    for name, index, exchange, _ in FEED_LEFT:
+        shapes = shape_of[name, index]
+        shapes[exchange + 1 :] = [vmem(16, LANES)] * (len(shapes) - exchange - 1)
+    lands = [shape for shapes in shape_of.values() for shape in shapes]
+    return pl.pallas_call(
+        ffn_body,
+        grid=(5,),
+        in_specs=[
+            pl.BlockSpec(memory_space=pltpu.SMEM),
+            rows_full,
+            rows_full,
+            once((1, width)),
+            pl.BlockSpec((width, tile), lambda j: (0, jnp.minimum(j, 3))),
+            pl.BlockSpec((tile, width), lambda j: (jnp.minimum(j, 3), 0)),
+        ]
+        + [anywhere] * 5,
+        out_specs=[anywhere] * 4 + [once((1, width)), once((su, hidden_units)), once((sd, width))] + [anywhere] * len(left),
+        out_shape=[
+            low(length, width),
+            full(length, width),
+            low(length, width),
+            low(length, width),
+            full(1, width),
+            full(su, hidden_units),
+            full(sd, width),
+            *left,
+        ],
+        scratch_shapes=[
+            wide(length, width),
+            wide(length, width),
+            vmem(length, tile),
+            vmem(length, tile),
+            vmem(length, width),
+            wide(length, width),
+            vmem(*wout.shape),
+            vmem(length, width),
+            vmem(length, width),
+            vmem(length, width),
+            sems(5),
+            sems(4 + len(left)),
+            vmem(*base_shape(su, tile, "x")) if set(ORDER[UP]) & set("xz") else vmem(16, LANES),
+            vmem(*base_shape(su, tile, "X")) if set(ORDER[UP]) & set("XZ") else vmem(16, LANES),
+            vmem(2, 2, sd, width) if "n" in ORDER[DOWN] else vmem(16, LANES),
+            vmem(2, 2, 2, sd, width // 2) if "Y" in ORDER[DOWN] else vmem(16, LANES),
+            vmem(2, *base_shape(su, width, "x")),
+            sems(4, 6, 2),
+            sems(4, 6, 2),
+            sems(2, 5, 2),
+            *lands,
+        ],
+        compiler_params=pltpu.CompilerParams(vmem_limit_bytes=62 * 1024 * 1024, collective_id=1, has_side_effects=True),
+        cost_estimate=cost(12 * length * width * hidden_units, 40e6),
+        name="feed_forward",
+    )(live, a_two, cot, gain, up, down, hidden, wout, state, q, a_one)
+
+
+BACK_PLAN = {
+    (0, 0): ((OUT, 0, 0, 1), (OUT, 1, 0, 1), (UP, 3, 1, 1), (GATE, 0, 1, 1), (GATE, 1, 1, 1), (DOWN, 1, 3, 1), (DOWN, 0, 4, 1)),
+    (1, 1): ((UP, 2, 2, 1),),
+    (2, 1): ((DOWN, 1, 3, 0),),
+    (2, 2): ((DOWN, 0, 4, 0),),
+    (2, 3): ((KERN, 0, 0, 1),),
+    (3, 2): ((DOWN, 2, 2, 1), (DOWN, 1, 4, 1)),
+    (3, 4): ((UP, 3, 1, 0), (GATE, 0, 1, 0), (GATE, 1, 1, 0), (UP, 2, 2, 0), (KERN, 0, 0, 0), (KERN, 0, 1, 1), (UP, 3, 2, 1)),
+    (3, 5): ((DOWN, 3, 1, 1), (VALUE, 0, 0, 1), (KEY, 0, 0, 1), (GATE, 0, 2, 1), (DOWN, 0, 5, 1)),
+    (4, 2): ((OUT, 0, 0, 0), (OUT, 1, 0, 0), (DOWN, 2, 2, 0), (DOWN, 1, 4, 0)),
+    (4, 3): ((VALUE, 0, 0, 0), (KEY, 0, 0, 0), (VALUE, 0, 1, 1), (KEY, 0, 1, 1)),
+    (4, 4): ((DOWN, 2, 3, 1), (GATE, 1, 2, 1)),
+    (4, 5): ((DOWN, 0, 5, 0), (VALUE, 1, 0, 1), (KEY, 1, 0, 1)),
+    (5, 1): ((GATE, 0, 2, 0), (UP, 3, 2, 0), (UP, 3, 3, 1), (DOWN, 1, 5, 1)),
+    (5, 2): ((UP, 1, 4, 1),),
+    (5, 3): ((VALUE, 1, 0, 0), (KEY, 1, 0, 0), (VALUE, 0, 1, 0), (KEY, 0, 1, 0), (VALUE, 1, 1, 1), (KEY, 1, 1, 1), (VALUE, 0, 2, 1)),
+    (5, 4): ((KERN, 0, 1, 0), (DOWN, 3, 1, 0), (KERN, 0, 2, 1), (KEY, 0, 2, 1), (UP, 0, 4, 1)),
+    (5, 5): ((UP, 3, 3, 0), (DOWN, 3, 2, 1), (VALUE, 2, 0, 1), (TAPS, 0, 0, 1), (KEY, 2, 0, 1)),
+    (5, 7): ((UP, 1, 4, 0), (DOWN, 2, 3, 0), (GATE, 1, 2, 0), (DOWN, 2, 4, 1), (ROW, 0, 0, 1)),
+    (5, 8): ((DOWN, 1, 5, 0), (ROW, 1, 0, 1)),
+    (5, 9): ((VALUE, 0, 2, 0), (VALUE, 2, 0, 0), (TAPS, 0, 0, 0), (KEY, 2, 0, 0), (TAPS, 0, 1, 1)),
+    (5, 10): ((KEY, 0, 2, 0), (VALUE, 1, 1, 0), (KEY, 1, 1, 0), (UP, 0, 4, 0), (KEY, 2, 1, 1)),
+    (5, 11): ((GAIN, 0, 0, 1),),
+}
+BACK_LEFT = (
+    (KEY, 1, 2, 1),
+    (DOWN, 3, 2, 0),
+    (VALUE, 1, 2, 1),
+    (GAIN, 0, 0, 0),
+    (DOWN, 3, 3, 1),
+    (UP, 2, 3, 1),
+    (GAIN, 0, 1, 1),
+    (KERN, 0, 2, 0),
+    (TAPS, 0, 1, 0),
+    (DOWN, 2, 4, 0),
+    (KEY, 1, 2, 0),
+    (KERN, 0, 3, 1),
+    (KEY, 2, 1, 0),
+    (VALUE, 1, 2, 0),
+    (GAIN, 0, 1, 0),
+    (TAPS, 0, 2, 1),
+    (UP, 2, 3, 0),
+    (KEY, 2, 2, 1),
+    (GATE, 0, 3, 1),
+    (DOWN, 3, 3, 0),
+    (VALUE, 2, 1, 1),
+    (DOWN, 3, 4, 1),
+    (TAPS, 0, 2, 0),
+    (DOWN, 2, 5, 1),
+    (KERN, 0, 3, 0),
+    (GATE, 1, 3, 1),
+    (ROW, 0, 0, 0),
+    (KERN, 0, 4, 1),
+    (KEY, 2, 2, 0),
+    (ROW, 1, 0, 0),
+    (UP, 3, 4, 1),
+    (UP, 2, 4, 1),
+    (VALUE, 2, 1, 0),
+    (GATE, 0, 3, 0),
+    (VALUE, 2, 2, 1),
+    (GAIN, 0, 2, 1),
+    (VALUE, 0, 3, 1),
+    (DOWN, 2, 5, 0),
+    (KERN, 0, 4, 0),
+    (COEF, 0, 0, 1),
+    (GATE, 0, 4, 1),
+    (VALUE, 1, 3, 1),
+    (TAPS, 0, 3, 1),
+    (VALUE, 2, 2, 0),
+    (VALUE, 2, 3, 1),
+    (KEY, 0, 3, 1),
+    (GATE, 1, 3, 0),
+    (GATE, 1, 4, 1),
+    (COEF, 0, 0, 0),
+    (GAIN, 0, 2, 0),
+    (COEF, 0, 1, 1),
+    (GAIN, 0, 3, 1),
+    (UP, 3, 4, 0),
+    (UP, 2, 4, 0),
+    (KEY, 1, 3, 1),
+    (VALUE, 0, 3, 0),
+    (DOWN, 3, 4, 0),
+    (DOWN, 3, 5, 1),
+    (VALUE, 1, 3, 0),
+    (GATE, 0, 4, 0),
+    (KEY, 2, 3, 1),
+    (VALUE, 0, 4, 1),
+    (VALUE, 2, 3, 0),
+    (TAPS, 0, 3, 0),
+    (TAPS, 0, 4, 1),
+    (VALUE, 1, 4, 1),
+    (GATE, 1, 4, 0),
+    (COEF, 0, 1, 0),
+    (KEY, 0, 3, 0),
+    (COEF, 0, 2, 1),
+    (KEY, 0, 4, 1),
+    (VALUE, 2, 4, 1),
+    (GAIN, 0, 3, 0),
+    (GAIN, 0, 4, 1),
+    (KEY, 1, 3, 0),
+    (KEY, 1, 4, 1),
+    (TAPS, 0, 4, 0),
+    (VALUE, 0, 4, 0),
+    (VALUE, 0, 5, 1),
+    (DOWN, 3, 5, 0),
+    (KEY, 0, 4, 0),
+    (KEY, 2, 3, 0),
+    (KEY, 2, 4, 1),
+    (COEF, 0, 2, 0),
+    (VALUE, 1, 4, 0),
+    (COEF, 0, 3, 1),
+    (VALUE, 1, 5, 1),
+    (VALUE, 2, 4, 0),
+    (VALUE, 2, 5, 1),
+    (GAIN, 0, 4, 0),
+    (KEY, 1, 4, 0),
+    (VALUE, 0, 5, 0),
+    (KEY, 2, 4, 0),
+    (VALUE, 1, 5, 0),
+    (VALUE, 2, 5, 0),
+    (COEF, 0, 3, 0),
+)
+
+
+def mixer_back_body(
+    length_ref, out_row_ref, d_state_ref, d_query_ref, mixed_ref, shifted_ref, k_ref, v_ref,
+    wq_ref, wk_ref, wv_ref, kern_ref, tapspec_ref, table_ref, back_ref, gain_ref, gain_two_grad_ref,
+    coef_ref, rate_ref, up_part_ref, down_part_ref, *rest,
+):
+    left = rest[: len(FEED_LEFT)]
+    (
+        a_one_hbm, x_hbm, d_hidden_hbm,
+        out_ref, d_tokens_ref, gains_out, taps_out, coef_out, rate_out, up_ref, down_ref, gate_out, kv_out,
+        total, spec_one, spec_two, prod, shift_prod, d_keys, d_values, d_x, a_one, x, d_hidden, d_taps, d_kern,
+        gain_refs, gain_lands, gain_sems, taps_base, taps_sems, coef_base, coef_sems,
+        kern_base, key_base, value_base, left_sems, kern_sems, kv_sems, out_sems, row_sems, own_sems, in_sems, *lands,
+    ) = rest[len(FEED_LEFT) :]
+    j = pl.program_id(0)
+    length, width = a_one.shape
+    half = length // 2
+    tile = k_ref.shape[1]
+    tiles = width // tile
+    blocks = length // BLOCK
+    live = length_ref[0]
+    side = lax.axis_index("seq")
+    own_rows = pl.ds(pl.multiple_of(side * half, half), half)
+
+    sums = {}
+    lands = list(lands)
+    kv_bases = (key_base, value_base)
+
+    def take(count):
+        taken = lands[:count]
+        del lands[:count]
+        return taken
+
+    for i, (name, index, exchange, _) in enumerate(FEED_LEFT):
+
+        def keep(own, given, sideways, name=name, index=index):
+            if name == UP:
+                put(up_ref, index * width, own, given, sideways)
+            elif name == DOWN:
+                put(down_ref, 0, own, given, sideways)
+            else:
+                put(gate_out.at[index], 0, own, given, sideways)
+
+        order = ORDER[name][index]
+        refs = [None] * (exchange + 1) + [left[i]] + take((5 if order in "XZY" else 4) - exchange)
+        if name == DOWN:
+            sums[name, index] = Gather(index, refs, left_sems.at[i], order == "Y", keep)
+        else:
+            sums[name, index] = Sum(refs, left_sems.at[i], order, keep)
+
+    states, channels = rate_ref.shape
+    each = states // 16
+
+    def keep_kern(own, given, sideways):
+        put(d_kern, 0, own, given, sideways)
+        steps = d_kern.shape[0]
+        first = lax.convert_element_type(lax.axis_index("dp") * steps, F32)
+        for low in range(0, channels, LANES):
+            lanes = slice(low, low + LANES)
+            rate = rate_ref[:, lanes]
+            from_lane = pl.ds(pl.multiple_of(side * channels + low, LANES), LANES)
+
+            def group(g, sums, rate=rate, from_lane=from_lane):
+                coef_sum, rate_sum = sums
+                rows = d_kern[pl.ds(pl.multiple_of(g * 8, 8), 8), from_lane]
+                for i in range(8):
+                    time = first + lax.convert_element_type(g * 8 + i, F32)
+                    term = jnp.exp(rate * -time) * rows[i : i + 1]
+                    coef_sum = coef_sum + term
+                    rate_sum = rate_sum + term * time
+                return coef_sum, rate_sum
+
+            zeros = jnp.zeros((states, LANES), F32)
+            coef_sum, rate_sum = lax.fori_loop(0, steps // 8, group, (zeros, zeros))
+            rate_sum = -coef_ref[:, lanes] * rate_sum
+            for owner, place in enumerate(places(lax.axis_index("dp"), 16, (1, 2, 4, 8))):
+                rows = slice(owner * each, (owner + 1) * each)
+                coef_base[(*place, slice(0, each), lanes)] = coef_sum[rows]
+                coef_base[(*place, slice(each, 2 * each), lanes)] = rate_sum[rows]
+
+    def keep_coef(value):
+        flat = jnp.transpose(value)
+        coef_out[...] = flat[:, :each]
+        rate_out[...] = flat[:, each:]
+
+    def keep_taps(own, given, sideways):
+        both = jnp.concatenate([own + given] * 2, axis=0)
+        flat = jnp.where(side == 0, both[:, :channels], both[:, channels:])
+        taps_out[...] = jnp.transpose(flat)[:, :each]
+
+    sums[COEF, 0] = Sum([coef_base] + take(4), coef_sems, "x", keep_coef, across=False)
+    sums[TAPS, 0] = Sum([taps_base] + take(5), taps_sems, "x", keep_taps)
+    sums[GAIN, 0] = Whole(gain_refs, gain_lands, gain_sems)
+
+    for i in range(2):
+        piece = pl.ds(i * (half // 2), half // 2)
+        other = pl.ds(pl.multiple_of((1 - side) * half + i * (half // 2), half // 2), half // 2)
+        sums[OUT, i] = Rows(out_row_ref.at[other], out_ref.at[side, piece], out_sems.at[i])
+        sums[ROW, i] = Rows(d_x.at[0, piece], d_tokens_ref.at[side, piece], row_sems.at[i])
+    kern_sideways = ORDER[KERN] in "XZ"
+    sums[KERN, 0] = Sum([kern_base] + take(6 if kern_sideways else 5), kern_sems, ORDER[KERN], keep_kern)
+    for t in range(tiles):
+        for i, name in enumerate((KEY, VALUE)):
+
+            def keep_kv(own, given, sideways, t=t, i=i):
+                put(kv_out.at[i], t * tile, own, given, sideways)
+
+            order = ORDER[KV][i]
+            refs = [kv_bases[i].at[t]] + take(6 if order in "XZ" else 5)
+            sums[name, t] = Sum(refs, kv_sems.at[t, i], order, keep_kv)
+
+    def events(step, number):
+        follow(sums, BACK_PLAN.get((step, number), ()))
+
+    def slots(first, last, number):
+        for step in range(first, last):
+            if BACK_PLAN.get((step, number)):
+                pl.when(j == step)(functools.partial(events, step, number))
+
+    def keep_out():
+        return pltpu.make_async_copy(out_row_ref.at[own_rows], out_ref.at[side], own_sems.at[0])
+
+    def keep_row():
+        return pltpu.make_async_copy(d_x.at[1], d_tokens_ref.at[side], own_sems.at[1])
+
+    late = [
+        pltpu.make_async_copy(source, target, in_sems.at[i])
+        for i, (source, target) in enumerate(((a_one_hbm, a_one), (x_hbm, x), (d_hidden_hbm, d_hidden)))
+    ]
+
+    @pl.when(j == 0)
+    def _():
+        greet((CORE, MIDDLE, NEAR, FAR, SIDE))
+        events(0, 0)
+        keep_out().start()
+        for copy in late:
+            copy.start()
+        up_ref[...] = up_part_ref[...]
+        down_ref[...] = down_part_ref[...]
+
+    def kernel_product(sign, re, im, lanes):
+        s = [(spec_one[b, re, lanes], spec_one[b, im, lanes]) for b in range(blocks)]
+        x = [(spec_two[b, re, lanes], spec_two[b, im, lanes]) for b in range(blocks)]
+        after = None
+        for d in range(blocks - 1, -1, -1):
+            yr, yi = multiply_conj(*x[0], *s[d])
+            for i in range(d + 1, blocks):
+                pr, pi = multiply_conj(*x[i - d], *s[i])
+                yr, yi = yr + pr, yi + pi
+            if after is None:
+                hr, hi = yr, yi
+            else:
+                hr, hi = yr + sign * after[1], yi - sign * after[0]
+            after = (yr, yi)
+            prod[d, re, lanes] = hr.astype(BF16)
+            prod[d, im, lanes] = hi.astype(BF16)
+
+    @pl.when(j < tiles)
+    def _():
+        for b in range(blocks):
+            rows = slice(b * BLOCK, (b + 1) * BLOCK)
+            spec_one[b] = dot(table_ref[...], d_state_ref[rows, :])
+            spec_two[b] = dot(table_ref[...], mixed_ref[rows, :])
+
+    slots(0, tiles, 1)
+
+    @pl.when(j < tiles)
+    def _():
+        spectral_loop(tile, kernel_product)
+
+    slots(0, tiles, 2)
+
+    @pl.when(j < tiles)
+    def _():
+        parts = [dot(back_ref[...], prod[b]) * (1.0 / BLOCK) for b in range(blocks)]
+        kern_parts = jnp.concatenate(parts, axis=0)
+        if kern_sideways:
+            columns = pl.ds(pl.multiple_of(j * (tile // 2), tile // 2), tile // 2)
+        else:
+            columns = pl.ds(pl.multiple_of(j * tile, tile), tile)
+        spread(kern_parts, kern_base.at[..., columns], kern_sideways)
+
+    @pl.when(j == tiles - 1)
+    def _():
+        total[...] = jnp.zeros_like(total)
+        late[0].wait()
+
+    slots(0, tiles, 3)
+
+    def state_product(sign, re, im, lanes):
+        s = [(spec_one[b, re, lanes], spec_one[b, im, lanes]) for b in range(blocks)]
+        h = [(kern_ref[b, re, lanes].astype(F32), kern_ref[b, im, lanes].astype(F32)) for b in range(blocks)]
+        for b in range(blocks):
+            yr, yi = multiply_conj(*h[0], *s[b])
+            for i in range(b + 1, blocks):
+                pr, pi = multiply_conj(*h[i - b], *s[i])
+                yr, yi = yr + pr, yi + pi
+            prod[b, re, lanes] = yr.astype(BF16)
+            prod[b, im, lanes] = yi.astype(BF16)
+
+    @pl.when(j >= tiles)
+    def _():
+        for b in range(blocks):
+            spec_one[b] = dot(table_ref[...], d_state_ref[b * BLOCK : (b + 1) * BLOCK, :])
+
+    slots(tiles, 2 * tiles, 1)
+
+    @pl.when(j >= tiles)
+    def _():
+        spectral_loop(tile, state_product)
+
+    slots(tiles, 2 * tiles, 2)
+
+    @pl.when(j >= tiles)
+    def _():
+        for b in range(blocks):
+            rows = slice(b * BLOCK, (b + 1) * BLOCK)
+            mask = live_rows(live, b * BLOCK, BLOCK)
+            d_mixed = dot(back_ref[...], prod[b]).astype(BF16).astype(F32)
+            d_values[rows, :] = (mask * d_mixed * shifted_ref[rows, :].astype(F32)).astype(BF16)
+            d_shifted = (d_mixed * v_ref[rows, :].astype(F32)).astype(BF16)
+            spec_one[b] = dot(table_ref[...], d_shifted)
+            spec_two[b] = dot(table_ref[...], k_ref[rows, :])
+
+    slots(tiles, 2 * tiles, 3)
+
+    def shift_product(sign, re, im, lanes):
+        tr = tapspec_ref[re, lanes]
+        ti = tapspec_ref[im, lanes]
+        s = [(spec_one[b, re, lanes], spec_one[b, im, lanes]) for b in range(blocks)]
+        x = [(spec_two[b, re, lanes], spec_two[b, im, lanes]) for b in range(blocks)]
+        u = [multiply_conj(tr, ti, *s[b]) for b in range(blocks)]
+        sum_re, sum_im = multiply_conj(*x[0], *s[0])
+        for b in range(blocks):
+            yr, yi = u[b]
+            if b < blocks - 1:
+                yr, yi = yr + sign * u[b + 1][1], yi - sign * u[b + 1][0]
+            prod[b, re, lanes] = yr.astype(BF16)
+            prod[b, im, lanes] = yi.astype(BF16)
+            if b > 0:
+                wr = x[b][0] - sign * x[b - 1][1]
+                wi = x[b][1] + sign * x[b - 1][0]
+                pr, pi = multiply_conj(wr, wi, *s[b])
+                sum_re, sum_im = sum_re + pr, sum_im + pi
+        shift_prod[re, lanes] = sum_re.astype(BF16)
+        shift_prod[im, lanes] = sum_im.astype(BF16)
+
+    def token_grad(rows):
+        return (
+            total[rows, :]
+            + dot_nt(d_query_ref[rows, :], wq_ref[...])
+            + dot_nt(d_keys[rows, :], wk_ref[...])
+            + dot_nt(d_values[rows, :], wv_ref[...])
+        )
+
+    @pl.when(j >= tiles)
+    def _():
+        spectral_loop(tile, shift_product)
+
+    slots(tiles, 2 * tiles, 4)
+
+    @pl.when(j >= tiles)
+    def _():
+        for b in range(blocks):
+            rows = slice(b * BLOCK, (b + 1) * BLOCK)
+            mask = live_rows(live, b * BLOCK, BLOCK)
+            d_keys[rows, :] = (mask * dot(back_ref[...], prod[b])).astype(BF16)
+        taps = d_taps.shape[0]
+        columns = pl.ds(pl.multiple_of((j - tiles) * tile, tile), tile)
+        d_taps[:, columns] = dot(back_ref[:taps, :], shift_prod[...]) * (1.0 / BLOCK)
+        spread(dot_tn(a_one[...], d_keys[...]), key_base.at[j - tiles], ORDER[KV][0] in "XZ")
+        spread(dot_tn(a_one[...], d_values[...]), value_base.at[j - tiles], ORDER[KV][1] in "XZ")
+
+    @pl.when(j == 2 * tiles - 1)
+    def _():
+        for owner, place in enumerate(places(lax.axis_index("dp"), 16, (1, 2, 4, 8))):
+            taps_base[place] = d_taps[owner * each : (owner + 1) * each, :]
+
+    slots(tiles, 2 * tiles, 5)
+
+    @pl.when(jnp.logical_and(j >= tiles, j < 2 * tiles - 1))
+    def _():
+        for b in range(blocks):
+            rows = slice(b * BLOCK, (b + 1) * BLOCK)
+            total[rows, :] = token_grad(rows)
+
+    slots(tiles, 2 * tiles, 6)
+
+    @pl.when(j == 2 * tiles - 1)
+    def _():
+        late[1].wait()
+        late[2].wait()
+        gain_sum = jnp.zeros((1, width), F32)
+        count = half // BLOCK
+        for b in range(2 * count):
+            low = (1 - side if b < count else side) * half + (b % count) * BLOCK
+            rows = pl.ds(pl.multiple_of(low, BLOCK), BLOCK)
+            normed, inv = norm_stats(x[rows, :].astype(F32))
+            grad_in = token_grad(rows)
+            gain_sum = gain_sum + jnp.sum(grad_in * normed, axis=0, keepdims=True)
+            pulled = d_hidden[rows, :] + norm_pull(grad_in, normed, inv, gain_ref[...])
+            d_x[b // count, (b % count) * BLOCK : (b % count + 1) * BLOCK, :] = pulled.astype(BF16)
+            events(2 * tiles - 1, 7 + b)
+        keep_row().start()
+        gain_refs[0] = jnp.concatenate([gain_sum, gain_two_grad_ref[...], jnp.zeros((6, width), F32)], axis=0)
+        events(2 * tiles - 1, 11)
+        follow(sums, BACK_LEFT)
+        gains_out[...] = gain_refs[5]
+        keep_out().wait()
+        keep_row().wait()
+
+
+def mixer_back_call(
+    live, out_row, a_one, d_state, d_query, mixed, shifted, k, v, wq, wk, wv, kern, tapspec, tables, x, gain, d_hidden,
+    d_gain_two, coef, rate, begun, taps_count, tile,
+):
+    length, width = a_one.shape
+    blocks = length // BLOCK
+    half = length // 2
+    table, back = tables
+    share = width // 16
+    ks = length // 16
+    count = width // tile
+    both = lambda j: (0, lax.rem(j, count))
+    first = lambda j: (0, jnp.minimum(j, count - 1))
+    second = lambda j: (0, jnp.maximum(j - count, 0))
+    rows_second = pl.BlockSpec((length, tile), second)
+    weight = pl.BlockSpec((width, tile), second)
+    anywhere = pl.BlockSpec(memory_space=pl.ANY)
+    low = lambda *shape: jax.ShapeDtypeStruct(shape, BF16)
+    full = lambda *shape: jax.ShapeDtypeStruct(shape, F32)
+    vmem = lambda *shape: pltpu.VMEM(shape, BF16)
+    wide = lambda *shape: pltpu.VMEM(shape, F32)
+    sems = lambda *shape: pltpu.SemaphoreType.DMA(shape)
+    up_part, down_part, left = begun
+    states, channels = rate.shape
+    each = states // 16
+    lands = []
+    for name, index, exchange, _ in FEED_LEFT:
+        order = ORDER[name][index]
+        if name == DOWN:
+            lands += gather_landings(*down_part.shape, order == "Y")[exchange + 1 :]
+        else:
+            lands += landings(share, width, order)[exchange + 1 :]
+    bits = [(2, 2, 2), (2, 2), (2,), (), ()]
+    lands += [wide(*bits[n], 2 * each, channels) for n in range(4)]
+    lands += [wide(*bits[n], each, width) for n in range(5)]
+    lands += landings(ks, width, ORDER[KERN])
+    for t in range(count):
+        lands += landings(share, tile, ORDER[KV][0]) + landings(share, tile, ORDER[KV][1])
+    out_shape = [
+        low(2, half, width),
+        low(2, half, width),
+        full(8, width),
+        full(channels, each),
+        full(channels, each),
+        full(channels, each),
+        full(*up_part.shape),
+        full(*down_part.shape),
+        full(2, share, width),
+        full(2, share, width),
+    ]
+    return pl.pallas_call(
+        mixer_back_body,
+        grid=(2 * count,),
+        in_specs=[pl.BlockSpec(memory_space=pltpu.SMEM), anywhere]
+        + [pl.BlockSpec((length, tile), both), rows_second, pl.BlockSpec((length, tile), first)]
+        + [rows_second] * 3
+        + [weight] * 3
+        + [
+            pl.BlockSpec((blocks, 2 * BLOCK, tile), lambda j: (0, 0, jnp.maximum(j - count, 0))),
+            pl.BlockSpec((2 * BLOCK, tile), second),
+            once(table.shape),
+            once(back.shape),
+            once((1, width)),
+            once((1, width)),
+            once(coef.shape),
+            once(rate.shape),
+            once(up_part.shape),
+            once(down_part.shape),
+        ]
+        + [once(s.shape) for s in left]
+        + [anywhere] * 3,
+        out_specs=[anywhere, anywhere] + [once(s.shape) for s in out_shape[2:]],
+        out_shape=out_shape,
+        scratch_shapes=[
+            wide(length, width),
+            wide(blocks, 2 * BLOCK, tile),
+            wide(blocks, 2 * BLOCK, tile),
+            vmem(blocks, 2 * BLOCK, tile),
+            vmem(2 * BLOCK, tile),
+            vmem(length, tile),
+            vmem(length, tile),
+            vmem(2, half, width),
+            vmem(length, width),
+            vmem(length, width),
+            wide(length, width),
+            wide(taps_count, width),
+            wide(ks, width),
+            wide(6, 8, width),
+            wide(5, 8, width),
+            sems(5, 2),
+            wide(2, 2, 2, 2, each, width),
+            sems(5, 2),
+            wide(2, 2, 2, 2, 2 * each, channels),
+            sems(4, 2),
+            vmem(*base_shape(ks, width, ORDER[KERN])),
+            vmem(count, *base_shape(share, tile, ORDER[KV][0])),
+            vmem(count, *base_shape(share, tile, ORDER[KV][1])),
+            sems(len(left), 6, 2),
+            sems(6, 2),
+            sems(count, 2, 6, 2),
+            sems(2, 2),
+            sems(2, 2),
+            sems(2),
+            sems(3),
+            *lands,
+        ],
+        compiler_params=pltpu.CompilerParams(
+            vmem_limit_bytes=62 * 1024 * 1024, collective_id=2, has_side_effects=True
+        ),
+        cost_estimate=cost(26e9, 40e6),
+        name="mixer_back",
+    )(
+        live, out_row, d_state, d_query, mixed, shifted, k, v, wq, wk, wv, kern, tapspec, table, back, gain,
+        d_gain_two, coef, rate, up_part, down_part, *left, a_one, x, d_hidden,
+    )
+
 
 MICRO = 2
 
@@ -103,7 +1573,7 @@
     return first - second
 
 
-def per_device(
+def split_channels(
     tokens,
     lengths,
     gain_one,
@@ -308,6 +1778,52 @@
     )
 
 
+def split_rows(
+    tokens, lengths, gain_one, w_query, w_key, w_value, w_out, gain_two, w_up, w_down,
+    shift_taps, diag_coef, diag_rate, cotangent,
+):
+    side = lax.axis_index("seq")
+    mine = lax.axis_index("dp")
+    devices = lax.axis_size("dp")
+    width = tokens.shape[2]
+    length = tokens.shape[1] * 2
+    channels, states = diag_coef.shape
+    tile = 256
+    tables = transform_tables()
+    live = lax.dynamic_slice_in_dim(lengths, side, 1, 0)
+    packed = jnp.stack([diag_coef.T, diag_rate.T])
+    row_one = gain_one[None, :]
+    row_two = gain_two[None, :]
+    x, cot, a_one, q, k, v, kern, tapspec, hidden, a_two, shifted, mixed, state = mixer_call(
+        live, tokens, cotangent, packed, shift_taps.T.astype(BF16), row_one, row_two, w_query, w_key, w_value, w_out,
+        tables, tile,
+    )
+    out_row, d_hidden, d_query, d_state, d_gain_two, up_part, down_part, *left = ffn_call(
+        live, a_two, cot, hidden, row_two, w_up, w_down, w_out, state, q, a_one
+    )
+    out, d_tokens, gains, taps_grad, coef_grad, rate_grad, up, down, gate, kv = mixer_back_call(
+        live, out_row, a_one, d_state, d_query, mixed, shifted, k, v, w_query, w_key, w_value, kern, tapspec, tables, x,
+        row_one, d_hidden, d_gain_two, packed[0], packed[1], (up_part, down_part, left), states, tile,
+    )
+    gain_each = width // devices
+    gains = lax.dynamic_slice_in_dim(gains, mine * gain_each, gain_each, 1)
+    return (
+        out,
+        d_tokens,
+        gains[0],
+        gate[1],
+        kv[0],
+        kv[1],
+        gate[0],
+        gains[1],
+        up,
+        down,
+        taps_grad,
+        coef_grad,
+        rate_grad,
+    )
+
+
 def solution(mesh):
     in_specs = (
         P("dp", "seq", None),
@@ -340,6 +1856,19 @@
         P("seq", "dp"),
         P("seq", "dp"),
     )
+
+    def per_device(*args):
+        tokens, shift_taps = args[0], args[10]
+        rows, positions, width = tokens.shape
+        fits = (
+            mesh.shape["seq"] == rows == 2
+            and mesh.shape["dp"] == 16
+            and positions * 2 % BLOCK == 0
+            and width % 256 == 0
+            and shift_taps.shape[1] <= BLOCK
+        )
+        return split_rows(*args) if fits else split_channels(*args)
+
     return jax.shard_map(
         per_device, mesh=mesh, in_specs=in_specs, out_specs=out_specs, check_vma=False
     )

time: 1370 us -> 216 us (0.16)
  matrix products: 732 us -> 0 us
  waiting for transfers between devices: 215 us -> 0 us
  Pallas kernels: 0 us -> 195 us
  other arithmetic: 180 us -> 3.15 us
  local copies, waits for them, and re-layouts: 159 us -> 17.1 us
  starting transfers between devices: 51.4 us -> 0 us
  between operations: 17.9 us -> 0.69 us
    dot_general x56 -> x0, matrix products: 678 us -> none  [the longest x4 114 us: inverse(): jnp.einsum('rfc,tf->rtc', imag_part, sin_weighted, precision=highest)]
    pallas_call x0 -> x3, Pallas kernels: none -> 195 us  [the longest x1 85.2 us: mixer_back_call(): pl.pallas_call(mixer_back_body, grid=(2 * count,), in_specs=[pl.BlockSpec...]
    reduce_scatter x6 -> x0, waiting for transfers between devices: 91 us -> none  [the longest x1 78.8 us: per_device(): lax.psum_scatter(grad_down.astype(jnp.bfloat16), 'dp', scatter_dimension=...]
    unnamed x9 -> x0, waiting for transfers between devices: 87.9 us -> none
    unnamed x13 -> x0, other arithmetic: 77.9 us -> none
    unnamed x345 -> x15, local copies, waits for them, and re-layouts: 83.3 us -> 9.93 us
    reduce_sum x8 -> x0, other arithmetic: 67.8 us -> none  [the longest x1 36.6 us: diag_kernel(): -rate[:, :, None] * steps]
    convert_element_type x24 -> x0, local copies, waits for them, and re-layouts: 54.7 us -> none  [the longest x2 9.91 us: per_device(): values_here = values_ch.astype(jnp.float32)]
  transfers between devices with their start and end apart: 20 -> 0, of which waited for: 6 -> 0; matrix products, arithmetic and copies ran while one was open for 60% -> 0% of each run, Pallas kernels for 0% -> 0%
where the time goes in v3:
time: 216 us
  Pallas kernels  195 us (90%)
  local copies, waits for them, and re-layouts  17.1 us (8%)
  other arithmetic  3.15 us (1%)
    pallas_call x1, Pallas kernels, mixer_back_call(): pl.pallas_call(mixer_back_body, grid=(2 * count,), in_specs=[pl.BlockSpec...  85.2 us
    pallas_call x1, Pallas kernels, ffn_call(): pl.pallas_call(ffn_body, grid=(5,), in_specs=[pl.BlockSpec(memory_space=p...  61.6 us
    pallas_call x1, Pallas kernels, mixer_call(): pl.pallas_call(mixer_body, grid=(1 + width // tile,), in_specs=[pl.BlockS...  48.3 us
    unnamed x15, local copies, waits for them, and re-layouts  9.93 us

profile of v3, /device:TPU:0, one launch (start us, length us, event | category | flops | bytes accessed | tf_op | source)
XLA Modules:
  0.0 216.0 jit_solution(16558523201390783311)
XLA Ops:
  0.6 1.2 dynamic_slice.6.length_ref
  1.9 1.3 broadcast_in_dim.6.gain_one_ref.gain_ref
  3.2 1.3 broadcast_in_dim.7.gain_two_ref.gain_ref
  4.4 1.5 convert_bitcast_fusion.taps_ref
  5.9 1.6 pad_maximum_fusion.own_ref
  7.6 48.3 %mixer_forward.1 = (bf16[1024,768]{1,0:T(8,128)(2,1)}, bf16[1024,768]{1,0:T(8,128)(2,1)}, bf16[1024,768]{1,0:T(8,128)(2,1)}, bf16[1024,768]{1,0:T(8,128)(2,1)}, ...) custom-call(s32[1]{0:T(128)} %dynamic_slice.6.length_ref, ...), custom_call_target="tpu_custom_call" | custom-call | flops 16000000000 | bytes 40000000 | tf_op jit(solution)/shard_map/mixer_forward/pallas_call | solution.py:576
  55.9 61.6 %feed_forward.1 = (bf16[1024,768]{1,0:T(8,128)(2,1)}, f32[1024,768]{1,0:T(8,128)}, bf16[1024,768]{1,0:T(8,128)(2,1)}, bf16[1024,768]{1,0:T(8,128)(2,1)}, f32[1,7...) custom-call(s32[1]{0:T(128)} %dynamic_slice.6.length_ref, ...), custom_call_target="tpu_custom_call" | custom-call | flops 28991029248 | bytes 40000000 | tf_op jit(solution)/shard_map/feed_forward/pallas_call | solution.py:874
  117.5 85.2 %mixer_back.1 = (bf16[2,512,768]{2,1,0:T(8,128)(2,1)}, bf16[2,512,768]{2,1,0:T(8,128)(2,1)}, f32[8,768]{1,0:T(8,128)}, f32[384,4]{1,0:T(8,128)}, f32[384,4]{1,0:...) custom-call(s32[1]{0:T(128)} %dynamic_slice.6.length_ref, ...), custom_call_target="tpu_custom_call" | custom-call | flops 25999998976 | bytes 40000000 | tf_op jit(solution)/shard_map/mixer_back/pallas_call | solution.py:1411
  202.7 0.0 copy-start.1
  202.7 0.9 constant_dynamic-slice_fusion
  203.6 0.5 slice_bitcast_fusion.4
  204.1 1.6 copy.29
  205.7 1.6 copy.30
  207.4 1.6 copy.31
  209.0 1.9 slice_bitcast_fusion
  210.9 0.0 copy-done.1
  210.9 0.0 copy-start
  210.9 1.1 copy.36
  212.1 0.8 copy-done
  212.9 0.0 copy-start.3
  212.9 0.0 copy-start.2
  212.9 1.1 copy.37
  214.1 0.3 copy-done.3
  214.4 0.8 copy.38
  215.2 0.0 copy-done.2
  215.2 0.8 copy.39
Async XLA Ops:
  202.7 8.2 %copy-start.1 = (bf16[2,512,768]{2,1,0:T(8,128)(2,1)S(1)}, bf16[2,512,768]{2,1,0:T(8,128)(2,1)}, u32[]{:S(2)}) copy-start(bf16[2,512,768]{2,1,0:T(8,128)(2,1)} %get-tuple-element.127) | copy-start | bytes 4718596
  210.9 2.0 copy-start
  212.9 1.4 copy-start.3
  212.9 2.3 %copy-start.2 = (f32[192,768]{1,0:T(8,128)S(1)}, f32[192,768]{1,0:T(8,128)}, u32[]{:S(2)}) copy-start(f32[192,768]{1,0:T(8,128)} %get-tuple-element.136) | copy-start | bytes 1769476

commit v4 on v3

--- a/solution.py
+++ b/solution.py
@@ -69,15 +69,13 @@
     half = BLOCK // 2
     for parity in range(2):
         sign = 1.0 if parity == 0 else -1.0
-        for lane in range(channels // LANES):
-            lanes = slice(lane * LANES, (lane + 1) * LANES)
-
-            def step(index, carry, sign=sign, lanes=lanes, parity=parity):
-                low = pl.multiple_of(parity * half + index * CHUNK, CHUNK)
-                body(sign, pl.ds(low, CHUNK), pl.ds(low + BLOCK, CHUNK), lanes)
-                return carry
-
-            lax.fori_loop(0, half // CHUNK, step, 0)
+
+        def step(index, carry, sign=sign, parity=parity):
+            low = pl.multiple_of(parity * half + index * CHUNK, CHUNK)
+            body(sign, pl.ds(low, CHUNK), pl.ds(low + BLOCK, CHUNK), slice(0, channels))
+            return carry
+
+        lax.fori_loop(0, half // CHUNK, step, 0)
 
 
 def multiply(ar, ai, br, bi):
@@ -110,7 +108,7 @@
     return {axis: index + bit * (1 - 2 * bit_of(index, bit))}
 
 
-UP, DOWN, GATE, KERN, KEY, VALUE, KV, OUT, ROW, COEF, TAPS, GAIN = range(12)
+UP, DOWN, GATE, KERN, KEY, VALUE, KV, OUT, ROW, COEF, TAPS = range(11)
 CORE, MIDDLE, NEAR, FAR, SIDE = ("dp", 1), ("dp", 2), ("dp", 4), ("dp", 8), ("seq", 1)
 
 
@@ -161,26 +159,26 @@
             base[(core, *place)] = rows
 
 
+AXES = {"c": CORE, "x": MIDDLE, "n": NEAR, "f": FAR, "y": SIDE}
+
+
 class Sum:
     def __init__(self, refs, sems, order, final=None, across=True):
-        self.refs, self.sems, self.final = refs, sems, final
-        self.outer, self.sideways = order in "zZ", order in "XZ"
-        self.lead = 2 if self.sideways else 1
-        self.last = self.lead + 3
-        self.across = across
+        self.refs, self.sems, self.final, self.across = refs, sems, final, across
+        self.order = "c" + order
+        self.sideways = "y" in order
+        self.last = len(self.order)
 
     def part(self, step, half):
         ref = self.refs[step]
         if step == self.last:
             return ref
-        if self.outer and self.lead <= step < self.lead + 2:
-            return ref.at[:, half]
-        return ref.at[half]
+        left = [axis for axis in "cyxnf" if axis in self.order[step:]]
+        return ref.at[(slice(None),) * left.index(self.order[step]) + (half,)]
 
     def copy(self, step):
-        order = (NEAR, FAR, MIDDLE) if self.outer else (MIDDLE, NEAR, FAR)
-        order = (CORE, *((SIDE,) if self.sideways else ()), *order, SIDE)
-        return transfer(self.part(step, 1), self.refs[step + 1], self.sems.at[step], order[step])
+        axis = AXES[(self.order + "y")[step]]
+        return transfer(self.part(step, 1), self.refs[step + 1], self.sems.at[step], axis)
 
     def start(self, step):
         self.copy(step).start()
@@ -195,25 +193,12 @@
             self.final(self.refs[step][...], self.refs[step + 1][...], self.sideways)
 
 
-class Whole:
-    def __init__(self, refs, lands, sems):
-        self.refs, self.lands, self.sems = refs, lands, sems
-
-    def copy(self, step):
-        return transfer(self.refs.at[step], self.lands.at[step], self.sems.at[step], (CORE, MIDDLE, NEAR, FAR, SIDE)[step])
-
-    def start(self, step):
-        self.copy(step).start()
-
-    def wait(self, step):
-        self.copy(step).wait()
-        self.refs[step + 1] = self.refs[step] + self.lands[step]
-
-
 class Gather:
-    def __init__(self, z, refs, sems, sideways, final=None):
-        self.refs, self.sems, self.final, self.sideways = refs, sems, final, sideways
-        self.lead = 3 if sideways else 2
+    def __init__(self, z, refs, sems, order, final=None):
+        self.refs, self.sems, self.final = refs, sems, final
+        self.order = "c" + order
+        self.sideways = "y" in order
+        self.lead = len(self.order)
         self.last = self.lead + 2
         mine = lax.axis_index("dp")
         near = bit_of(mine, 4) == z % 2
@@ -223,11 +208,15 @@
         self.takes = (near, both, both)
 
     def part(self, step, half):
-        return self.refs[step].at[half] if step < self.lead else self.refs[step]
+        ref = self.refs[step]
+        if step >= self.lead:
+            return ref
+        left = [axis for axis in "cyx" if axis in self.order[step:]]
+        return ref.at[(slice(None),) * left.index(self.order[step]) + (half,)]
 
     def copy(self, step):
-        order = (CORE, *((SIDE,) if self.sideways else ()), MIDDLE, NEAR, FAR, SIDE)
-        return transfer(self.part(step, 1), self.refs[step + 1], self.sems.at[step], order[step])
+        axis = AXES[(self.order + "nfy")[step]]
+        return transfer(self.part(step, 1), self.refs[step + 1], self.sems.at[step], axis)
 
     def start(self, step):
         if step < self.lead:
@@ -287,7 +276,7 @@
 
 
 def base_shape(rows, columns, order):
-    return (2, 2, 2, 2, 2, rows, columns // 2) if order in "XZ" else (2, 2, 2, 2, rows, columns)
+    return (2, 2, 2, 2, 2, rows, columns // 2) if "y" in order else (2, 2, 2, 2, rows, columns)
 
 
 def landings(rows, columns, order):
@@ -295,12 +284,15 @@
     return [pltpu.VMEM((*bits[n + 1 :], rows, columns), BF16) for n in range(len(bits))] + [pltpu.VMEM((rows, columns), BF16)]
 
 
-def gather_landings(rows, columns, sideways):
-    bits = (2, 2) if sideways else (2,)
-    columns = columns // 2 if sideways else columns
-    return [pltpu.VMEM((*bits[n:], rows, columns), BF16) for n in range(len(bits) + 1)] + [
+def gather_landings(rows, columns, order):
+    columns = columns // 2 if "y" in order else columns
+    return [pltpu.VMEM((*(2,) * (len(order) - n), rows, columns), BF16) for n in range(len(order) + 1)] + [
         pltpu.VMEM((rows, columns), BF16) for _ in range(3)
     ]
+
+
+def row_of(ref):
+    return ref[...].reshape(1, ref.shape[0])
 
 
 def once(shape):
@@ -309,7 +301,7 @@
 
 
 def mixer_body(
-    length_ref, tokens_hbm, cot_hbm, own_ref, taps_ref, gain_one_ref, gain_two_ref, wq_hbm, wk_hbm, wv_hbm, wout_hbm,
+    lengths_ref, tokens_hbm, cot_hbm, coef_ref, rate_ref, taps_ref, gain_one_ref, gain_two_ref, wq_hbm, wk_hbm, wv_hbm, wout_hbm,
     table_ref, back_ref,
     x_hbm, cot_out, a_one_hbm, q_hbm, k_hbm, v_hbm, kern_hbm, tapspec_hbm, hidden_hbm, a_two_hbm,
     shifted_ref, mixed_ref, state_ref,
@@ -322,9 +314,9 @@
     half = length // 2
     tile = shifted_ref.shape[1]
     blocks = length // BLOCK
-    states, channels = own_ref.shape[1:]
-    live = length_ref[0]
+    states, channels = coef_ref.shape
     side = lax.axis_index("seq")
+    live = lengths_ref[side]
     core = bit_of(lax.axis_index("dp"), 1)
     own_rows = pl.ds(pl.multiple_of(side * half, half), half)
 
@@ -337,18 +329,27 @@
         for i, (source, target) in enumerate(
             (
                 (x, x_hbm), (a_one, a_one_hbm), (q, q_hbm), (k, k_hbm), (v, v_hbm), (kern, kern_hbm),
-                (tapspec, tapspec_hbm), (total, hidden_hbm), (a_two, a_two_hbm),
+                (tapspec, tapspec_hbm),
             )
         )
     ]
     own_x = pltpu.make_async_copy(tokens_hbm.at[side], x.at[own_rows], own_sems.at[0])
     own_cot = pltpu.make_async_copy(cot_hbm.at[side], cot_out.at[own_rows], own_sems.at[1])
-    other_x = transfer(tokens_hbm.at[1 - side], x.at[own_rows], token_sems, SIDE)
+    other_x = [
+        transfer(
+            tokens_hbm.at[1 - side, pl.ds(i * BLOCK, BLOCK)],
+            x.at[pl.ds(pl.multiple_of(side * half + i * BLOCK, BLOCK), BLOCK)],
+            token_sems.at[i],
+            SIDE,
+        )
+        for i in range(half // BLOCK)
+    ]
     other_cot = transfer(cot_hbm.at[1 - side], cot_out.at[own_rows], cot_sems, SIDE)
     wanted = pl.ds(pl.multiple_of(core * LANES, LANES), 2 * LANES)
-    other_params = transfer(own_ref.at[:, :, wanted], other, other_sems, SIDE)
+    params = (coef_ref, rate_ref)
+    other_params = [transfer(params[i].at[:, wanted], other.at[i], other_sems.at[i], SIDE) for i in range(2)]
     own_lanes = pl.ds(pl.multiple_of(side * channels, LANES), channels)
-    other_taps = transfer(taps_ref, taps.at[:, own_lanes], taps_sems, SIDE)
+    other_taps = transfer(taps.at[:, own_lanes], taps.at[:, own_lanes], taps_sems, SIDE)
 
     def unit_columns(number, of_core):
         tile_of = (2 * of_core, 1, 2 * of_core)[number]
@@ -362,26 +363,26 @@
     def unit(number):
         if number == 0:
             for part in range(2):
-                current[part] = own_ref[part, :, pl.ds(pl.multiple_of(core * 2 * LANES, LANES), LANES)]
+                current[part] = params[part][:, pl.ds(pl.multiple_of(core * 2 * LANES, LANES), LANES)]
         elif number == 1:
 
             @pl.when(core == 0)
             def _():
                 for part in range(2):
-                    current[part] = own_ref[part, :, LANES : 2 * LANES]
+                    current[part] = params[part][:, LANES : 2 * LANES]
 
             @pl.when(core == 1)
             def _():
-                other_params.wait()
                 for part in range(2):
+                    other_params[part].wait()
                     current[part] = other[part, :, :LANES]
 
         else:
 
             @pl.when(core == 0)
             def _():
-                other_params.wait()
                 for part in range(2):
+                    other_params[part].wait()
                     current[part] = other[part, :, :LANES]
 
             @pl.when(core == 1)
@@ -420,19 +421,15 @@
         lax.fori_loop(0, groups // together, group, 0)
         unit_copy(number).start()
 
-    def project_rows(low):
-        def block(b, carry):
-            rows = pl.ds(pl.multiple_of(low + b * BLOCK, BLOCK), BLOCK)
-            normed, _ = norm_stats(x[rows, :].astype(F32))
-            a_rows = (normed * gain_one_ref[...]).astype(BF16)
-            a_one[rows, :] = a_rows
-            mask = live_rows(live, low + b * BLOCK, BLOCK)
-            k[rows, :] = (dot(a_rows, wk[...]) * mask).astype(BF16)
-            v[rows, :] = (dot(a_rows, wv[...]) * mask).astype(BF16)
-            q[rows, :] = dot(a_rows, wq[...]).astype(BF16)
-            return carry
-
-        lax.fori_loop(0, half // BLOCK, block, 0)
+    def project_block(low):
+        rows = pl.ds(pl.multiple_of(low, BLOCK), BLOCK)
+        normed, _ = norm_stats(x[rows, :].astype(F32))
+        a_rows = (normed * row_of(gain_one_ref)).astype(BF16)
+        a_one[rows, :] = a_rows
+        mask = live_rows(live, low, BLOCK)
+        k[rows, :] = (dot(a_rows, wk[...]) * mask).astype(BF16)
+        v[rows, :] = (dot(a_rows, wv[...]) * mask).astype(BF16)
+        q[rows, :] = dot(a_rows, wq[...]).astype(BF16)
 
     @pl.when(j == 0)
     def _():
@@ -441,10 +438,12 @@
         for copy in weights:
             copy.start()
         greet((CORE, SIDE))
-        other_params.start()
+        for copy in other_params:
+            copy.start()
+        for copy in other_x:
+            copy.start()
+        taps[:, own_lanes] = taps_ref[...].astype(BF16)
         other_taps.start()
-        other_x.start()
-        taps[:, own_lanes] = taps_ref[...]
         total[...] = jnp.zeros_like(total)
         unit(0)
         unit(1)
@@ -452,7 +451,12 @@
         for copy in weights:
             copy.wait()
         own_x.wait()
-        project_rows(side * half)
+
+        def own_block(b, carry):
+            project_block(side * half + b * BLOCK)
+            return carry
+
+        lax.fori_loop(0, half // BLOCK, own_block, 0)
         other_taps.wait()
         for number in range(3):
             unit_copy(number).wait()
@@ -463,7 +467,7 @@
                 spec[b] = dot(table_ref[...], kern_time[b * BLOCK : (b + 1) * BLOCK, columns])
 
             def combine(sign, re, im, lanes):
-                to = pl.ds(pl.multiple_of(t * tile + lanes.start, LANES), LANES)
+                to = pl.ds(pl.multiple_of(t * tile + lanes.start, LANES), lanes.stop - lanes.start)
                 for b in range(blocks):
                     out_re = spec[b, re, lanes]
                     out_im = spec[b, im, lanes]
@@ -480,10 +484,12 @@
         lax.fori_loop(0, width // tile, tile_spectra, 0)
         outs[5].start()
         outs[6].start()
-        other_x.wait()
         other_cot.start()
-        outs[0].start()
-        project_rows((1 - side) * half)
+        for i, copy in enumerate(other_x):
+            copy.wait()
+            if i == len(other_x) - 1:
+                outs[0].start()
+            project_block((1 - side) * half + i * BLOCK)
         for copy in outs[1:5]:
             copy.start()
 
@@ -495,7 +501,7 @@
             spec[b] = dot(table_ref[...], k[b * BLOCK : (b + 1) * BLOCK, columns])
 
         def shift_product(sign, re, im, lanes):
-            at = pl.ds(pl.multiple_of(t * tile + lanes.start, LANES), LANES)
+            at = pl.ds(pl.multiple_of(t * tile + lanes.start, LANES), lanes.stop - lanes.start)
             tr = tapspec[re, at]
             ti = tapspec[im, at]
             before = None
@@ -520,7 +526,7 @@
             spec[b] = dot(table_ref[...], mixed_ref[rows, :])
 
         def state_product(sign, re, im, lanes):
-            at = pl.ds(pl.multiple_of(t * tile + lanes.start, LANES), LANES)
+            at = pl.ds(pl.multiple_of(t * tile + lanes.start, LANES), lanes.stop - lanes.start)
             s = [(spec[b, re, lanes], spec[b, im, lanes]) for b in range(blocks)]
             h = [(kern[b, re, at].astype(F32), kern[b, im, at].astype(F32)) for b in range(blocks)]
             for i in range(blocks):
@@ -541,25 +547,35 @@
 
     @pl.when(j == steps - 1)
     def _():
+        def last_copies(b):
+            rows = pl.ds(pl.multiple_of(b * BLOCK, BLOCK), BLOCK)
+            return [
+                pltpu.make_async_copy(total.at[rows], hidden_hbm.at[rows], out_sems.at[7 + b]),
+                pltpu.make_async_copy(a_two.at[rows], a_two_hbm.at[rows], out_sems.at[7 + blocks + b]),
+            ]
+
         def block(b, carry):
             rows = pl.ds(pl.multiple_of(b * BLOCK, BLOCK), BLOCK)
             mask = live_rows(live, b * BLOCK, BLOCK)
             hidden = x[rows, :].astype(F32) + mask * total[rows, :]
             total[rows, :] = hidden
             normed, _ = norm_stats(hidden)
-            a_two[rows, :] = (normed * gain_two_ref[...]).astype(BF16)
+            a_two[rows, :] = (normed * row_of(gain_two_ref)).astype(BF16)
+            for copy in last_copies(b):
+                copy.start()
             return carry
 
         lax.fori_loop(0, blocks, block, 0)
-        outs[7].start()
-        outs[8].start()
+        for b in range(blocks):
+            for copy in last_copies(b):
+                copy.wait()
         for copy in outs:
             copy.wait()
         own_cot.wait()
         other_cot.wait()
 
 
-def mixer_call(live, tokens, cot, own, taps, gain_one, gain_two, wq, wk, wv, wout, tables, tile):
+def mixer_call(lengths, tokens, cot, coef, rate, taps, gain_one, gain_two, wq, wk, wv, wout, tables, tile):
     _, half, width = tokens.shape
     length = 2 * half
     blocks = length // BLOCK
@@ -580,10 +596,11 @@
             pl.BlockSpec(memory_space=pltpu.SMEM),
             anywhere,
             anywhere,
-            once(own.shape),
+            once(coef.shape),
+            once(rate.shape),
             once(taps.shape),
-            once((1, width)),
-            once((1, width)),
+            once((width,)),
+            once((width,)),
             anywhere,
             anywhere,
             anywhere,
@@ -621,54 +638,54 @@
             vmem(blocks, 2 * BLOCK, tile),
             sems(4),
             sems(2),
-            sems(9),
+            sems(7 + 2 * blocks),
+            sems(half // BLOCK, 2),
             sems(2),
-            sems(2),
-            sems(2),
+            sems(2, 2),
             sems(2),
             sems(3, 2),
         ],
         compiler_params=pltpu.CompilerParams(vmem_limit_bytes=VMEM_BYTES, collective_id=3, has_side_effects=True),
         cost_estimate=cost(16e9, 40e6),
         name="mixer_forward",
-    )(live, tokens, cot, own, taps, gain_one, gain_two, wq, wk, wv, wout, table, back)
-
-
-ORDER = {UP: "zxxz", DOWN: "YYYY", GATE: "xx", KERN: "x", KV: "xX"}
+    )(lengths, tokens, cot, coef, rate, taps, gain_one, gain_two, wq, wk, wv, wout, table, back)
+
+
+ORDER = {UP: ["ynfx", "ynfx", "ynfx", "yxnf"], DOWN: ["xy", "xy", "xy", "yx"], GATE: ["xfn", "xnf"], KERN: "xnf", KV: [["nxf"], ["xnf", "nxf"], ["nxf", "xfn"]]}
 FEED_PLAN = {
     (0, 4): ((DOWN, 0, 0, 1),),
     (0, 5): ((UP, 0, 0, 1),),
-    (1, 1): ((DOWN, 0, 0, 0), (UP, 0, 0, 0), (DOWN, 0, 1, 1), (UP, 0, 1, 1)),
+    (1, 1): ((DOWN, 0, 0, 0), (UP, 0, 0, 0), (UP, 0, 1, 1), (DOWN, 0, 1, 1)),
     (1, 4): ((DOWN, 1, 0, 1),),
     (1, 5): ((UP, 1, 0, 1),),
-    (2, 1): ((DOWN, 1, 0, 0), (DOWN, 0, 1, 0), (UP, 0, 1, 0), (UP, 1, 0, 0), (DOWN, 1, 1, 1), (UP, 1, 1, 1), (UP, 0, 2, 1)),
+    (2, 1): ((DOWN, 1, 0, 0), (UP, 0, 1, 0), (DOWN, 0, 1, 0), (UP, 1, 0, 0), (UP, 1, 1, 1), (DOWN, 1, 1, 1), (UP, 0, 2, 1), (DOWN, 0, 2, 1)),
     (2, 4): ((DOWN, 2, 0, 1),),
-    (2, 5): ((UP, 2, 0, 1), (DOWN, 0, 2, 1)),
-    (3, 1): ((DOWN, 2, 0, 0), (DOWN, 1, 1, 0), (UP, 1, 1, 0), (UP, 0, 2, 0), (UP, 2, 0, 0), (DOWN, 2, 1, 1), (UP, 2, 1, 1), (UP, 1, 2, 1)),
-    (3, 3): ((DOWN, 0, 2, 0), (DOWN, 0, 3, 1)),
+    (2, 5): ((UP, 0, 2, 0), (UP, 2, 0, 1), (UP, 0, 3, 1)),
+    (3, 1): ((DOWN, 2, 0, 0), (DOWN, 1, 1, 0), (DOWN, 0, 2, 0), (UP, 2, 0, 0), (UP, 2, 1, 1), (DOWN, 2, 1, 1), (DOWN, 1, 2, 1), (DOWN, 0, 3, 1)),
+    (3, 3): ((UP, 1, 1, 0), (UP, 0, 3, 0), (UP, 1, 2, 1), (UP, 0, 4, 1)),
     (3, 4): ((DOWN, 3, 0, 1),),
-    (3, 5): ((UP, 1, 2, 0), (UP, 3, 0, 1), (DOWN, 1, 2, 1)),
-    (4, 1): ((UP, 1, 3, 1),),
-    (4, 4): ((DOWN, 3, 0, 0), (DOWN, 2, 1, 0), (UP, 2, 1, 0)),
-    (4, 5): ((DOWN, 0, 3, 0), (UP, 3, 0, 0), (GATE, 0, 0, 1), (UP, 0, 3, 1)),
-    (4, 7): ((DOWN, 1, 2, 0), (GATE, 1, 0, 1)),
+    (3, 5): ((DOWN, 0, 3, 0), (UP, 3, 0, 1), (DOWN, 0, 4, 1)),
+    (4, 3): ((UP, 0, 4, 0), (UP, 0, 5, 1)),
+    (4, 4): ((DOWN, 3, 0, 0), (DOWN, 1, 2, 0), (DOWN, 1, 3, 1)),
+    (4, 5): ((DOWN, 2, 1, 0), (UP, 3, 0, 0), (UP, 1, 2, 0), (GATE, 0, 0, 1), (DOWN, 2, 2, 1)),
+    (4, 7): ((GATE, 1, 0, 1),),
+    (4, 8): ((UP, 0, 5, 0),),
 }
 FEED_LEFT = (
+    (UP, 3, 0, True),
     (DOWN, 3, 0, True),
-    (UP, 3, 0, True),
-    (DOWN, 2, 1, True),
-    (DOWN, 1, 2, True),
-    (UP, 2, 1, True),
-    (DOWN, 0, 3, True),
-    (UP, 1, 3, False),
+    (UP, 1, 2, True),
+    (UP, 2, 1, False),
+    (DOWN, 0, 4, False),
     (GATE, 0, 0, False),
-    (UP, 0, 3, False),
+    (DOWN, 1, 3, False),
     (GATE, 1, 0, False),
+    (DOWN, 2, 2, False),
 )
 
 
 def ffn_body(
-    length_ref, a_two_ref, cot_ref, gain_ref, up_ref, down_ref, hidden_hbm, wout_hbm, state_hbm, q_hbm, a_one_hbm,
+    lengths_ref, a_two_ref, cot_ref, gain_ref, up_ref, down_ref, hidden_hbm, wout_hbm, state_hbm, q_hbm, a_one_hbm,
     out_hbm, d_hidden_hbm, d_query_hbm, d_state_hbm, gain_grad_ref, up_out, down_out, *rest,
 ):
     left = rest[: len(FEED_LEFT)]
@@ -680,7 +697,7 @@
     quarters = 4
     length, width = a_two_ref.shape
     tile = up_ref.shape[1]
-    live = length_ref[0]
+    live = lengths_ref[lax.axis_index("seq")]
     rows_count = 256
 
     sums = {}
@@ -693,7 +710,7 @@
         return taken
 
     for t in range(quarters):
-        order, sideways = ORDER[UP][t], ORDER[DOWN][t] == "Y"
+        order, gather = ORDER[UP][t], ORDER[DOWN][t]
 
         def keep_up(own, given, sideways, t=t):
             put(up_out, t * tile, own, given, sideways)
@@ -701,10 +718,10 @@
         def keep_down(own, given, sideways):
             put(down_out, 0, own, given, sideways)
 
-        refs = [up_bases[order in "XZ"]] + take(6 if order in "XZ" else 5)
+        refs = [up_bases["y" in order]] + take(len(order) + 2)
         sums[UP, t] = Sum(refs, up_sems.at[t], order, keep_up)
-        refs = [down_bases[sideways]] + take(6 if sideways else 5)
-        sums[DOWN, t] = Gather(t, refs, down_sems.at[t], sideways, keep_down)
+        refs = [down_bases["y" in gather]] + take(len(gather) + 4)
+        sums[DOWN, t] = Gather(t, refs, down_sems.at[t], gather, keep_down)
     for i in range(2):
         sums[GATE, i] = Sum([gate_base.at[i]] + take(5), gate_sems.at[i], ORDER[GATE][i])
 
@@ -766,7 +783,7 @@
 
     share = tile // 4
     for sideways in (False, True):
-        steps = [t for t in range(quarters) if (ORDER[DOWN][t] == "Y") == sideways]
+        steps = [t for t in range(quarters) if ("y" in ORDER[DOWN][t]) == sideways]
 
         @pl.when(functools.reduce(jnp.logical_or, [j == t for t in steps], False))
         def _(sideways=sideways):
@@ -783,7 +800,7 @@
     slots(4)
 
     for sideways in (False, True):
-        steps = [t for t in range(quarters) if (ORDER[UP][t] in "XZ") == sideways]
+        steps = [t for t in range(quarters) if ("y" in ORDER[UP][t]) == sideways]
 
         @pl.when(functools.reduce(jnp.logical_or, [j == t for t in steps], False))
         def _(sideways=sideways):
@@ -809,7 +826,7 @@
             normed, inv = norm_stats(before)
             grad_in = back[rows, :]
             gain_sum = gain_sum + jnp.sum(grad_in * normed, axis=0, keepdims=True)
-            d_hidden = cot_ref[rows, :].astype(F32) + norm_pull(grad_in, normed, inv, gain_ref[...])
+            d_hidden = cot_ref[rows, :].astype(F32) + norm_pull(grad_in, normed, inv, row_of(gain_ref))
             back[rows, :] = d_hidden
             d_down[rows, :] = (mask * d_hidden).astype(BF16)
             gated = q[rows, :].astype(F32) * state[rows, :].astype(F32)
@@ -848,7 +865,7 @@
             copy.wait()
 
 
-def ffn_call(live, a_two, cot, hidden, gain, up, down, wout, state, q, a_one):
+def ffn_call(lengths, a_two, cot, hidden, gain, up, down, wout, state, q, a_one):
     length, width = a_two.shape
     hidden_units = up.shape[1]
     tile = hidden_units // 4
@@ -863,7 +880,7 @@
     shape_of = {}
     for t in range(4):
         shape_of[UP, t] = landings(su, tile, ORDER[UP][t])
-        shape_of[DOWN, t] = gather_landings(sd, width, ORDER[DOWN][t] == "Y")
+        shape_of[DOWN, t] = gather_landings(sd, width, ORDER[DOWN][t])
     for i in range(2):
         shape_of[GATE, i] = landings(su, width, ORDER[GATE][i])
     left = [low(*shape_of[name, index][exchange].shape) for name, index, exchange, _ in FEED_LEFT]
@@ -878,7 +895,7 @@
             pl.BlockSpec(memory_space=pltpu.SMEM),
             rows_full,
             rows_full,
-            once((1, width)),
+            once((width,)),
             pl.BlockSpec((width, tile), lambda j: (0, jnp.minimum(j, 3))),
             pl.BlockSpec((tile, width), lambda j: (jnp.minimum(j, 3), 0)),
         ]
@@ -907,11 +924,11 @@
             vmem(length, width),
             sems(5),
             sems(4 + len(left)),
-            vmem(*base_shape(su, tile, "x")) if set(ORDER[UP]) & set("xz") else vmem(16, LANES),
-            vmem(*base_shape(su, tile, "X")) if set(ORDER[UP]) & set("XZ") else vmem(16, LANES),
-            vmem(2, 2, sd, width) if "n" in ORDER[DOWN] else vmem(16, LANES),
-            vmem(2, 2, 2, sd, width // 2) if "Y" in ORDER[DOWN] else vmem(16, LANES),
-            vmem(2, *base_shape(su, width, "x")),
+            vmem(*base_shape(su, tile, "")) if any("y" not in order for order in ORDER[UP]) else vmem(16, LANES),
+            vmem(*base_shape(su, tile, "y")) if any("y" in order for order in ORDER[UP]) else vmem(16, LANES),
+            vmem(2, 2, sd, width) if any("y" not in order for order in ORDER[DOWN]) else vmem(16, LANES),
+            vmem(2, 2, 2, sd, width // 2) if any("y" in order for order in ORDER[DOWN]) else vmem(16, LANES),
+            vmem(2, *base_shape(su, width, "")),
             sems(4, 6, 2),
             sems(4, 6, 2),
             sems(2, 5, 2),
@@ -920,145 +937,133 @@
         compiler_params=pltpu.CompilerParams(vmem_limit_bytes=62 * 1024 * 1024, collective_id=1, has_side_effects=True),
         cost_estimate=cost(12 * length * width * hidden_units, 40e6),
         name="feed_forward",
-    )(live, a_two, cot, gain, up, down, hidden, wout, state, q, a_one)
+    )(lengths, a_two, cot, gain, up, down, hidden, wout, state, q, a_one)
 
 
 BACK_PLAN = {
-    (0, 0): ((OUT, 0, 0, 1), (OUT, 1, 0, 1), (UP, 3, 1, 1), (GATE, 0, 1, 1), (GATE, 1, 1, 1), (DOWN, 1, 3, 1), (DOWN, 0, 4, 1)),
-    (1, 1): ((UP, 2, 2, 1),),
-    (2, 1): ((DOWN, 1, 3, 0),),
-    (2, 2): ((DOWN, 0, 4, 0),),
+    (0, 0): ((GATE, 0, 1, 1), (GATE, 1, 1, 1), (OUT, 0, 0, 1), (OUT, 1, 0, 1), (UP, 2, 2, 1), (UP, 1, 3, 1)),
+    (0, 1): ((DOWN, 2, 3, 1),),
+    (1, 1): ((DOWN, 1, 4, 1),),
+    (1, 2): ((UP, 1, 3, 0),),
+    (2, 1): ((UP, 2, 2, 0), (UP, 2, 3, 1)),
     (2, 3): ((KERN, 0, 0, 1),),
-    (3, 2): ((DOWN, 2, 2, 1), (DOWN, 1, 4, 1)),
-    (3, 4): ((UP, 3, 1, 0), (GATE, 0, 1, 0), (GATE, 1, 1, 0), (UP, 2, 2, 0), (KERN, 0, 0, 0), (KERN, 0, 1, 1), (UP, 3, 2, 1)),
-    (3, 5): ((DOWN, 3, 1, 1), (VALUE, 0, 0, 1), (KEY, 0, 0, 1), (GATE, 0, 2, 1), (DOWN, 0, 5, 1)),
-    (4, 2): ((OUT, 0, 0, 0), (OUT, 1, 0, 0), (DOWN, 2, 2, 0), (DOWN, 1, 4, 0)),
-    (4, 3): ((VALUE, 0, 0, 0), (KEY, 0, 0, 0), (VALUE, 0, 1, 1), (KEY, 0, 1, 1)),
-    (4, 4): ((DOWN, 2, 3, 1), (GATE, 1, 2, 1)),
-    (4, 5): ((DOWN, 0, 5, 0), (VALUE, 1, 0, 1), (KEY, 1, 0, 1)),
-    (5, 1): ((GATE, 0, 2, 0), (UP, 3, 2, 0), (UP, 3, 3, 1), (DOWN, 1, 5, 1)),
-    (5, 2): ((UP, 1, 4, 1),),
-    (5, 3): ((VALUE, 1, 0, 0), (KEY, 1, 0, 0), (VALUE, 0, 1, 0), (KEY, 0, 1, 0), (VALUE, 1, 1, 1), (KEY, 1, 1, 1), (VALUE, 0, 2, 1)),
-    (5, 4): ((KERN, 0, 1, 0), (DOWN, 3, 1, 0), (KERN, 0, 2, 1), (KEY, 0, 2, 1), (UP, 0, 4, 1)),
-    (5, 5): ((UP, 3, 3, 0), (DOWN, 3, 2, 1), (VALUE, 2, 0, 1), (TAPS, 0, 0, 1), (KEY, 2, 0, 1)),
-    (5, 7): ((UP, 1, 4, 0), (DOWN, 2, 3, 0), (GATE, 1, 2, 0), (DOWN, 2, 4, 1), (ROW, 0, 0, 1)),
-    (5, 8): ((DOWN, 1, 5, 0), (ROW, 1, 0, 1)),
-    (5, 9): ((VALUE, 0, 2, 0), (VALUE, 2, 0, 0), (TAPS, 0, 0, 0), (KEY, 2, 0, 0), (TAPS, 0, 1, 1)),
-    (5, 10): ((KEY, 0, 2, 0), (VALUE, 1, 1, 0), (KEY, 1, 1, 0), (UP, 0, 4, 0), (KEY, 2, 1, 1)),
-    (5, 11): ((GAIN, 0, 0, 1),),
+    (3, 1): ((DOWN, 2, 3, 0), (DOWN, 2, 4, 1)),
+    (3, 2): ((UP, 1, 4, 1),),
+    (3, 4): ((GATE, 0, 1, 0), (GATE, 1, 1, 0), (KERN, 0, 0, 0), (KERN, 0, 1, 1), (GATE, 0, 2, 1)),
+    (3, 5): ((DOWN, 1, 4, 0), (UP, 1, 4, 0), (UP, 3, 1, 1), (GATE, 1, 2, 1), (DOWN, 3, 1, 1), (KEY, 0, 0, 1)),
+    (3, 6): ((UP, 2, 3, 0), (UP, 2, 4, 1)),
+    (4, 2): ((OUT, 0, 0, 0), (OUT, 1, 0, 0)),
+    (4, 3): ((KEY, 0, 0, 0), (DOWN, 2, 4, 0)),
+    (4, 4): ((UP, 2, 4, 0), (KEY, 0, 1, 1)),
+    (4, 5): ((VALUE, 1, 0, 1), (KEY, 1, 0, 1)),
+    (5, 2): ((GATE, 1, 2, 0), (GATE, 0, 2, 0), (GATE, 1, 3, 1)),
+    (5, 3): ((VALUE, 1, 0, 0), (KEY, 1, 0, 0), (KERN, 0, 1, 0), (KERN, 0, 2, 1), (KEY, 1, 1, 1)),
+    (5, 4): ((UP, 1, 5, 1), (UP, 2, 5, 1)),
+    (5, 5): ((KEY, 0, 1, 0), (VALUE, 2, 0, 1), (GATE, 0, 3, 1), (KEY, 2, 0, 1), (KEY, 0, 2, 1)),
+    (5, 7): ((ROW, 0, 0, 1), (DOWN, 0, 5, 1)),
+    (5, 8): ((UP, 3, 1, 0), (DOWN, 3, 1, 0), (GATE, 1, 3, 0), (UP, 3, 2, 1), (DOWN, 3, 2, 1)),
+    (5, 9): ((KEY, 1, 1, 0), (VALUE, 2, 0, 0), (KEY, 2, 0, 0), (UP, 1, 5, 0), (UP, 2, 5, 0), (VALUE, 1, 1, 1)),
+    (5, 10): ((KEY, 2, 1, 1),),
+    (5, 11): ((ROW, 1, 0, 1), (TAPS, 0, 0, 1)),
 }
 BACK_LEFT = (
+    (KEY, 0, 2, 0),
+    (GATE, 0, 3, 0),
+    (KERN, 0, 2, 0),
+    (KERN, 0, 3, 1),
+    (TAPS, 0, 0, 0),
+    (DOWN, 0, 5, 0),
+    (VALUE, 2, 1, 1),
+    (TAPS, 0, 1, 1),
     (KEY, 1, 2, 1),
+    (VALUE, 1, 1, 0),
+    (KEY, 0, 3, 1),
+    (UP, 3, 2, 0),
     (DOWN, 3, 2, 0),
+    (UP, 3, 3, 1),
+    (KEY, 2, 1, 0),
     (VALUE, 1, 2, 1),
-    (GAIN, 0, 0, 0),
     (DOWN, 3, 3, 1),
-    (UP, 2, 3, 1),
-    (GAIN, 0, 1, 1),
-    (KERN, 0, 2, 0),
+    (KEY, 2, 2, 1),
+    (KEY, 1, 2, 0),
+    (KERN, 0, 3, 0),
+    (KEY, 1, 3, 1),
+    (KERN, 0, 4, 1),
+    (VALUE, 2, 1, 0),
     (TAPS, 0, 1, 0),
-    (DOWN, 2, 4, 0),
-    (KEY, 1, 2, 0),
-    (KERN, 0, 3, 1),
-    (KEY, 2, 1, 0),
+    (VALUE, 2, 2, 1),
+    (KEY, 0, 3, 0),
+    (UP, 3, 3, 0),
     (VALUE, 1, 2, 0),
-    (GAIN, 0, 1, 0),
+    (KEY, 2, 2, 0),
     (TAPS, 0, 2, 1),
-    (UP, 2, 3, 0),
-    (KEY, 2, 2, 1),
-    (GATE, 0, 3, 1),
+    (ROW, 0, 0, 0),
+    (UP, 3, 4, 1),
+    (GATE, 1, 4, 1),
+    (KEY, 1, 3, 0),
+    (VALUE, 1, 3, 1),
+    (GATE, 0, 4, 1),
+    (KEY, 2, 3, 1),
+    (VALUE, 2, 2, 0),
     (DOWN, 3, 3, 0),
-    (VALUE, 2, 1, 1),
+    (VALUE, 2, 3, 1),
+    (KERN, 0, 4, 0),
+    (COEF, 0, 0, 1),
+    (DOWN, 1, 5, 1),
     (DOWN, 3, 4, 1),
     (TAPS, 0, 2, 0),
+    (TAPS, 0, 3, 1),
     (DOWN, 2, 5, 1),
-    (KERN, 0, 3, 0),
-    (GATE, 1, 3, 1),
-    (ROW, 0, 0, 0),
-    (KERN, 0, 4, 1),
-    (KEY, 2, 2, 0),
     (ROW, 1, 0, 0),
-    (UP, 3, 4, 1),
-    (UP, 2, 4, 1),
-    (VALUE, 2, 1, 0),
-    (GATE, 0, 3, 0),
-    (VALUE, 2, 2, 1),
-    (GAIN, 0, 2, 1),
-    (VALUE, 0, 3, 1),
+    (COEF, 0, 0, 0),
+    (COEF, 0, 1, 1),
+    (UP, 3, 4, 0),
+    (GATE, 1, 4, 0),
+    (VALUE, 1, 3, 0),
+    (UP, 3, 5, 1),
+    (VALUE, 2, 3, 0),
+    (KEY, 2, 3, 0),
+    (GATE, 0, 4, 0),
+    (VALUE, 1, 4, 1),
+    (VALUE, 2, 4, 1),
+    (KEY, 0, 4, 1),
+    (KEY, 1, 4, 1),
+    (TAPS, 0, 3, 0),
+    (DOWN, 1, 5, 0),
+    (COEF, 0, 1, 0),
+    (COEF, 0, 2, 1),
+    (TAPS, 0, 4, 1),
+    (UP, 3, 5, 0),
+    (KEY, 2, 4, 1),
     (DOWN, 2, 5, 0),
-    (KERN, 0, 4, 0),
-    (COEF, 0, 0, 1),
-    (GATE, 0, 4, 1),
-    (VALUE, 1, 3, 1),
-    (TAPS, 0, 3, 1),
-    (VALUE, 2, 2, 0),
-    (VALUE, 2, 3, 1),
-    (KEY, 0, 3, 1),
-    (GATE, 1, 3, 0),
-    (GATE, 1, 4, 1),
-    (COEF, 0, 0, 0),
-    (GAIN, 0, 2, 0),
-    (COEF, 0, 1, 1),
-    (GAIN, 0, 3, 1),
-    (UP, 3, 4, 0),
-    (UP, 2, 4, 0),
-    (KEY, 1, 3, 1),
-    (VALUE, 0, 3, 0),
     (DOWN, 3, 4, 0),
     (DOWN, 3, 5, 1),
-    (VALUE, 1, 3, 0),
-    (GATE, 0, 4, 0),
-    (KEY, 2, 3, 1),
-    (VALUE, 0, 4, 1),
-    (VALUE, 2, 3, 0),
-    (TAPS, 0, 3, 0),
-    (TAPS, 0, 4, 1),
-    (VALUE, 1, 4, 1),
-    (GATE, 1, 4, 0),
-    (COEF, 0, 1, 0),
-    (KEY, 0, 3, 0),
-    (COEF, 0, 2, 1),
-    (KEY, 0, 4, 1),
-    (VALUE, 2, 4, 1),
-    (GAIN, 0, 3, 0),
-    (GAIN, 0, 4, 1),
-    (KEY, 1, 3, 0),
-    (KEY, 1, 4, 1),
+    (VALUE, 1, 4, 0),
+    (VALUE, 2, 4, 0),
+    (KEY, 1, 4, 0),
+    (COEF, 0, 2, 0),
+    (COEF, 0, 3, 1),
+    (KEY, 0, 4, 0),
     (TAPS, 0, 4, 0),
-    (VALUE, 0, 4, 0),
-    (VALUE, 0, 5, 1),
+    (KEY, 2, 4, 0),
     (DOWN, 3, 5, 0),
-    (KEY, 0, 4, 0),
-    (KEY, 2, 3, 0),
-    (KEY, 2, 4, 1),
-    (COEF, 0, 2, 0),
-    (VALUE, 1, 4, 0),
-    (COEF, 0, 3, 1),
-    (VALUE, 1, 5, 1),
-    (VALUE, 2, 4, 0),
-    (VALUE, 2, 5, 1),
-    (GAIN, 0, 4, 0),
-    (KEY, 1, 4, 0),
-    (VALUE, 0, 5, 0),
-    (KEY, 2, 4, 0),
-    (VALUE, 1, 5, 0),
-    (VALUE, 2, 5, 0),
     (COEF, 0, 3, 0),
 )
 
 
 def mixer_back_body(
-    length_ref, out_row_ref, d_state_ref, d_query_ref, mixed_ref, shifted_ref, k_ref, v_ref,
+    lengths_ref, out_row_ref, d_state_ref, d_query_ref, mixed_ref, shifted_ref, k_ref, v_ref,
     wq_ref, wk_ref, wv_ref, kern_ref, tapspec_ref, table_ref, back_ref, gain_ref, gain_two_grad_ref,
     coef_ref, rate_ref, up_part_ref, down_part_ref, *rest,
 ):
     left = rest[: len(FEED_LEFT)]
     (
         a_one_hbm, x_hbm, d_hidden_hbm,
-        out_ref, d_tokens_ref, gains_out, taps_out, coef_out, rate_out, up_ref, down_ref, gate_out, kv_out,
+        out_ref, d_tokens_ref, gain_one_out, gain_two_out, taps_out, coef_out, rate_out, up_ref, down_ref,
+        wout_out, query_out, key_out, value_out,
         total, spec_one, spec_two, prod, shift_prod, d_keys, d_values, d_x, a_one, x, d_hidden, d_taps, d_kern,
-        gain_refs, gain_lands, gain_sems, taps_base, taps_sems, coef_base, coef_sems,
-        kern_base, key_base, value_base, left_sems, kern_sems, kv_sems, out_sems, row_sems, own_sems, in_sems, *lands,
+        taps_base, taps_sems, coef_base, coef_sems,
+        kern_base, kv_base, left_sems, kern_sems, kv_sems, out_sems, row_sems, own_sems, in_sems, *lands,
     ) = rest[len(FEED_LEFT) :]
     j = pl.program_id(0)
     length, width = a_one.shape
@@ -1066,13 +1071,12 @@
     tile = k_ref.shape[1]
     tiles = width // tile
     blocks = length // BLOCK
-    live = length_ref[0]
     side = lax.axis_index("seq")
+    live = lengths_ref[side]
     own_rows = pl.ds(pl.multiple_of(side * half, half), half)
 
     sums = {}
     lands = list(lands)
-    kv_bases = (key_base, value_base)
 
     def take(count):
         taken = lands[:count]
@@ -1087,12 +1091,12 @@
             elif name == DOWN:
                 put(down_ref, 0, own, given, sideways)
             else:
-                put(gate_out.at[index], 0, own, given, sideways)
+                put((wout_out, query_out)[index], 0, own, given, sideways)
 
         order = ORDER[name][index]
-        refs = [None] * (exchange + 1) + [left[i]] + take((5 if order in "XZY" else 4) - exchange)
+        refs = [None] * (exchange + 1) + [left[i]] + take(len(order) + (3 if name == DOWN else 1) - exchange)
         if name == DOWN:
-            sums[name, index] = Gather(index, refs, left_sems.at[i], order == "Y", keep)
+            sums[name, index] = Gather(index, refs, left_sems.at[i], order, keep)
         else:
             sums[name, index] = Sum(refs, left_sems.at[i], order, keep)
 
@@ -1127,35 +1131,48 @@
                 coef_base[(*place, slice(each, 2 * each), lanes)] = rate_sum[rows]
 
     def keep_coef(value):
-        flat = jnp.transpose(value)
-        coef_out[...] = flat[:, :each]
-        rate_out[...] = flat[:, each:]
+        coef_out[...] = value[:each]
+        rate_out[...] = value[each:]
 
     def keep_taps(own, given, sideways):
-        both = jnp.concatenate([own + given] * 2, axis=0)
-        flat = jnp.where(side == 0, both[:, :channels], both[:, channels:])
-        taps_out[...] = jnp.transpose(flat)[:, :each]
-
-    sums[COEF, 0] = Sum([coef_base] + take(4), coef_sems, "x", keep_coef, across=False)
-    sums[TAPS, 0] = Sum([taps_base] + take(5), taps_sems, "x", keep_taps)
-    sums[GAIN, 0] = Whole(gain_refs, gain_lands, gain_sems)
+        both = own + given
+        taps_out[...] = jnp.where(side == 0, both[:each, :channels], both[:each, channels:])
+        gain_each = gain_one_out.shape[1]
+        gains = pltpu.roll(both, width - lax.axis_index("dp") * gain_each, 1)
+        gain_one_out[...] = gains[each : each + 1, :gain_each]
+        gain_two_out[...] = gains[each + 1 : each + 2, :gain_each]
+
+    sums[COEF, 0] = Sum([coef_base] + take(4), coef_sems, "xnf", keep_coef, across=False)
+    sums[TAPS, 0] = Sum([taps_base] + take(5), taps_sems, "xnf", keep_taps)
 
     for i in range(2):
         piece = pl.ds(i * (half // 2), half // 2)
         other = pl.ds(pl.multiple_of((1 - side) * half + i * (half // 2), half // 2), half // 2)
         sums[OUT, i] = Rows(out_row_ref.at[other], out_ref.at[side, piece], out_sems.at[i])
         sums[ROW, i] = Rows(d_x.at[0, piece], d_tokens_ref.at[side, piece], row_sems.at[i])
-    kern_sideways = ORDER[KERN] in "XZ"
-    sums[KERN, 0] = Sum([kern_base] + take(6 if kern_sideways else 5), kern_sems, ORDER[KERN], keep_kern)
+    kern_sideways = "y" in ORDER[KERN]
+    sums[KERN, 0] = Sum([kern_base] + take(len(ORDER[KERN]) + 2), kern_sems, ORDER[KERN], keep_kern)
+    share = width // 16
     for t in range(tiles):
-        for i, name in enumerate((KEY, VALUE)):
-
-            def keep_kv(own, given, sideways, t=t, i=i):
-                put(kv_out.at[i], t * tile, own, given, sideways)
-
-            order = ORDER[KV][i]
-            refs = [kv_bases[i].at[t]] + take(6 if order in "XZ" else 5)
-            sums[name, t] = Sum(refs, kv_sems.at[t, i], order, keep_kv)
+
+        def keep_both(own, given, sideways, t=t):
+            for i, target in enumerate((key_out, value_out)):
+                part = slice(i * share, (i + 1) * share)
+                put(target, t * tile, own[part], given[part], sideways)
+
+        def keep_key(own, given, sideways, t=t):
+            put(key_out, t * tile, own, given, sideways)
+
+        def keep_value(own, given, sideways, t=t):
+            put(value_out, t * tile, own, given, sideways)
+
+        orders = ORDER[KV][t]
+        if len(orders) == 1:
+            sums[KEY, t] = Sum([kv_base.at[t]] + take(5), kv_sems.at[t, 0], orders[0], keep_both)
+        else:
+            for i, (name, keep) in enumerate(((KEY, keep_key), (VALUE, keep_value))):
+                part = kv_base.at[t, :, :, :, :, i * share : (i + 1) * share]
+                sums[name, t] = Sum([part] + take(5), kv_sems.at[t, i], orders[i], keep)
 
     def events(step, number):
         follow(sums, BACK_PLAN.get((step, number), ()))
@@ -1316,13 +1333,8 @@
         taps = d_taps.shape[0]
         columns = pl.ds(pl.multiple_of((j - tiles) * tile, tile), tile)
         d_taps[:, columns] = dot(back_ref[:taps, :], shift_prod[...]) * (1.0 / BLOCK)
-        spread(dot_tn(a_one[...], d_keys[...]), key_base.at[j - tiles], ORDER[KV][0] in "XZ")
-        spread(dot_tn(a_one[...], d_values[...]), value_base.at[j - tiles], ORDER[KV][1] in "XZ")
-
-    @pl.when(j == 2 * tiles - 1)
-    def _():
-        for owner, place in enumerate(places(lax.axis_index("dp"), 16, (1, 2, 4, 8))):
-            taps_base[place] = d_taps[owner * each : (owner + 1) * each, :]
+        for i, source in enumerate((d_keys, d_values)):
+            spread(dot_tn(a_one[...], source[...]), kv_base.at[j - tiles, :, :, :, :, i * share : (i + 1) * share])
 
     slots(tiles, 2 * tiles, 5)
 
@@ -1346,20 +1358,22 @@
             normed, inv = norm_stats(x[rows, :].astype(F32))
             grad_in = token_grad(rows)
             gain_sum = gain_sum + jnp.sum(grad_in * normed, axis=0, keepdims=True)
-            pulled = d_hidden[rows, :] + norm_pull(grad_in, normed, inv, gain_ref[...])
+            pulled = d_hidden[rows, :] + norm_pull(grad_in, normed, inv, row_of(gain_ref))
             d_x[b // count, (b % count) * BLOCK : (b % count + 1) * BLOCK, :] = pulled.astype(BF16)
             events(2 * tiles - 1, 7 + b)
         keep_row().start()
-        gain_refs[0] = jnp.concatenate([gain_sum, gain_two_grad_ref[...], jnp.zeros((6, width), F32)], axis=0)
+        gains = jnp.concatenate([gain_sum, gain_two_grad_ref[...], jnp.zeros((6 - each, width), F32)], axis=0)
+        for owner, place in enumerate(places(lax.axis_index("dp"), 16, (1, 2, 4, 8))):
+            taps_base[(*place, slice(0, each))] = d_taps[owner * each : (owner + 1) * each, :]
+            taps_base[(*place, slice(each, 8))] = gains
         events(2 * tiles - 1, 11)
         follow(sums, BACK_LEFT)
-        gains_out[...] = gain_refs[5]
         keep_out().wait()
         keep_row().wait()
 
 
 def mixer_back_call(
-    live, out_row, a_one, d_state, d_query, mixed, shifted, k, v, wq, wk, wv, kern, tapspec, tables, x, gain, d_hidden,
+    lengths, out_row, a_one, d_state, d_query, mixed, shifted, k, v, wq, wk, wv, kern, tapspec, tables, x, gain, d_hidden,
     d_gain_two, coef, rate, begun, taps_count, tile,
 ):
     length, width = a_one.shape
@@ -1387,26 +1401,31 @@
     for name, index, exchange, _ in FEED_LEFT:
         order = ORDER[name][index]
         if name == DOWN:
-            lands += gather_landings(*down_part.shape, order == "Y")[exchange + 1 :]
+            lands += gather_landings(*down_part.shape, order)[exchange + 1 :]
         else:
             lands += landings(share, width, order)[exchange + 1 :]
     bits = [(2, 2, 2), (2, 2), (2,), (), ()]
     lands += [wide(*bits[n], 2 * each, channels) for n in range(4)]
-    lands += [wide(*bits[n], each, width) for n in range(5)]
+    lands += [wide(*bits[n], 8, width) for n in range(5)]
     lands += landings(ks, width, ORDER[KERN])
     for t in range(count):
-        lands += landings(share, tile, ORDER[KV][0]) + landings(share, tile, ORDER[KV][1])
+        orders = ORDER[KV][t]
+        for order in orders:
+            lands += landings(2 * share // len(orders), tile, order)
     out_shape = [
         low(2, half, width),
         low(2, half, width),
-        full(8, width),
-        full(channels, each),
-        full(channels, each),
-        full(channels, each),
+        full(1, width // 16),
+        full(1, width // 16),
+        full(each, channels),
+        full(each, channels),
+        full(each, channels),
         full(*up_part.shape),
         full(*down_part.shape),
-        full(2, share, width),
-        full(2, share, width),
+        full(share, width),
+        full(share, width),
+        full(share, width),
+        full(share, width),
     ]
     return pl.pallas_call(
         mixer_back_body,
@@ -1420,7 +1439,7 @@
             pl.BlockSpec((2 * BLOCK, tile), second),
             once(table.shape),
             once(back.shape),
-            once((1, width)),
+            once((width,)),
             once((1, width)),
             once(coef.shape),
             once(rate.shape),
@@ -1445,16 +1464,12 @@
             wide(length, width),
             wide(taps_count, width),
             wide(ks, width),
-            wide(6, 8, width),
-            wide(5, 8, width),
-            sems(5, 2),
-            wide(2, 2, 2, 2, each, width),
+            wide(2, 2, 2, 2, 8, width),
             sems(5, 2),
             wide(2, 2, 2, 2, 2 * each, channels),
             sems(4, 2),
             vmem(*base_shape(ks, width, ORDER[KERN])),
-            vmem(count, *base_shape(share, tile, ORDER[KV][0])),
-            vmem(count, *base_shape(share, tile, ORDER[KV][1])),
+            vmem(count, *base_shape(2 * share, tile, "")),
             sems(len(left), 6, 2),
             sems(6, 2),
             sems(count, 2, 6, 2),
@@ -1470,7 +1485,7 @@
         cost_estimate=cost(26e9, 40e6),
         name="mixer_back",
     )(
-        live, out_row, d_state, d_query, mixed, shifted, k, v, wq, wk, wv, kern, tapspec, table, back, gain,
+        lengths, out_row, d_state, d_query, mixed, shifted, k, v, wq, wk, wv, kern, tapspec, table, back, gain,
         d_gain_two, coef, rate, up_part, down_part, *left, a_one, x, d_hidden,
     )
 
@@ -1778,49 +1793,69 @@
     )
 
 
+def settle_body(*refs):
+    count = (len(refs) - 1) // 3
+    sources, targets, held, sems = refs[:count], refs[count : 2 * count], refs[2 * count : 3 * count], refs[-1]
+    reads = [pltpu.make_async_copy(sources[i], held[i], sems.at[0, i]) for i in range(count)]
+    writes = [pltpu.make_async_copy(held[i], targets[i], sems.at[1, i]) for i in range(count)]
+    for copy in reads:
+        copy.start()
+    for read, write in zip(reads, writes):
+        read.wait()
+        write.start()
+    for copy in writes:
+        copy.wait()
+
+
+def settle_call(arrays):
+    anywhere = pl.BlockSpec(memory_space=pl.ANY)
+    return pl.pallas_call(
+        settle_body,
+        in_specs=[anywhere] * len(arrays),
+        out_specs=[anywhere] * len(arrays),
+        out_shape=[jax.ShapeDtypeStruct(array.shape, array.dtype) for array in arrays],
+        scratch_shapes=[pltpu.VMEM(array.shape, array.dtype) for array in arrays]
+        + [pltpu.SemaphoreType.DMA((2, len(arrays)))],
+        compiler_params=params(),
+        cost_estimate=cost(1e3, 10e6),
+        name="settle",
+    )(*arrays)
+
+
 def split_rows(
     tokens, lengths, gain_one, w_query, w_key, w_value, w_out, gain_two, w_up, w_down,
     shift_taps, diag_coef, diag_rate, cotangent,
 ):
-    side = lax.axis_index("seq")
-    mine = lax.axis_index("dp")
-    devices = lax.axis_size("dp")
-    width = tokens.shape[2]
-    length = tokens.shape[1] * 2
-    channels, states = diag_coef.shape
+    states = diag_coef.shape[1]
     tile = 256
     tables = transform_tables()
-    live = lax.dynamic_slice_in_dim(lengths, side, 1, 0)
-    packed = jnp.stack([diag_coef.T, diag_rate.T])
-    row_one = gain_one[None, :]
-    row_two = gain_two[None, :]
+    coef, rate, taps = diag_coef.T, diag_rate.T, shift_taps.T
     x, cot, a_one, q, k, v, kern, tapspec, hidden, a_two, shifted, mixed, state = mixer_call(
-        live, tokens, cotangent, packed, shift_taps.T.astype(BF16), row_one, row_two, w_query, w_key, w_value, w_out,
-        tables, tile,
+        lengths, tokens, cotangent, coef, rate, taps, gain_one, gain_two, w_query, w_key, w_value, w_out, tables, tile
     )
     out_row, d_hidden, d_query, d_state, d_gain_two, up_part, down_part, *left = ffn_call(
-        live, a_two, cot, hidden, row_two, w_up, w_down, w_out, state, q, a_one
+        lengths, a_two, cot, hidden, gain_two, w_up, w_down, w_out, state, q, a_one
     )
-    out, d_tokens, gains, taps_grad, coef_grad, rate_grad, up, down, gate, kv = mixer_back_call(
-        live, out_row, a_one, d_state, d_query, mixed, shifted, k, v, w_query, w_key, w_value, kern, tapspec, tables, x,
-        row_one, d_hidden, d_gain_two, packed[0], packed[1], (up_part, down_part, left), states, tile,
+    out, d_tokens, gain_one_grad, gain_two_grad, taps_grad, coef_grad, rate_grad, up, down, wout, query, key, value = (
+        settle_call(mixer_back_call(
+            lengths, out_row, a_one, d_state, d_query, mixed, shifted, k, v, w_query, w_key, w_value, kern, tapspec,
+            tables, x, gain_one, d_hidden, d_gain_two, coef, rate, (up_part, down_part, left), states, tile,
+        ))
     )
-    gain_each = width // devices
-    gains = lax.dynamic_slice_in_dim(gains, mine * gain_each, gain_each, 1)
     return (
         out,
         d_tokens,
-        gains[0],
-        gate[1],
-        kv[0],
-        kv[1],
-        gate[0],
-        gains[1],
+        gain_one_grad.reshape(-1),
+        query,
+        key,
+        value,
+        wout,
+        gain_two_grad.reshape(-1),
         up,
         down,
-        taps_grad,
-        coef_grad,
-        rate_grad,
+        taps_grad.T,
+        coef_grad.T,
+        rate_grad.T,
     )
 
 

time: 216 us -> 197 us (0.912)
  local copies, waits for them, and re-layouts: 17.1 us -> 0 us
  other arithmetic: 3.15 us -> 0 us
    unnamed x15 -> x0, local copies, waits for them, and re-layouts: 9.93 us -> none
    pallas_call x0 -> x1, Pallas kernels: none -> 3.89 us  [settle_call(): pl.pallas_call(settle_body, in_specs=[anywhere] * len(arrays), out_specs=...]
    pallas_call x1, Pallas kernels: 85.2 us -> 81.6 us  [mixer_back_call(): pl.pallas_call(mixer_back_body, grid=(2 * count,), in_specs=[pl.BlockSpec...]
    broadcast_in_dim x2 -> x0, local copies, waits for them, and re-layouts: 2.53 us -> none  [the longest x1 1.27 us: split_rows(): row_one = gain_one[None, :]]
    squeeze x2 -> x0, local copies, waits for them, and re-layouts: 2.46 us -> none  [the longest x1 1.94 us: split_rows(): gate[0]]
where the time goes in v4:
time: 197 us
  Pallas kernels  196 us (99%)
    pallas_call x1, Pallas kernels, mixer_back_call(): pl.pallas_call(mixer_back_body, grid=(2 * count,), in_specs=[pl.BlockSpec...  81.6 us
    pallas_call x1, Pallas kernels, ffn_call(): pl.pallas_call(ffn_body, grid=(5,), in_specs=[pl.BlockSpec(memory_space=p...  61.4 us
    pallas_call x1, Pallas kernels, mixer_call(): pl.pallas_call(mixer_body, grid=(1 + width // tile,), in_specs=[pl.BlockS...  49.2 us

profile of v4, /device:TPU:0, one launch (start us, length us, event | category | flops | bytes accessed | tf_op | source)
XLA Modules:
  0.0 196.9 jit_solution(2174665020275036725)
XLA Ops:
  0.6 49.2 %mixer_forward.1 = (bf16[1024,768]{1,0:T(8,128)(2,1)}, bf16[1024,768]{1,0:T(8,128)(2,1)}, bf16[1024,768]{1,0:T(8,128)(2,1)}, bf16[1024,768]{1,0:T(8,128)(2,1)}, ...) custom-call(s32[2]{0:T(128)} %lengths_ref.5, ...), custom_call_target="tpu_custom_call" | custom-call | flops 16000000000 | bytes 40000000 | tf_op jit(solution)/shard_map/mixer_forward/pallas_call | solution.py:592
  49.8 61.4 %feed_forward.1 = (bf16[1024,768]{1,0:T(8,128)(2,1)}, f32[1024,768]{1,0:T(8,128)}, bf16[1024,768]{1,0:T(8,128)(2,1)}, bf16[1024,768]{1,0:T(8,128)(2,1)}, f32[1,7...) custom-call(s32[2]{0:T(128)} %lengths_ref.5, ...), custom_call_target="tpu_custom_call" | custom-call | flops 28991029248 | bytes 40000000 | tf_op jit(solution)/shard_map/feed_forward/pallas_call | solution.py:891
  111.3 81.6 %mixer_back.1 = (bf16[2,512,768]{2,1,0:T(8,128)(2,1)}, bf16[2,512,768]{2,1,0:T(8,128)(2,1)}, f32[1,48]{1,0:T(1,128)}, f32[1,48]{1,0:T(1,128)}, f32[4,384]{1,0:T(...) custom-call(s32[2]{0:T(128)} %lengths_ref.5, ...), custom_call_target="tpu_custom_call" | custom-call | flops 25999998976 | bytes 40000000 | tf_op jit(solution)/shard_map/mixer_back/pallas_call | solution.py:1430
  192.9 3.9 %settle.1 = (bf16[2,512,768]{2,1,0:T(8,128)(2,1)}, bf16[2,512,768]{2,1,0:T(8,128)(2,1)}, f32[1,48]{1,0:T(1,128)}, f32[1,48]{1,0:T(1,128)}, f32[4,384]{1,0:T(4,12...) custom-call(bf16[2,512,768]{2,1,0:T(8,128)(2,1)} %get-tuple-element., ...), custom_call_target="tpu_custom_call" | custom-call | flops 1000 | bytes 10000000 | tf_op jit(solution)/shard_map/settle/pallas_call | solution.py:1812

commit v5 on v4

--- a/solution.py
+++ b/solution.py
@@ -440,12 +440,12 @@
         greet((CORE, SIDE))
         for copy in other_params:
             copy.start()
-        for copy in other_x:
-            copy.start()
         taps[:, own_lanes] = taps_ref[...].astype(BF16)
         other_taps.start()
         total[...] = jnp.zeros_like(total)
         unit(0)
+        for copy in other_x:
+            copy.start()
         unit(1)
         unit(2)
         for copy in weights:
@@ -651,47 +651,53 @@
     )(lengths, tokens, cot, coef, rate, taps, gain_one, gain_two, wq, wk, wv, wout, table, back)
 
 
-ORDER = {UP: ["ynfx", "ynfx", "ynfx", "yxnf"], DOWN: ["xy", "xy", "xy", "yx"], GATE: ["xfn", "xnf"], KERN: "xnf", KV: [["nxf"], ["xnf", "nxf"], ["nxf", "xfn"]]}
+FIRST_ROWS = 128
+
+ORDER = {UP: ["nyfx", "nfyx", "yxnf", "xynf"], DOWN: ["yx", "yx", "xy", "yx"], GATE: ["nfx", "xnf"], KERN: ["xnf", "nxf", "xnf"], KV: [["xnf"], ["xnf"], ["xnf", "xfn"]]}
 FEED_PLAN = {
     (0, 4): ((DOWN, 0, 0, 1),),
     (0, 5): ((UP, 0, 0, 1),),
     (1, 1): ((DOWN, 0, 0, 0), (UP, 0, 0, 0), (UP, 0, 1, 1), (DOWN, 0, 1, 1)),
     (1, 4): ((DOWN, 1, 0, 1),),
     (1, 5): ((UP, 1, 0, 1),),
-    (2, 1): ((DOWN, 1, 0, 0), (UP, 0, 1, 0), (DOWN, 0, 1, 0), (UP, 1, 0, 0), (UP, 1, 1, 1), (DOWN, 1, 1, 1), (UP, 0, 2, 1), (DOWN, 0, 2, 1)),
+    (2, 1): ((DOWN, 1, 0, 0), (UP, 0, 1, 0), (DOWN, 0, 1, 0), (UP, 1, 0, 0), (UP, 1, 1, 1), (DOWN, 1, 1, 1), (DOWN, 0, 2, 1)),
     (2, 4): ((DOWN, 2, 0, 1),),
-    (2, 5): ((UP, 0, 2, 0), (UP, 2, 0, 1), (UP, 0, 3, 1)),
-    (3, 1): ((DOWN, 2, 0, 0), (DOWN, 1, 1, 0), (DOWN, 0, 2, 0), (UP, 2, 0, 0), (UP, 2, 1, 1), (DOWN, 2, 1, 1), (DOWN, 1, 2, 1), (DOWN, 0, 3, 1)),
-    (3, 3): ((UP, 1, 1, 0), (UP, 0, 3, 0), (UP, 1, 2, 1), (UP, 0, 4, 1)),
+    (2, 5): ((UP, 2, 0, 1), (UP, 0, 2, 1)),
+    (3, 0): ((DOWN, 0, 2, 0), (DOWN, 0, 3, 1)),
+    (3, 1): ((DOWN, 2, 0, 0), (UP, 1, 1, 0), (DOWN, 1, 1, 0), (UP, 2, 0, 0), (UP, 2, 1, 1), (DOWN, 2, 1, 1)),
+    (3, 2): ((UP, 1, 2, 1),),
+    (3, 3): ((UP, 0, 2, 0),),
     (3, 4): ((DOWN, 3, 0, 1),),
-    (3, 5): ((DOWN, 0, 3, 0), (UP, 3, 0, 1), (DOWN, 0, 4, 1)),
-    (4, 3): ((UP, 0, 4, 0), (UP, 0, 5, 1)),
-    (4, 4): ((DOWN, 3, 0, 0), (DOWN, 1, 2, 0), (DOWN, 1, 3, 1)),
-    (4, 5): ((DOWN, 2, 1, 0), (UP, 3, 0, 0), (UP, 1, 2, 0), (GATE, 0, 0, 1), (DOWN, 2, 2, 1)),
-    (4, 7): ((GATE, 1, 0, 1),),
-    (4, 8): ((UP, 0, 5, 0),),
+    (3, 5): ((DOWN, 0, 3, 0), (UP, 3, 0, 1), (DOWN, 1, 2, 1)),
+    (4, 2): ((UP, 0, 3, 1),),
+    (4, 3): ((OUT, 2, 0, 1),),
+    (4, 4): ((DOWN, 3, 0, 0),),
+    (4, 5): ((UP, 2, 1, 0), (DOWN, 2, 1, 0), (UP, 3, 0, 0), (GATE, 0, 0, 1)),
+    (4, 7): ((UP, 1, 2, 0), (GATE, 1, 0, 1)),
+    (4, 8): ((OUT, 2, 0, 0),),
 }
 FEED_LEFT = (
     (UP, 3, 0, True),
     (DOWN, 3, 0, True),
+    (UP, 2, 1, True),
+    (DOWN, 2, 1, True),
     (UP, 1, 2, True),
-    (UP, 2, 1, False),
-    (DOWN, 0, 4, False),
+    (DOWN, 0, 3, True),
+    (DOWN, 1, 2, False),
     (GATE, 0, 0, False),
-    (DOWN, 1, 3, False),
+    (UP, 0, 3, False),
     (GATE, 1, 0, False),
-    (DOWN, 2, 2, False),
 )
 
 
 def ffn_body(
     lengths_ref, a_two_ref, cot_ref, gain_ref, up_ref, down_ref, hidden_hbm, wout_hbm, state_hbm, q_hbm, a_one_hbm,
-    out_hbm, d_hidden_hbm, d_query_hbm, d_state_hbm, gain_grad_ref, up_out, down_out, *rest,
+    out_hbm, d_hidden_hbm, d_query_hbm, d_state_hbm, out_first_hbm, gain_grad_ref, up_out, down_out, *rest,
 ):
     left = rest[: len(FEED_LEFT)]
     (
         total, back, act, d_pre, d_down, hidden, wout, state, q, a_one, in_sems, out_sems,
-        up_flat, up_side, down_flat, down_side, gate_base, up_sems, down_sems, gate_sems, *lands,
+        up_flat, up_side, down_flat, down_side, gate_base, up_sems, down_sems, gate_sems, row_sems, *lands,
     ) = rest[len(FEED_LEFT) :]
     j = pl.program_id(0)
     quarters = 4
@@ -724,6 +730,10 @@
         sums[DOWN, t] = Gather(t, refs, down_sems.at[t], gather, keep_down)
     for i in range(2):
         sums[GATE, i] = Sum([gate_base.at[i]] + take(5), gate_sems.at[i], ORDER[GATE][i])
+
+    half = length // 2
+    first = pl.ds(pl.multiple_of((1 - lax.axis_index("seq")) * half, half), out_first_hbm.shape[0])
+    sums[OUT, 2] = Rows(d_pre.at[first], out_first_hbm, row_sems)
 
     def run(step, number):
         follow(sums, FEED_PLAN.get((step, number), ()))
@@ -900,12 +910,13 @@
             pl.BlockSpec((tile, width), lambda j: (jnp.minimum(j, 3), 0)),
         ]
         + [anywhere] * 5,
-        out_specs=[anywhere] * 4 + [once((1, width)), once((su, hidden_units)), once((sd, width))] + [anywhere] * len(left),
+        out_specs=[anywhere] * 5 + [once((1, width)), once((su, hidden_units)), once((sd, width))] + [anywhere] * len(left),
         out_shape=[
             low(length, width),
             full(length, width),
             low(length, width),
             low(length, width),
+            low(FIRST_ROWS, width),
             full(1, width),
             full(su, hidden_units),
             full(sd, width),
@@ -932,6 +943,7 @@
             sems(4, 6, 2),
             sems(4, 6, 2),
             sems(2, 5, 2),
+            sems(2),
             *lands,
         ],
         compiler_params=pltpu.CompilerParams(vmem_limit_bytes=62 * 1024 * 1024, collective_id=1, has_side_effects=True),
@@ -940,114 +952,108 @@
     )(lengths, a_two, cot, gain, up, down, hidden, wout, state, q, a_one)
 
 
+KERN_LAST = 2
 BACK_PLAN = {
-    (0, 0): ((GATE, 0, 1, 1), (GATE, 1, 1, 1), (OUT, 0, 0, 1), (OUT, 1, 0, 1), (UP, 2, 2, 1), (UP, 1, 3, 1)),
-    (0, 1): ((DOWN, 2, 3, 1),),
-    (1, 1): ((DOWN, 1, 4, 1),),
-    (1, 2): ((UP, 1, 3, 0),),
-    (2, 1): ((UP, 2, 2, 0), (UP, 2, 3, 1)),
-    (2, 3): ((KERN, 0, 0, 1),),
-    (3, 1): ((DOWN, 2, 3, 0), (DOWN, 2, 4, 1)),
-    (3, 2): ((UP, 1, 4, 1),),
-    (3, 4): ((GATE, 0, 1, 0), (GATE, 1, 1, 0), (KERN, 0, 0, 0), (KERN, 0, 1, 1), (GATE, 0, 2, 1)),
-    (3, 5): ((DOWN, 1, 4, 0), (UP, 1, 4, 0), (UP, 3, 1, 1), (GATE, 1, 2, 1), (DOWN, 3, 1, 1), (KEY, 0, 0, 1)),
-    (3, 6): ((UP, 2, 3, 0), (UP, 2, 4, 1)),
-    (4, 2): ((OUT, 0, 0, 0), (OUT, 1, 0, 0)),
-    (4, 3): ((KEY, 0, 0, 0), (DOWN, 2, 4, 0)),
-    (4, 4): ((UP, 2, 4, 0), (KEY, 0, 1, 1)),
-    (4, 5): ((VALUE, 1, 0, 1), (KEY, 1, 0, 1)),
-    (5, 2): ((GATE, 1, 2, 0), (GATE, 0, 2, 0), (GATE, 1, 3, 1)),
-    (5, 3): ((VALUE, 1, 0, 0), (KEY, 1, 0, 0), (KERN, 0, 1, 0), (KERN, 0, 2, 1), (KEY, 1, 1, 1)),
-    (5, 4): ((UP, 1, 5, 1), (UP, 2, 5, 1)),
-    (5, 5): ((KEY, 0, 1, 0), (VALUE, 2, 0, 1), (GATE, 0, 3, 1), (KEY, 2, 0, 1), (KEY, 0, 2, 1)),
-    (5, 7): ((ROW, 0, 0, 1), (DOWN, 0, 5, 1)),
-    (5, 8): ((UP, 3, 1, 0), (DOWN, 3, 1, 0), (GATE, 1, 3, 0), (UP, 3, 2, 1), (DOWN, 3, 2, 1)),
-    (5, 9): ((KEY, 1, 1, 0), (VALUE, 2, 0, 0), (KEY, 2, 0, 0), (UP, 1, 5, 0), (UP, 2, 5, 0), (VALUE, 1, 1, 1)),
-    (5, 10): ((KEY, 2, 1, 1),),
-    (5, 11): ((ROW, 1, 0, 1), (TAPS, 0, 0, 1)),
+    (0, 0): ((UP, 3, 1, 1), (DOWN, 3, 1, 1), (UP, 2, 2, 1), (DOWN, 2, 2, 1), (UP, 1, 3, 1), (GATE, 0, 1, 1), (DOWN, 1, 3, 1), (GATE, 1, 1, 1), (DOWN, 0, 4, 1)),
+    (0, 3): ((KERN, 0, 0, 1), (OUT, 0, 0, 1)),
+    (1, 3): ((KERN, 0, 0, 0), (KERN, 1, 0, 1)),
+    (2, 1): ((UP, 1, 3, 0), (KERN, 0, 1, 1), (OUT, 1, 0, 1)),
+    (2, 2): ((DOWN, 1, 3, 0), (DOWN, 1, 4, 1)),
+    (2, 3): ((DOWN, 0, 4, 0), (KERN, 1, 0, 0), (KERN, 2, 0, 1), (KERN, 1, 1, 1)),
+    (3, 2): ((DOWN, 2, 2, 0), (UP, 2, 2, 0), (GATE, 0, 1, 0), (UP, 2, 3, 1)),
+    (3, 3): ((KERN, 2, 0, 0),),
+    (3, 5): ((KERN, 2, 1, 1), (KEY, 0, 0, 1), (DOWN, 2, 3, 1), (UP, 0, 4, 1), (UP, 1, 4, 1), (GATE, 0, 2, 1), (DOWN, 0, 5, 1)),
+    (4, 3): ((KEY, 0, 0, 0), (DOWN, 3, 1, 0), (UP, 3, 1, 0), (GATE, 1, 1, 0), (KERN, 0, 1, 0), (UP, 2, 3, 0), (DOWN, 1, 4, 0), (KERN, 1, 1, 0), (KERN, 0, 2, 1), (KERN, 1, 2, 1), (UP, 3, 2, 1), (DOWN, 3, 2, 1), (KEY, 0, 1, 1)),
+    (4, 4): ((DOWN, 1, 5, 1),),
+    (4, 5): ((UP, 0, 4, 0), (UP, 1, 4, 0), (KEY, 1, 0, 1), (UP, 2, 4, 1), (UP, 0, 5, 1), (GATE, 1, 2, 1)),
+    (4, 6): ((OUT, 0, 0, 0),),
+    (5, 1): ((KERN, 2, 1, 0), (KERN, 2, 2, 1)),
+    (5, 2): ((DOWN, 0, 5, 0), (UP, 1, 5, 1)),
+    (5, 3): ((OUT, 1, 0, 0), (KEY, 1, 0, 0), (DOWN, 2, 3, 0), (GATE, 0, 2, 0), (KEY, 1, 1, 1), (DOWN, 2, 4, 1)),
+    (5, 4): ((KERN, 0, 2, 0), (KERN, 1, 2, 0), (KERN, 0, 3, 1), (GATE, 0, 3, 1)),
+    (5, 5): ((UP, 0, 5, 0), (UP, 3, 2, 0), (UP, 2, 4, 0), (VALUE, 2, 0, 1), (KERN, 1, 3, 1), (KEY, 2, 0, 1), (UP, 2, 5, 1)),
+    (5, 7): ((DOWN, 1, 5, 0), (UP, 1, 5, 0), (ROW, 0, 0, 1), (UP, 3, 3, 1)),
+    (5, 8): ((KERN, 2, 2, 0), (DOWN, 3, 2, 0), (ROW, 1, 0, 1), (KERN, 2, 3, 1)),
+    (5, 9): ((VALUE, 2, 0, 0), (KEY, 2, 0, 0), (GATE, 1, 2, 0), (VALUE, 2, 1, 1), (KEY, 2, 1, 1)),
+    (5, 10): ((KEY, 0, 1, 0), (DOWN, 3, 3, 1)),
+    (5, 11): ((UP, 2, 5, 0), (TAPS, 0, 0, 1)),
 }
 BACK_LEFT = (
+    (KEY, 0, 2, 1),
+    (KERN, 0, 3, 0),
+    (KERN, 0, 4, 1),
+    (GATE, 1, 3, 1),
+    (GATE, 0, 3, 0),
+    (KERN, 1, 3, 0),
+    (TAPS, 0, 0, 0),
+    (KERN, 1, 4, 1),
+    (TAPS, 0, 1, 1),
+    (KEY, 1, 1, 0),
+    (KERN, 2, 3, 0),
+    (UP, 3, 3, 0),
+    (KERN, 2, 4, 1),
+    (UP, 3, 4, 1),
+    (DOWN, 2, 4, 0),
+    (KEY, 1, 2, 1),
+    (KERN, 0, 4, 0),
+    (DOWN, 2, 5, 1),
+    (VALUE, 2, 1, 0),
+    (KEY, 2, 1, 0),
+    (VALUE, 2, 2, 1),
+    (KEY, 2, 2, 1),
+    (KERN, 1, 4, 0),
+    (TAPS, 0, 1, 0),
+    (GATE, 1, 3, 0),
     (KEY, 0, 2, 0),
-    (GATE, 0, 3, 0),
-    (KERN, 0, 2, 0),
-    (KERN, 0, 3, 1),
-    (TAPS, 0, 0, 0),
-    (DOWN, 0, 5, 0),
-    (VALUE, 2, 1, 1),
-    (TAPS, 0, 1, 1),
-    (KEY, 1, 2, 1),
-    (VALUE, 1, 1, 0),
     (KEY, 0, 3, 1),
-    (UP, 3, 2, 0),
-    (DOWN, 3, 2, 0),
-    (UP, 3, 3, 1),
-    (KEY, 2, 1, 0),
-    (VALUE, 1, 2, 1),
-    (DOWN, 3, 3, 1),
-    (KEY, 2, 2, 1),
+    (KERN, 2, 4, 0),
+    (COEF, 0, 0, 1),
+    (TAPS, 0, 2, 1),
+    (DOWN, 3, 3, 0),
+    (UP, 3, 4, 0),
+    (DOWN, 3, 4, 1),
+    (COEF, 0, 0, 0),
+    (COEF, 0, 1, 1),
+    (UP, 3, 5, 1),
+    (GATE, 0, 4, 1),
+    (KEY, 2, 2, 0),
+    (VALUE, 2, 2, 0),
+    (VALUE, 2, 3, 1),
+    (KEY, 2, 3, 1),
+    (GATE, 1, 4, 1),
     (KEY, 1, 2, 0),
-    (KERN, 0, 3, 0),
     (KEY, 1, 3, 1),
-    (KERN, 0, 4, 1),
-    (VALUE, 2, 1, 0),
-    (TAPS, 0, 1, 0),
-    (VALUE, 2, 2, 1),
-    (KEY, 0, 3, 0),
-    (UP, 3, 3, 0),
-    (VALUE, 1, 2, 0),
-    (KEY, 2, 2, 0),
-    (TAPS, 0, 2, 1),
     (ROW, 0, 0, 0),
-    (UP, 3, 4, 1),
-    (GATE, 1, 4, 1),
-    (KEY, 1, 3, 0),
-    (VALUE, 1, 3, 1),
-    (GATE, 0, 4, 1),
-    (KEY, 2, 3, 1),
-    (VALUE, 2, 2, 0),
-    (DOWN, 3, 3, 0),
-    (VALUE, 2, 3, 1),
-    (KERN, 0, 4, 0),
-    (COEF, 0, 0, 1),
-    (DOWN, 1, 5, 1),
-    (DOWN, 3, 4, 1),
+    (DOWN, 2, 5, 0),
     (TAPS, 0, 2, 0),
     (TAPS, 0, 3, 1),
-    (DOWN, 2, 5, 1),
-    (ROW, 1, 0, 0),
-    (COEF, 0, 0, 0),
-    (COEF, 0, 1, 1),
-    (UP, 3, 4, 0),
-    (GATE, 1, 4, 0),
-    (VALUE, 1, 3, 0),
-    (UP, 3, 5, 1),
-    (VALUE, 2, 3, 0),
-    (KEY, 2, 3, 0),
-    (GATE, 0, 4, 0),
-    (VALUE, 1, 4, 1),
-    (VALUE, 2, 4, 1),
+    (KEY, 0, 3, 0),
     (KEY, 0, 4, 1),
-    (KEY, 1, 4, 1),
-    (TAPS, 0, 3, 0),
-    (DOWN, 1, 5, 0),
     (COEF, 0, 1, 0),
     (COEF, 0, 2, 1),
-    (TAPS, 0, 4, 1),
     (UP, 3, 5, 0),
+    (ROW, 1, 0, 0),
+    (VALUE, 2, 3, 0),
+    (VALUE, 2, 4, 1),
+    (GATE, 0, 4, 0),
+    (KEY, 2, 3, 0),
     (KEY, 2, 4, 1),
-    (DOWN, 2, 5, 0),
+    (GATE, 1, 4, 0),
     (DOWN, 3, 4, 0),
     (DOWN, 3, 5, 1),
-    (VALUE, 1, 4, 0),
-    (VALUE, 2, 4, 0),
-    (KEY, 1, 4, 0),
+    (KEY, 0, 4, 0),
     (COEF, 0, 2, 0),
     (COEF, 0, 3, 1),
-    (KEY, 0, 4, 0),
+    (TAPS, 0, 3, 0),
+    (TAPS, 0, 4, 1),
+    (KEY, 1, 3, 0),
+    (KEY, 1, 4, 1),
+    (VALUE, 2, 4, 0),
+    (KEY, 2, 4, 0),
+    (COEF, 0, 3, 0),
     (TAPS, 0, 4, 0),
-    (KEY, 2, 4, 0),
     (DOWN, 3, 5, 0),
-    (COEF, 0, 3, 0),
+    (KEY, 1, 4, 0),
 )
 
 
@@ -1103,8 +1109,10 @@
     states, channels = rate_ref.shape
     each = states // 16
 
-    def keep_kern(own, given, sideways):
-        put(d_kern, 0, own, given, sideways)
+    def keep_kern(own, given, sideways, t):
+        put(d_kern, t * tile, own, given, sideways)
+        if t != KERN_LAST:
+            return
         steps = d_kern.shape[0]
         first = lax.convert_element_type(lax.axis_index("dp") * steps, F32)
         for low in range(0, channels, LANES):
@@ -1145,13 +1153,16 @@
     sums[COEF, 0] = Sum([coef_base] + take(4), coef_sems, "xnf", keep_coef, across=False)
     sums[TAPS, 0] = Sum([taps_base] + take(5), taps_sems, "xnf", keep_taps)
 
+    later = (half - FIRST_ROWS) // 2
     for i in range(2):
+        low = FIRST_ROWS + i * later
+        other = pl.ds(pl.multiple_of((1 - side) * half + low, 16), later)
+        sums[OUT, i] = Rows(out_row_ref.at[other], out_ref.at[side, pl.ds(low, later)], out_sems.at[i])
         piece = pl.ds(i * (half // 2), half // 2)
-        other = pl.ds(pl.multiple_of((1 - side) * half + i * (half // 2), half // 2), half // 2)
-        sums[OUT, i] = Rows(out_row_ref.at[other], out_ref.at[side, piece], out_sems.at[i])
         sums[ROW, i] = Rows(d_x.at[0, piece], d_tokens_ref.at[side, piece], row_sems.at[i])
-    kern_sideways = "y" in ORDER[KERN]
-    sums[KERN, 0] = Sum([kern_base] + take(len(ORDER[KERN]) + 2), kern_sems, ORDER[KERN], keep_kern)
+    for t in range(tiles):
+        keep = functools.partial(keep_kern, t=t)
+        sums[KERN, t] = Sum([kern_base.at[t]] + take(5), kern_sems.at[t], ORDER[KERN][t], keep)
     share = width // 16
     for t in range(tiles):
 
@@ -1238,12 +1249,7 @@
     @pl.when(j < tiles)
     def _():
         parts = [dot(back_ref[...], prod[b]) * (1.0 / BLOCK) for b in range(blocks)]
-        kern_parts = jnp.concatenate(parts, axis=0)
-        if kern_sideways:
-            columns = pl.ds(pl.multiple_of(j * (tile // 2), tile // 2), tile // 2)
-        else:
-            columns = pl.ds(pl.multiple_of(j * tile, tile), tile)
-        spread(kern_parts, kern_base.at[..., columns], kern_sideways)
+        spread(jnp.concatenate(parts, axis=0), kern_base.at[j])
 
     @pl.when(j == tiles - 1)
     def _():
@@ -1407,7 +1413,8 @@
     bits = [(2, 2, 2), (2, 2), (2,), (), ()]
     lands += [wide(*bits[n], 2 * each, channels) for n in range(4)]
     lands += [wide(*bits[n], 8, width) for n in range(5)]
-    lands += landings(ks, width, ORDER[KERN])
+    for t in range(count):
+        lands += landings(ks, tile, ORDER[KERN][t])
     for t in range(count):
         orders = ORDER[KV][t]
         for order in orders:
@@ -1468,10 +1475,10 @@
             sems(5, 2),
             wide(2, 2, 2, 2, 2 * each, channels),
             sems(4, 2),
-            vmem(*base_shape(ks, width, ORDER[KERN])),
+            vmem(count, *base_shape(ks, tile, "")),
             vmem(count, *base_shape(2 * share, tile, "")),
             sems(len(left), 6, 2),
-            sems(6, 2),
+            sems(count, 5, 2),
             sems(count, 2, 6, 2),
             sems(2, 2),
             sems(2, 2),
@@ -1793,33 +1800,39 @@
     )
 
 
-def settle_body(*refs):
+def settle_body(first_ref, *refs):
     count = (len(refs) - 1) // 3
     sources, targets, held, sems = refs[:count], refs[count : 2 * count], refs[2 * count : 3 * count], refs[-1]
     reads = [pltpu.make_async_copy(sources[i], held[i], sems.at[0, i]) for i in range(count)]
     writes = [pltpu.make_async_copy(held[i], targets[i], sems.at[1, i]) for i in range(count)]
+    place = held[0].at[1 - lax.axis_index("seq"), pl.ds(0, first_ref.shape[0])]
+    first = pltpu.make_async_copy(first_ref, place, sems.at[0, count])
     for copy in reads:
         copy.start()
-    for read, write in zip(reads, writes):
+    reads[0].wait()
+    first.start()
+    for read, write in zip(reads[1:], writes[1:]):
         read.wait()
         write.start()
+    first.wait()
+    writes[0].start()
     for copy in writes:
         copy.wait()
 
 
-def settle_call(arrays):
+def settle_call(first, arrays):
     anywhere = pl.BlockSpec(memory_space=pl.ANY)
     return pl.pallas_call(
         settle_body,
-        in_specs=[anywhere] * len(arrays),
+        in_specs=[anywhere] * (1 + len(arrays)),
         out_specs=[anywhere] * len(arrays),
         out_shape=[jax.ShapeDtypeStruct(array.shape, array.dtype) for array in arrays],
         scratch_shapes=[pltpu.VMEM(array.shape, array.dtype) for array in arrays]
-        + [pltpu.SemaphoreType.DMA((2, len(arrays)))],
+        + [pltpu.SemaphoreType.DMA((2, len(arrays) + 1))],
         compiler_params=params(),
         cost_estimate=cost(1e3, 10e6),
         name="settle",
-    )(*arrays)
+    )(first, *arrays)
 
 
 def split_rows(
@@ -1833,11 +1846,11 @@
     x, cot, a_one, q, k, v, kern, tapspec, hidden, a_two, shifted, mixed, state = mixer_call(
         lengths, tokens, cotangent, coef, rate, taps, gain_one, gain_two, w_query, w_key, w_value, w_out, tables, tile
     )
-    out_row, d_hidden, d_query, d_state, d_gain_two, up_part, down_part, *left = ffn_call(
+    out_row, d_hidden, d_query, d_state, out_first, d_gain_two, up_part, down_part, *left = ffn_call(
         lengths, a_two, cot, hidden, gain_two, w_up, w_down, w_out, state, q, a_one
     )
     out, d_tokens, gain_one_grad, gain_two_grad, taps_grad, coef_grad, rate_grad, up, down, wout, query, key, value = (
-        settle_call(mixer_back_call(
+        settle_call(out_first, mixer_back_call(
             lengths, out_row, a_one, d_state, d_query, mixed, shifted, k, v, w_query, w_key, w_value, kern, tapspec,
             tables, x, gain_one, d_hidden, d_gain_two, coef, rate, (up_part, down_part, left), states, tile,
         ))

time: 197 us -> 194 us (0.985)
  Pallas kernels: 196 us -> 193 us
    pallas_call x1, Pallas kernels: 49.2 us -> 45.5 us  [mixer_call(): pl.pallas_call(mixer_body, grid=(1 + width // tile,), in_specs=[pl.BlockS...]
where the time goes in v5:
time: 194 us
  Pallas kernels  193 us (99%)
    pallas_call x1, Pallas kernels, mixer_back_call(): pl.pallas_call(mixer_back_body, grid=(2 * count,), in_specs=[pl.BlockSpec...  81.5 us
    pallas_call x1, Pallas kernels, ffn_call(): pl.pallas_call(ffn_body, grid=(5,), in_specs=[pl.BlockSpec(memory_space=p...  61.8 us
    pallas_call x1, Pallas kernels, mixer_call(): pl.pallas_call(mixer_body, grid=(1 + width // tile,), in_specs=[pl.BlockS...  45.5 us
    pallas_call x1, Pallas kernels, settle_call(): pl.pallas_call(settle_body, in_specs=[anywhere] * (1 + len(arrays)), out_...  4.42 us

profile of v5, /device:TPU:0, one launch (start us, length us, event | category | flops | bytes accessed | tf_op | source)
XLA Modules:
  0.0 194.0 jit_solution(14808788389638007311)
XLA Ops:
  0.6 45.5 %mixer_forward.1 = (bf16[1024,768]{1,0:T(8,128)(2,1)}, bf16[1024,768]{1,0:T(8,128)(2,1)}, bf16[1024,768]{1,0:T(8,128)(2,1)}, bf16[1024,768]{1,0:T(8,128)(2,1)}, ...) custom-call(s32[2]{0:T(128)} %lengths_ref.5, ...), custom_call_target="tpu_custom_call" | custom-call | flops 16000000000 | bytes 40000000 | tf_op jit(solution)/shard_map/mixer_forward/pallas_call | solution.py:592
  46.1 61.8 %feed_forward.1 = (bf16[1024,768]{1,0:T(8,128)(2,1)}, f32[1024,768]{1,0:T(8,128)}, bf16[1024,768]{1,0:T(8,128)(2,1)}, bf16[1024,768]{1,0:T(8,128)(2,1)}, bf16[12...) custom-call(s32[2]{0:T(128)} %lengths_ref.5, ...), custom_call_target="tpu_custom_call" | custom-call | flops 28991029248 | bytes 40000000 | tf_op jit(solution)/shard_map/feed_forward/pallas_call | solution.py:901
  108.0 81.5 %mixer_back.1 = (bf16[2,512,768]{2,1,0:T(8,128)(2,1)}, bf16[2,512,768]{2,1,0:T(8,128)(2,1)}, f32[1,48]{1,0:T(1,128)}, f32[1,48]{1,0:T(1,128)}, f32[4,384]{1,0:T(...) custom-call(s32[2]{0:T(128)} %lengths_ref.5, ...), custom_call_target="tpu_custom_call" | custom-call | flops 25999998976 | bytes 40000000 | tf_op jit(solution)/shard_map/mixer_back/pallas_call | solution.py:1437
  189.4 4.4 %settle.1 = (bf16[2,512,768]{2,1,0:T(8,128)(2,1)}, bf16[2,512,768]{2,1,0:T(8,128)(2,1)}, f32[1,48]{1,0:T(1,128)}, f32[1,48]{1,0:T(1,128)}, f32[4,384]{1,0:T(4,12...) custom-call(bf16[128,768]{1,0:T(8,128)(2,1)} %get-tuple-element.76.f, ...), custom_call_target="tpu_custom_call" | custom-call | flops 1000 | bytes 10000000 | tf_op jit(solution)/shard_map/settle/pallas_call | solution.py:1825
